TPU v7x, 512 devices: a whole 4x4x16 slice. The times are simulated.
512 devices in a mesh: slide: 8 (over x, core), grid: 64 (over y, z).
Axes of the slice: x: 4, y: 4, z: 16, core: 2. Of those that a mesh axis runs over, the one named last changes fastest.
Arguments:
- embeddings: bfloat16 [8, 8192, 512], P('slide', 'grid'), may hold values from -6 to 6
- visible: int32 [8, 2048], P('slide'), may hold values from 0 to 8191, as said below
- window_id: int32 [8, 8192], P('slide'), may hold values from 0 to 126, as said below
- output_gradient: bfloat16 [8, 8192, 512], P('slide', 'grid'), may hold values from -6 to 6
- mask_token: float32 [512], replicated, may hold values from -4 to 4
- enc_qkv: bfloat16 [512, 1536], replicated, may hold values from -2 to 2
- enc_out: bfloat16 [512, 512], replicated, may hold values from -0.25 to 0.25
- dec_qkv: bfloat16 [512, 1536], replicated, may hold values from -2 to 2
- decoder_projected: bfloat16 [512, 512], replicated, may hold values from -0.25 to 0.25
Outputs:
- grad_embeddings: bfloat16 [8, 8192, 512], P('slide', 'grid')
- grad_enc_out: float32 [512, 512], P('grid', 'slide')
- grad_dec_out: float32 [512, 512], P('grid', 'slide')
Inputs may be any that keep to these rules, and one draw needn't show every extreme that they name: Each row holds 2048 different tile numbers in ascending order. Visible tiles come in aligned runs of 32; in every slide all 128 tiles of one block of 128 aligned tiles are visible, and so are the runs that hold tiles 128 - 128 // 2 to 191. `window_id`: window numbers start at 0 in every slide and rise by 0 or 1 from tile to tile; a window holds 1 to 128 consecutive tiles; the last tile of every slide is in window 2 * 64 - 2.
All inputs are finite; a program needn't handle non-finite values.
Results may differ from a plain program's by a relative error of at most 0.019.
Values may be sent and summed in bfloat16 or wider, within the bound.
No kernel may reach another device: no remote copies, remote signals or barrier semaphores. Data moves between devices by JAX's collectives and lax.ppermute only.
A program may use at most 64 MiB of HBM per device.

v0:
```python
import math

import jax
import jax.numpy as jnp
from jax import lax
from jax.sharding import PartitionSpec as P

HEADS = 8
WIN = 128


EPS = 1e-06


def shortened(array):

    def short(part):
        return part.astype(jnp.bfloat16) if part.dtype == jnp.float32 else part

    return jax.tree.map(short, array)


def extended_2(block, sides, width):
    for axis, dim in sides:
        count = lax.axis_size(axis)
        forward = [(i, i + 1) for i in range(count - 1)]
        backward = [(target, source) for source, target in forward]
        low = lax.ppermute(
            lax.slice_in_dim(block, block.shape[dim] - width, None, axis=dim), axis, forward
        )
        high = lax.ppermute(lax.slice_in_dim(block, 0, width, axis=dim), axis, backward)
        block = jnp.concatenate([low, block, high], axis=dim)
    return block


def shifted(block, axis, distance):
    devices = range(lax.axis_size(axis))
    route = [(i - distance, i) for i in devices if i - distance in devices]
    return lax.ppermute(block, axis, route)


def rms_f(values):
    return values * lax.rsqrt(jnp.mean(values * values, axis=-1, keepdims=True) + EPS)


def attend(queries, key_vecs, values, allowed, head_count):
    shape_q = queries.shape
    head_width = shape_q[-1] // head_count
    query_per_head = queries.reshape(shape_q[:-1] + (head_count, head_width))
    key_per_head = key_vecs.reshape(key_vecs.shape[:-1] + (head_count, head_width))
    value_per_head = values.reshape(values.shape[:-1] + (head_count, head_width))
    logit_scores = jnp.einsum("...vys,...rys->...yvr", query_per_head, key_per_head) * (
        1.0 / math.sqrt(head_width)
    )
    if allowed is not None:
        logit_scores = jnp.where(allowed[..., None, :, :], logit_scores, -1e30)
    row_top = lax.stop_gradient(jnp.max(logit_scores, axis=-1, keepdims=True))
    weights = jnp.exp(logit_scores - row_top)
    attention_probs = (weights / jnp.sum(weights, axis=-1, keepdims=True)).astype(jnp.bfloat16)
    attention_probs = lax.optimization_barrier(attention_probs).astype(jnp.float32)
    attended_rows = jnp.einsum("...wvy,...ywj->...vwj", attention_probs, value_per_head)
    return attended_rows.reshape(shape_q).astype(jnp.bfloat16)


def encoder_block(tokens, enc_qkv, enc_out):
    width = tokens.shape[-1]
    residual = tokens.astype(jnp.float32)
    normed = rms_f(residual).astype(jnp.bfloat16)
    projected = jnp.dot(normed, enc_qkv, preferred_element_type=jnp.float32).astype(jnp.bfloat16)
    projected = lax.optimization_barrier(projected).astype(jnp.float32)
    attended_rows = attend(
        projected[..., :width],
        projected[..., width : 2 * width],
        projected[..., 2 * width :],
        None,
        HEADS,
    )
    hidden = residual + jnp.dot(attended_rows, enc_out, preferred_element_type=jnp.float32)
    return (hidden.astype(jnp.bfloat16), attended_rows)


def pick_rows(lookup, index_rows):
    return jax.vmap(lambda source_rows, where_at: source_rows[where_at])(lookup, index_rows)


def place_rows(blank, index_rows, updates):
    return jax.vmap(lambda target, where_at, update: target.at[where_at].set(update))(
        blank, index_rows, updates
    )


def back_project(gradient, weight):
    return jnp.einsum(
        "snc,dc->snd",
        gradient,
        weight,
        precision=lax.Precision.HIGHEST,
        preferred_element_type=jnp.float32,
    )


def shards(
    embeddings,
    visible,
    window_id,
    output_gradient,
    mask_token,
    enc_qkv,
    enc_out,
    dec_qkv,
    decoder_projected,
):
    groups = lax.axis_size("grid")
    shard_index = lax.axis_index("grid")
    slides, tile_dev, width = embeddings.shape
    vis_all = visible.shape[1]
    vis_dev = vis_all // groups
    capacity = -(-tile_dev // groups)
    tiles_all = window_id.shape[1]
    slot_count = groups * capacity
    owner_shard = visible // tile_dev
    counts = jnp.sum(
        (owner_shard[:, :, None] == jnp.arange(groups, dtype=jnp.int32)[None, None, :]).astype(
            jnp.int32
        ),
        axis=1,
    )
    before = jnp.cumsum(counts, axis=1) - counts
    own_start = lax.dynamic_index_in_dim(before, shard_index, axis=1, keepdims=False)
    own_count = lax.dynamic_index_in_dim(counts, shard_index, axis=1, keepdims=False)
    peer_ids = jnp.arange(groups, dtype=jnp.int32)[:, None]
    slot_ids = jnp.arange(capacity, dtype=jnp.int32)[None, :]
    start_box = own_start[:, None, None]
    rank_ids = start_box + slot_ids[None] * groups + jnp.mod(peer_ids[None] - start_box, groups)
    is_live = rank_ids < (own_start + own_count)[:, None, None]
    safe_ranks = jnp.minimum(rank_ids, vis_all - 1).reshape(slides, slot_count)
    tile_ids = pick_rows(visible, safe_ranks).reshape(slides, groups, capacity)
    local_rows = jnp.where(is_live, tile_ids - shard_index * tile_dev, tile_dev).reshape(
        slides, slot_count
    )
    my_ranks = jnp.arange(vis_dev, dtype=jnp.int32) * groups + shard_index
    my_tiles = visible[:, my_ranks]
    sources = my_tiles // tile_dev
    source_start = pick_rows(before, sources)
    positions = sources * capacity + (my_ranks[None, :] - source_start) // groups

    def to_slots(values):
        blank = jnp.zeros((slides, slot_count + 1, width), values.dtype)
        return place_rows(blank, positions, values)[:, :slot_count].reshape(
            slides, groups, capacity, width
        )

    def from_tiles(tile_values):
        extended_rows = jnp.concatenate(
            [tile_values, jnp.zeros((slides, 1, width), tile_values.dtype)], axis=1
        )
        return pick_rows(extended_rows, local_rows).reshape(slides, groups, capacity, width)

    arrived = lax.all_to_all(
        from_tiles(embeddings), "grid", split_axis=1, concat_axis=1, tiled=True
    )
    tokens = pick_rows(arrived.reshape(slides, slot_count, width), positions)

    def encode(inputs):
        return encoder_block(inputs, enc_qkv, enc_out)

    encoded, enc_back, encoder_attended = jax.vjp(encode, tokens, has_aux=True)
    returned = lax.all_to_all(
        shortened(to_slots(encoded)), "grid", split_axis=1, concat_axis=1, tiled=True
    )
    base_inputs = jnp.broadcast_to(mask_token, (slides, tile_dev + 1, width))
    inputs = place_rows(
        base_inputs, local_rows, returned.reshape(slides, slot_count, width).astype(jnp.float32)
    )[:, :tile_dev]
    w_query = dec_qkv[:, :width]
    w_keyval = dec_qkv[:, width:]
    normed = rms_f(inputs).astype(jnp.bfloat16)
    queries = jnp.dot(normed, w_query, preferred_element_type=jnp.float32).astype(jnp.bfloat16)
    keyvals = jnp.dot(normed, w_keyval, preferred_element_type=jnp.float32).astype(jnp.bfloat16)
    margin = WIN
    ext_spots = shard_index * tile_dev - margin + jnp.arange(tile_dev + 2 * margin, dtype=jnp.int32)
    inside = (ext_spots >= 0) & (ext_spots < tiles_all)
    ext_ids = jnp.where(inside[None, :], window_id[:, jnp.clip(ext_spots, 0, tiles_all - 1)], -1)
    own_ids = lax.dynamic_slice_in_dim(window_id, shard_index * tile_dev, tile_dev, axis=1)
    extended = extended_2(keyvals, (("grid", 1),), margin)
    queries, extended = lax.optimization_barrier((queries, extended))
    dcontext = jnp.einsum(
        "aph,bh->apb", output_gradient, decoder_projected, preferred_element_type=jnp.float32
    ).astype(jnp.bfloat16)
    block = math.gcd(tile_dev, 256)

    def block_step(carry, index):
        query_block = queries.astype(jnp.float32)
        keyval_block = extended.astype(jnp.float32)
        allowed = own_ids[:, :, None] == ext_ids[:, None, :]

        def window_attend(query_f, keyval_f):
            return attend(query_f, keyval_f[..., :width], keyval_f[..., width:], allowed, HEADS)

        context_block, attn_back = jax.vjp(window_attend, query_block, keyval_block)
        grad_q_block, grad_kv_block = attn_back(dcontext)
        current = carry
        carry = current + grad_kv_block
        return (carry, (grad_q_block, context_block))

    grad_kv, (grad_q_blocks, context_blocks) = lax.scan(
        block_step,
        jnp.zeros((slides, tile_dev + 2 * margin, 2 * width), jnp.float32),
        jnp.arange(tile_dev // block, dtype=jnp.int32),
    )
    grad_q = grad_q_blocks.transpose(1, 0, 2, 3).reshape(slides, tile_dev, width)
    decoder_attended = context_blocks.transpose(1, 0, 2, 3).reshape(slides, tile_dev, width)
    dnormed = back_project(grad_q, w_query)
    from_right = shifted(grad_kv[:, :margin].astype(jnp.bfloat16), "grid", -1).astype(jnp.float32)
    from_left = shifted(grad_kv[:, -margin:].astype(jnp.bfloat16), "grid", 1).astype(jnp.float32)
    middle = grad_kv[:, margin : margin + tile_dev]
    middle = middle.at[:, :margin].add(from_left).at[:, -margin:].add(from_right)
    dnormed = dnormed + back_project(middle, w_keyval)
    _, norm_back = jax.vjp(rms_f, inputs)
    dinputs = norm_back(dnormed)[0] + output_gradient.astype(jnp.float32)
    grad_dec_part = jnp.einsum(
        "qcr,qcu->ru", decoder_attended, output_gradient, preferred_element_type=jnp.float32
    )
    arrived_grads = lax.all_to_all(
        from_tiles(dinputs.astype(jnp.bfloat16)), "grid", split_axis=1, concat_axis=1, tiled=True
    )
    encoded_cotangent = pick_rows(arrived_grads.reshape(slides, slot_count, width), positions)
    grad_enc_part = jnp.einsum(
        "qcr,qcu->ru", encoder_attended, encoded_cotangent, preferred_element_type=jnp.float32
    )
    (dtokens,) = enc_back(encoded_cotangent)
    back_home = lax.all_to_all(
        shortened(to_slots(dtokens)), "grid", split_axis=1, concat_axis=1, tiled=True
    )
    grad_tiles = place_rows(
        jnp.zeros((slides, tile_dev + 1, width), jnp.bfloat16),
        local_rows,
        back_home.reshape(slides, slot_count, width),
    )[:, :tile_dev]
    stacked = jnp.stack([grad_enc_part, grad_dec_part])
    partial_sum = lax.psum_scatter(stacked, "grid", scatter_dimension=1, tiled=True)
    partial_sum = lax.psum_scatter(
        partial_sum.astype(jnp.bfloat16), "slide", scatter_dimension=2, tiled=True
    ).astype(jnp.float32)
    return (grad_tiles, partial_sum[0], partial_sum[1])


def solution(mesh):
    placed = (
        P("slide", "grid", None),
        P("slide", None),
        P("slide", None),
        P("slide", "grid", None),
        P(),
        P(),
        P(),
        P(),
        P(),
    )
    return jax.shard_map(
        shards,
        mesh=mesh,
        in_specs=placed,
        out_specs=(P("slide", "grid", None), P("grid", "slide"), P("grid", "slide")),
        check_vma=False,
    )
```

profile of v0, /device:TPU:8, one launch (start us, length us, event | category | flops | bytes accessed | tf_op | source)
XLA Modules:
  0.0 880.4 jit_solution(15217913457122179177)
XLA Ops:
  7.2 0.9 and_select_fusion
  11.4 1.6 gather_fusion.2
  14.3 0.9 concatenate.13
  15.3 1.2 gather_fusion.4
  16.4 0.7 reshape.1040
  17.2 18.7 %all-to-all-start = ((bf16[1,64,2,512]{3,2,0,1:T(2,128)(2,1)}), bf16[1,64,2,512]{3,2,0,1:T(2,128)(2,1)S(1)}, u32[]{:S(2)}, u32[]{:S(2)}) async-start(bf16[1,64,2,512]{3,2,0,1:T(2,128)(2,1)} %bitcast.25), calls=%async_computation | async-start | bytes 262144 | tf_op jit(solution)/shard_map/all_to_all | solution.py:159
  36.0 0.7 gather_fusion
  36.7 0.7 gather_fusion.3
  37.5 13.9 %all-to-all-done = bf16[1,64,2,512]{3,2,0,1:T(2,128)(2,1)S(1)} async-done(((bf16[1,64,2,512]{3,2,0,1:T(2,128)(2,1)}), bf16[1,64,2,512]{3,2,0,1:T(2,128)(2,1)S(1)}, u32[]{:S(2)}, u32[]{:S(2)}) %all-to-all-start) | async-done | bytes 131104 | tf_op jit(solution)/shard_map/all_to_all | solution.py:159
  54.7 0.7 scatter_custom_fusion
  55.5 0.7 reshape.1046
  56.2 6.4 all-to-all-start.1
  63.1 2.5 gather_fusion.1
  65.7 1.0 convolution_convert_fusion.4
  66.7 11.1 %all-to-all-done.1 = bf16[1,64,2,512]{3,2,0,1:T(2,128)(2,1)S(1)} async-done(((bf16[1,64,2,512]{3,2,0,1:T(2,128)(2,1)}), bf16[1,64,2,512]{3,2,0,1:T(2,128)(2,1)S(1)}, u32[]{:S(2)}, u32[]{:S(2)}) %all-to-all-start.1) | async-done | bytes 131104 | tf_op jit(solution)/shard_map/all_to_all | solution.py:168
  77.8 0.7 reshape.1158
  78.6 1.6 scatter_fusion
  80.9 1.0 fusion.14
  82.0 3.7 collective-permute-start.1
  85.7 2.1 collective-permute-start
  87.8 0.7 broadcast_compare_fusion
  88.5 1.7 copy.67
  90.2 0.9 fusion.16
  91.1 5.2 collective-permute-done
  96.4 1.2 pad_maximum_fusion.1
  98.8 1.3 fusion.13
  100.1 2.6 fusion.122
  102.7 1.8 fusion.27
  107.1 1.9 collective-permute-start.2
  109.0 6.3 collective-permute-start.3
  116.1 0.7 fusion.35
  117.4 1.6 collective-permute-done.3
  119.0 1.1 fusion.40
  120.3 1.2 gather_fusion.6
  121.5 0.7 reshape.1057
  122.2 8.7 all-to-all-start.2
  131.7 13.3 %all-to-all-done.2 = bf16[1,64,2,512]{3,2,0,1:T(2,128)(2,1)S(1)} async-done(((bf16[1,64,2,512]{3,2,0,1:T(2,128)(2,1)}), bf16[1,64,2,512]{3,2,0,1:T(2,128)(2,1)S(1)}, u32[]{:S(2)}, u32[]{:S(2)}) %all-to-all-start.2) | async-done | bytes 131104 | tf_op jit(solution)/shard_map/all_to_all | solution.py:224
  146.1 1.5 pad_maximum_fusion
  147.7 1.0 copy-done.8
  151.1 0.9 scatter_custom_fusion.2
  152.0 0.7 reshape.1066
  152.7 6.4 all-to-all-start.3
  159.2 673.6 %reduce-scatter.5.cloned.1.call-done = f32[2,8,512]{2,1,0:T(8,128)} async-done(((f32[2,512,512]{2,1,0:T(8,128)}), f32[2,8,512]{2,1,0:T(8,128)}) %reduce-scatter.5.cloned.1.call-update) | async-done | bytes 32784 | tf_op jit(solution)/shard_map/reduce_scatter | solution.py:241
  832.8 0.8 convert_element_type.252
  833.8 0.8 reshape.1203
  834.7 1.1 scatter_custom_fusion.3
  836.4 35.6 %reduce-scatter.7.cloned.1.call-done = bf16[64,16]{1,0:T(8,128)(2,1)} async-done(((bf16[512,16]{1,0:T(8,128)(2,1)}), bf16[64,16]{1,0:T(8,128)(2,1)}) %reduce-scatter.7.cloned.1.call-update) | async-done | bytes 2064
  872.0 0.8 reshape.1204
  (167 shorter events, 19.0 us)
Async XLA Ops:
  7.2 45.1 %copy-start = (bf16[512,1536]{1,0:T(8,128)(2,1)S(1)}, bf16[512,1536]{1,0:T(8,128)(2,1)}, u32[]{:S(2)}) copy-start(bf16[512,1536]{1,0:T(8,128)(2,1)} %param.22) | copy-start | bytes 4718596
  7.2 28.8 %copy-start.1 = (s32[1,2048]{1,0:T(1,128)S(1)}, s32[1,2048]{1,0:T(1,128)}, u32[]{:S(2)}) copy-start(s32[1,2048]{1,0:T(1,128)} %param.18) | copy-start | bytes 24580
  17.2 34.2 %all-to-all-start = ((bf16[1,64,2,512]{3,2,0,1:T(2,128)(2,1)}), bf16[1,64,2,512]{3,2,0,1:T(2,128)(2,1)S(1)}, u32[]{:S(2)}, u32[]{:S(2)}) async-start(bf16[1,64,2,512]{3,2,0,1:T(2,128)(2,1)} %bitcast.25), calls=%async_computation | async-start | bytes 262144 | tf_op jit(solution)/shard_map/all_to_all | solution.py:159
  37.5 17.2 %copy-start.32 = (s32[32]{0:T(128)}, s32[32]{0:T(128)S(1)}, u32[]{:S(2)}) copy-start(s32[32]{0:T(128)S(1)} %get-tuple-element.95) | copy-start | bytes 388
  52.3 1.8 copy-start.7
  52.7 9.9 %copy-start.2 = (s32[1,8192]{1,0:T(1,128)S(1)}, s32[1,8192]{1,0:T(1,128)}, u32[]{:S(2)}) copy-start(s32[1,8192]{1,0:T(1,128)} %param.19) | copy-start | bytes 98308
  53.0 0.6 copy-start.23
  53.1 0.6 copy-start.25
  53.3 0.8 copy-start.17
  53.7 12.0 %copy-start.13 = (bf16[1,8,32,32]{2,3,1,0:T(8,128)(2,1)}, bf16[1,8,32,32]{2,3,1,0:T(8,128)(2,1)S(1)}, u32[]{:S(2)}) copy-start(bf16[1,8,32,32]{2,3,1,0:T(8,128)(2,1)S(1)} %fusion.65) | copy-start | bytes 49156
  54.1 0.6 copy-start.19
  54.7 11.0 %copy-start.9 = (bf16[1,128,512]{2,1,0:T(8,128)(2,1)S(1)}, bf16[1,128,512]{2,1,0:T(8,128)(2,1)}, u32[]{:S(2)}) copy-start(bf16[1,128,512]{2,1,0:T(8,128)(2,1)} %param.20) | copy-start | bytes 393220
  54.7 11.0 %copy-start.16 = (bf16[512,512]{1,0:T(8,128)(2,1)S(1)}, bf16[512,512]{1,0:T(8,128)(2,1)}, u32[]{:S(2)}) copy-start(bf16[512,512]{1,0:T(8,128)(2,1)} %param.25) | copy-start | bytes 1572868
  56.2 21.6 %all-to-all-start.1 = ((bf16[1,64,2,512]{3,2,0,1:T(2,128)(2,1)}), bf16[1,64,2,512]{3,2,0,1:T(2,128)(2,1)S(1)}, u32[]{:S(2)}, u32[]{:S(2)}) async-start(bf16[1,64,2,512]{3,2,0,1:T(2,128)(2,1)} %reshape.1046), calls=%async_computation.1 | async-start | bytes 262144 | tf_op jit(solution)/shard_map/all_to_all | solution.py:168
  63.1 15.4 %copy-start.28 = (f32[512]{0:T(512)S(1)}, f32[512]{0:T(512)}, u32[]{:S(2)}) copy-start(f32[512]{0:T(512)} %param.21) | copy-start | bytes 6148
  78.5 2.4 copy-start.4
  80.2 7.6 copy-start.31
  80.3 0.6 copy-start.29
  82.0 9.2 %collective-permute-start.1 = (bf16[1,128,1024]{2,1,0:T(8,128)(2,1)}, bf16[1,128,1024]{2,1,0:T(8,128)(2,1)}, u32[]{:S(2)}, u32[]{:S(2)}) collective-permute-start(bf16[1,128,1024]{2,1,0:T(8,128)(2,1)} %fusion.14), channel_id=1, source_target_pairs={{1,0},{2,1},{3,2},{4,3},{5,4},{6,5},{7,6},{8,7},{9,8},{10,9},{11,1... | collective-permute-start | bytes 786440 | tf_op jit(solution)/shard_map/ppermute | solution.py:31
  85.7 10.7 %collective-permute-start = (bf16[1,128,1024]{2,1,0:T(8,128)(2,1)}, bf16[1,128,1024]{2,1,0:T(8,128)(2,1)}, u32[]{:S(2)}, u32[]{:S(2)}) collective-permute-start(bf16[1,128,1024]{2,1,0:T(8,128)(2,1)} %fusion.14), channel_id=1, source_target_pairs={{0,1},{1,2},{2,3},{3,4},{4,5},{5,6},{6,7},{7,8},{8,9},{9,10},{10,1... | collective-permute-start | bytes 786440 | tf_op jit(solution)/shard_map/ppermute | solution.py:28
  97.5 0.9 copy-start.15
  97.5 1.3 copy-start.11
  98.6 4.2 copy-start.21
  102.7 1.9 copy-start.3
  102.7 2.1 copy-start.6
  104.8 0.9 copy-start.22
  104.8 0.9 copy-start.27
  105.7 0.9 copy-start.12
  107.1 10.4 %collective-permute-start.2 = (bf16[1,128,1024]{1,2,0:T(8,128)(2,1)S(1)}, bf16[1,128,1024]{1,2,0:T(8,128)(2,1)S(1)}, u32[]{:S(2)}, u32[]{:S(2)}) collective-permute-start(bf16[1,128,1024]{1,2,0:T(8,128)(2,1)S(1)} %get-tuple-element.76), channel_id=1, source_target_pairs={{0,1},{1,2},{2,3},{3,4},{4,5},{5,6},{6,7},{7,8},{8,9},{9,10},{10,1... | collective-permute-start | bytes 786440 | tf_op jit(solution)/shard_map/ppermute | solution.py:39
  109.0 7.1 copy-start.5
  109.0 10.0 %collective-permute-start.3 = (bf16[1,128,1024]{1,2,0:T(8,128)(2,1)S(1)}, bf16[1,128,1024]{1,2,0:T(8,128)(2,1)S(1)}, u32[]{:S(2)}, u32[]{:S(2)}) collective-permute-start(bf16[1,128,1024]{1,2,0:T(8,128)(2,1)S(1)} %get-tuple-element.77), channel_id=1, source_target_pairs={{1,0},{2,1},{3,2},{4,3},{5,4},{6,5},{7,6},{8,7},{9,8},{10,9},{11,1... | collective-permute-start | bytes 786440 | tf_op jit(solution)/shard_map/ppermute | solution.py:39
  116.8 3.4 copy-start.30
  116.8 3.4 copy-start.10
  122.2 22.8 %all-to-all-start.2 = ((bf16[1,64,2,512]{3,2,0,1:T(2,128)(2,1)}), bf16[1,64,2,512]{3,2,0,1:T(2,128)(2,1)S(1)}, u32[]{:S(2)}, u32[]{:S(2)}) async-start(bf16[1,64,2,512]{3,2,0,1:T(2,128)(2,1)} %bitcast.60), calls=%async_computation.2 | async-start | bytes 262144 | tf_op jit(solution)/shard_map/all_to_all | solution.py:224
  130.9 14.9 %copy-start.20 = (bf16[32,512]{1,0:T(8,128)(2,1)S(1)}, bf16[32,512]{1,0:T(8,128)(2,1)}, u32[]{:S(2)}) copy-start(bf16[32,512]{1,0:T(8,128)(2,1)} %copy-done.19) | copy-start | bytes 98308
  130.9 702.0 %reduce-scatter.5.cloned.1.call-start = ((), (), s32[]{:S(2)}) async-start(), calls=%async_computation.6 | async-start | bytes 2129920 | tf_op jit(solution)/shard_map/reduce_scatter | solution.py:241
  147.6 1.0 copy-start.8
  147.6 1.6 copy-start.18
  147.6 1.6 copy-start.14
  147.6 2.0 copy-start.26
  147.7 2.3 copy-start.24
  152.7 681.9 %all-to-all-start.3 = ((bf16[1,64,2,512]{3,2,0,1:T(2,128)(2,1)}), bf16[1,64,2,512]{3,2,0,1:T(2,128)(2,1)S(1)}, u32[]{:S(2)}, u32[]{:S(2)}) async-start(bf16[1,64,2,512]{3,2,0,1:T(2,128)(2,1)} %reshape.1066), calls=%async_computation.3 | async-start | bytes 262144 | tf_op jit(solution)/shard_map/all_to_all | solution.py:232
  159.2 712.9 %reduce-scatter.7.cloned.1.call-start = ((), (), s32[]{:S(2)}) async-start(), calls=%async_computation.7 | async-start | bytes 147456
Sparse Core Ops, SparseCore 0:
  147.8 685.0 reduce-scatter.4
  835.8 36.1 reduce-scatter.6
where the time goes:
time: 881 us; the launch traced here: 880 us
  waiting for transfers between devices  755 us (86%)
  starting transfers between devices  54.4 us (6%)
  local copies, waits for them, and re-layouts  30.1 us (3%)
  between operations  16.2 us (2%)
  matrix products  13.9 us (2%)
  other arithmetic  10.6 us (1%)
    reduce_scatter x1, waiting for transfers between devices, shards(): lax.psum_scatter(stacked, 'grid', scatter_dimension=1, tiled=True)  674 us
    unnamed x3, waiting for transfers between devices  35.7 us
    all_to_all x1, starting transfers between devices, shards(): lax.all_to_all(from_tiles(embeddings), 'grid', split_axis=1, concat_axis=...  18.7 us
  transfers between devices with their start and end apart: 10, of which 8 were waited for; matrix products, arithmetic and copies ran while one was open for 2% of the time, Pallas kernels for 0%

commit v1 on v0

v1 whole, which is shorter than its diff:
```python
import functools

import jax
import jax.numpy as jnp
from jax import lax
from jax.experimental import pallas as pl
from jax.experimental.pallas import tpu as pltpu
from jax.sharding import PartitionSpec as P

HEADS = 8
HEAD = 64
D = 512
TILE = 128
FRAME = 256
RUN = 32
GROUPS = 64
TOKENS = 32
EPS = 1e-06
SCALE = 0.125
NEG = -1e30
BF = jnp.bfloat16
F32 = jnp.float32
I32 = jnp.int32


def nn(a, b):
    return lax.dot_general(a, b, (((1,), (0,)), ((), ())), preferred_element_type=F32)


def nt(a, b):
    return lax.dot_general(a, b, (((1,), (1,)), ((), ())), preferred_element_type=F32)


def tn(a, b):
    return lax.dot_general(a, b, (((0,), (0,)), ((), ())), preferred_element_type=F32)


def iota(shape, dim):
    return lax.broadcasted_iota(I32, shape, dim)


def onehot(cond):
    return jnp.where(cond, 1.0, 0.0).astype(BF)


def own_slots(counts, spots):
    base = counts[0]
    place = spots // RUN
    slot = jnp.full(spots.shape, -1, I32)
    for p in range(TILE // RUN):
        rank = counts[p] + spots % RUN
        target = (rank % GROUPS) * 2 + (rank - base) // GROUPS
        slot = jnp.where((place == p) & (counts[p + 1] > counts[p]), target, slot)
    return slot


def send_tokens_kernel(visible_ref, emb_ref, out_ref):
    first = lax.axis_index("grid") * TILE
    visible = visible_ref[...]
    counts = []
    for p in range(TILE // RUN + 1):
        below = jnp.where(visible < first + p * RUN, 1.0, 0.0)
        counts.append(jnp.sum(jnp.sum(below, axis=0, keepdims=True), axis=1, keepdims=True).astype(I32))
    slot = own_slots(counts, iota((1, TILE), 1))
    rows = iota((GROUPS * 8, TILE), 0)
    total = jnp.zeros((GROUPS * 8, TILE), F32)
    for part in range(4):
        total += nn(onehot(rows == slot * 4 + part), emb_ref[:, part * 128 : (part + 1) * 128])
    out_ref[...] = total.astype(BF)


def per_head(rows):
    stacked = jnp.concatenate([rows] * HEADS, axis=0)
    shape = stacked.shape
    same = iota(shape, 0) // TOKENS == iota(shape, 1) // HEAD
    return jnp.where(same, stacked.astype(F32), 0.0).astype(BF)


def fold_heads(stacked):
    shape = stacked.shape
    same = iota(shape, 0) // TOKENS == iota(shape, 1) // HEAD
    kept = jnp.where(same, stacked, 0.0)
    total = kept[:TOKENS]
    for h in range(1, HEADS):
        total += kept[h * TOKENS : (h + 1) * TOKENS]
    return total


def group_match(low_ref, high_ref):
    ranks = iota((TOKENS, GROUPS * 8), 0) * GROUPS + lax.axis_index("grid")
    return (ranks >= low_ref[...]) & (ranks < high_ref[...])


def encode_kernel(recv_ref, low1_ref, high1_ref, low2_ref, high2_ref, qkv_ref, out_ref, tokens_ref, proj_ref, probs_ref):
    match1 = group_match(low1_ref, high1_ref)
    lanes = iota((TOKENS, GROUPS * 8), 1)
    recv = recv_ref[...]
    tokens = jnp.concatenate(
        [nn(onehot(match1 & (lanes % 4 == part)), recv) for part in range(4)], axis=1
    )
    tokens_ref[...] = tokens
    normed = (tokens * lax.rsqrt(jnp.mean(tokens * tokens, axis=1, keepdims=True) + EPS)).astype(BF)
    proj = nn(normed, qkv_ref[...]).astype(BF)
    proj_ref[...] = proj
    scores = nt(per_head(proj[:, :D]), proj[:, D : 2 * D]) * SCALE
    weights = jnp.exp(scores - jnp.max(scores, axis=1, keepdims=True))
    probs = weights / jnp.sum(weights, axis=1, keepdims=True)
    probs_ref[...] = probs
    context = fold_heads(nn(probs.astype(BF), proj[:, 2 * D :])).astype(BF)
    match2 = group_match(low2_ref, high2_ref)
    out = tn(onehot(match2 & (lanes % 2 == 0)), context[:, :256])
    out += tn(onehot(match2 & (lanes % 2 == 1)), context[:, 256:])
    out_ref[...] = out.astype(BF)


def decode_kernel(
    info_ref,
    recv_ref,
    embt_ref,
    og_ref,
    ogt_ref,
    wid_row_ref,
    wid_col_ref,
    mask_ref,
    enc_out_t_ref,
    qkv_t_ref,
    qkv_ref,
    proj_ref,
    out_ref,
    part_ref,
    dqkv_ref,
    ctx_ref,
):
    first = lax.axis_index("grid") * TILE
    begin, end = info_ref[9], info_ref[10]
    low, high = info_ref[11] - first, info_ref[12] - first
    lane = iota((1, FRAME), 1)
    place = lane // RUN
    rank = jnp.full((1, FRAME), -1, I32)
    for p in range(FRAME // RUN):
        seen = (place == p) & (info_ref[p + 1] > info_ref[p])
        rank = jnp.where(seen, info_ref[p] + lane % RUN, rank)
    live = (rank >= begin) & (rank < end)
    slot = jnp.where(live, (rank % GROUPS) * 4 + (rank - begin) // GROUPS, -1)
    owned = (lane >= low) & (lane < high)
    rows = iota((GROUPS * 8, FRAME), 0)
    pick = [onehot(rows == slot * 2 + half) for half in range(2)]

    recv = recv_ref[...]
    ctx_enc = jnp.concatenate([tn(recv, pick[half]) for half in range(2)], axis=0).astype(BF)
    encoded = (embt_ref[...].astype(F32) + nn(enc_out_t_ref[...], ctx_enc)).astype(BF)
    x = jnp.where(live, encoded.astype(F32), mask_ref[...])
    inv = lax.rsqrt(jnp.mean(x * x, axis=0, keepdims=True) + EPS)
    normed = (x * inv).astype(BF)
    qkv = nn(qkv_t_ref[...], normed).astype(BF)
    og_t = jnp.where(owned, ogt_ref[...].astype(F32), 0.0)
    dctx = nn(proj_ref[...], og_t.astype(BF)).astype(BF)
    keys = qkv[D : 2 * D].T
    vals = qkv[2 * D :].T

    col = iota((FRAME, 1), 0)
    owned_col = (col >= low) & (col < high)
    same = jnp.where(owned_col, wid_col_ref[...], -1 - col) == jnp.where(owned, wid_row_ref[...], -1 - lane)
    for h in range(HEADS):
        spot = slice(h * HEAD, (h + 1) * HEAD)
        q_t, k_t, v_t = qkv[spot], qkv[D + h * HEAD : D + (h + 1) * HEAD], qkv[2 * D + h * HEAD : 2 * D + (h + 1) * HEAD]
        d_t = dctx[spot]
        scores = jnp.where(same, nn(keys[:, spot], q_t) * SCALE, NEG)
        weights = jnp.exp(scores - jnp.max(scores, axis=0, keepdims=True))
        probs = weights * (1.0 / jnp.sum(weights, axis=0, keepdims=True))
        probs_b = probs.astype(BF)
        ctx_ref[spot, :] = jnp.where(owned, nn(v_t, probs_b), 0.0).astype(BF)
        dprobs = nn(vals[:, spot], d_t).astype(BF).astype(F32)
        inner = jnp.sum(probs * dprobs, axis=0, keepdims=True)
        dscores = (probs * (dprobs - inner) * SCALE).astype(BF)
        dqkv_ref[spot, :] = nn(k_t, dscores).astype(BF)
        dqkv_ref[D + h * HEAD : D + (h + 1) * HEAD, :] = nt(q_t, dscores).astype(BF)
        dqkv_ref[2 * D + h * HEAD : 2 * D + (h + 1) * HEAD, :] = nt(d_t, probs_b).astype(BF)

    dnormed = nn(qkv_ref[...], dqkv_ref[...])
    slope = inv * inv * inv * jnp.mean(x * dnormed, axis=0, keepdims=True)
    dx = (inv * dnormed - x * slope + og_t).astype(BF)
    dx_rows = dx.T
    out = nn(pick[0], dx_rows[:, :256]) + nn(pick[1], dx_rows[:, 256:])
    out_ref[...] = out.astype(BF)
    grad_enc = nn(ctx_enc, dx_rows).astype(BF)
    grad_dec = nn(ctx_ref[...], og_ref[...]).astype(BF)
    for s in range(8):
        spot = slice(s * 64, (s + 1) * 64)
        part_ref[s] = jnp.concatenate([grad_enc[:, spot], grad_dec[:, spot]], axis=1)


def encode_back_kernel(
    recv_ref, parts_ref, low1_ref, high1_ref, low2_ref, high2_ref, tokens_ref, proj_ref, probs_ref, qkv_ref, enc_out_ref, out_ref
):
    match2 = group_match(low2_ref, high2_ref)
    lanes = iota((TOKENS, GROUPS * 8), 1)
    recv = recv_ref[...]
    grad = jnp.concatenate(
        [nn(onehot(match2 & (lanes % 2 == half)), recv) for half in range(2)], axis=1
    )
    proj = proj_ref[...]
    probs = probs_ref[...]
    dctx = per_head(nt(grad.astype(BF), enc_out_ref[...]).astype(BF))
    dprobs = nt(dctx, proj[:, 2 * D :]).astype(BF).astype(F32)
    inner = jnp.sum(probs * dprobs, axis=1, keepdims=True)
    dscores = (probs * (dprobs - inner) * SCALE).astype(BF)
    dq = fold_heads(nn(dscores, proj[:, D : 2 * D]))
    dk = tn(dscores, per_head(proj[:, :D]))
    dv = tn(probs.astype(BF), dctx)
    dproj = jnp.concatenate([dq, dk, dv], axis=1).astype(BF)
    dnormed = nt(dproj, qkv_ref[...]).astype(BF).astype(F32)
    x = tokens_ref[...]
    inv = lax.rsqrt(jnp.mean(x * x, axis=1, keepdims=True) + EPS)
    slope = inv * inv * inv * jnp.mean(x * dnormed, axis=1, keepdims=True)
    dtokens = (grad + (inv * dnormed - x * slope)).astype(BF)
    match1 = group_match(low1_ref, high1_ref)
    out = jnp.zeros((GROUPS * 8, 128), F32)
    for part in range(4):
        out += tn(onehot(match1 & (lanes % 4 == part)), dtokens[:, part * 128 : (part + 1) * 128])
    out_ref[:, :128] = out.astype(BF)
    total = parts_ref[0].astype(F32)
    for s in range(1, 8):
        total += parts_ref[s].astype(F32)
    out_ref[:, 128:] = total.astype(BF)


def finish_kernel(info_ref, recv_ref, tiles_ref, enc_ref, dec_ref):
    counts = [info_ref[p] for p in range(TILE // RUN + 1)]
    slot = own_slots(counts, iota((TILE, 1), 0))
    lanes = iota((TILE, GROUPS * 8), 1)
    recv = recv_ref[:, :128]
    for part in range(4):
        tiles_ref[:, part * 128 : (part + 1) * 128] = nn(onehot(lanes == slot * 4 + part), recv).astype(BF)
    rows = recv_ref[:, 128:].astype(F32).reshape(GROUPS, 8, 128)
    total = jnp.sum(rows, axis=0)
    enc_ref[...] = total[:, :64]
    dec_ref[...] = total[:, 64:]


VM = pl.BlockSpec(memory_space=pltpu.VMEM)
SM = pl.BlockSpec(memory_space=pltpu.SMEM)


def call(kernel, shapes, args, name, scratch=(), scalars=0):
    outs = [jax.ShapeDtypeStruct(s, t) for s, t in shapes]
    return pl.pallas_call(
        kernel,
        out_shape=outs,
        in_specs=[SM] * scalars + [VM] * (len(args) - scalars),
        out_specs=[VM] * len(outs),
        scratch_shapes=list(scratch),
        compiler_params=pltpu.CompilerParams(vmem_limit_bytes=40 * 1024 * 1024),
        name=name,
    )(*args)


def exchange(rows, axis):
    return lax.all_to_all(rows, axis, split_axis=0, concat_axis=0, tiled=True)


def slot_bounds(starts, turns):
    low = starts[:-1, None] + GROUPS * jnp.arange(turns, dtype=I32)[None, :]
    high = jnp.minimum(low + GROUPS, starts[1:, None])
    wide = [jnp.repeat(b.reshape(-1), 8 // turns).reshape(1, GROUPS * 8) for b in (low, high)]
    return wide


def shards(
    embeddings,
    visible,
    window_id,
    output_gradient,
    mask_token,
    enc_qkv,
    enc_out,
    dec_qkv,
    decoder_projected,
):
    emb = embeddings[0]
    og = output_gradient[0]
    (send1,) = call(
        send_tokens_kernel,
        [((GROUPS * 8, 128), BF)],
        (visible.reshape(16, 128), emb),
        "send_tokens",
    )
    recv1 = exchange(send1, "grid")

    d = lax.axis_index("grid")
    runs = visible.reshape(GROUPS, RUN)[:, 0] // RUN
    edge = jnp.arange(GROUPS + 1, dtype=I32)
    start1 = RUN * jnp.sum((runs[None, :] < 4 * edge[:, None]).astype(I32), axis=1)
    wid = window_id.reshape(GROUPS, TILE)
    before = jnp.concatenate([jnp.full((1,), -1, I32), wid[:-1, -1]])
    head = edge[:-1] * TILE + jnp.sum((wid == before[:, None]).astype(I32), axis=1)
    head = jnp.concatenate([head, jnp.full((1,), GROUPS * TILE, I32)])
    start2 = jnp.sum(jnp.clip(head[:, None] - RUN * runs[None, :], 0, RUN), axis=1)
    low1, high1 = slot_bounds(start1, 2)
    low2, high2 = slot_bounds(start2, 4)
    frame_runs = 4 * d + jnp.arange(9, dtype=I32)
    frame_counts = RUN * jnp.sum((runs[None, :] < frame_runs[:, None]).astype(I32), axis=1)
    info = jnp.concatenate(
        [
            frame_counts,
            lax.dynamic_slice_in_dim(start2, d, 2),
            lax.dynamic_slice_in_dim(head, d, 2),
        ]
    )
    wid_pad = jnp.concatenate([window_id[0], jnp.full((TILE,), -1, I32)])
    wid_frame = lax.dynamic_slice_in_dim(wid_pad, d * TILE, FRAME)

    halo = lax.ppermute(
        jnp.concatenate([emb, og], axis=1), "grid", [(i + 1, i) for i in range(GROUPS - 1)]
    )
    emb_t = jnp.concatenate([emb, halo[:, :D]], axis=0).T
    og_frame = jnp.concatenate([og, halo[:, D:]], axis=0)

    send2, tokens, proj, probs = call(
        encode_kernel,
        [((GROUPS * 8, 256), BF), ((TOKENS, D), F32), ((TOKENS, 3 * D), BF), ((HEADS * TOKENS, TOKENS), F32)],
        (recv1, low1, high1, low2, high2, enc_qkv),
        "encode",
    )
    recv2 = exchange(send2, "grid")
    send3, parts = call(
        decode_kernel,
        [((GROUPS * 8, 256), BF), ((8, D, 128), BF)],
        (
            info,
            recv2,
            emb_t,
            og_frame,
            og_frame.T,
            wid_frame[None, :],
            wid_frame[:, None],
            mask_token[:, None],
            enc_out.T,
            dec_qkv.T,
            dec_qkv,
            decoder_projected,
        ),
        "decode",
        scratch=[pltpu.VMEM((3 * D, FRAME), BF), pltpu.VMEM((D, FRAME), BF)],
        scalars=1,
    )
    recv3 = exchange(send3, "grid")
    parts = exchange(parts, "slide")
    (send4,) = call(
        encode_back_kernel,
        [((GROUPS * 8, 256), BF)],
        (recv3, parts, low1, high1, low2, high2, tokens, proj, probs, enc_qkv, enc_out),
        "encode_back",
    )
    recv4 = exchange(send4, "grid")
    tiles, grad_enc, grad_dec = call(
        finish_kernel,
        [((TILE, D), BF), ((8, 64), F32), ((8, 64), F32)],
        (info, recv4),
        "finish",
        scalars=1,
    )
    return tiles[None], grad_enc, grad_dec


def solution(mesh):
    placed = (
        P("slide", "grid", None),
        P("slide", None),
        P("slide", None),
        P("slide", "grid", None),
        P(),
        P(),
        P(),
        P(),
        P(),
    )
    return jax.shard_map(
        shards,
        mesh=mesh,
        in_specs=placed,
        out_specs=(P("slide", "grid", None), P("grid", "slide"), P("grid", "slide")),
        check_vma=False,
    )
```

time: 881 us -> 165 us (0.19)
  waiting for transfers between devices: 755 us -> 14.6 us
  blocking collectives: 0 us -> 73.7 us
  starting transfers between devices: 54.4 us -> 32.6 us
  Pallas kernels: 0 us -> 16.1 us
  between operations: 16.2 us -> 0.98 us
  matrix products: 13.9 us -> 0 us
    reduce_scatter x1 -> x0, waiting for transfers between devices: 674 us -> none  [shards(): lax.psum_scatter(stacked, 'grid', scatter_dimension=1, tiled=True)]
    all_to_all x0 -> x3, blocking collectives: none -> 73.7 us  [exchange(): return lax.all_to_all(rows, axis, split_axis=0, concat_axis=0, tiled=True)]
    unnamed x3 -> x0, waiting for transfers between devices: 35.7 us -> none
    all_to_all x4 -> x2, waiting for transfers between devices: 38.3 us -> 14.6 us  [exchange(): return lax.all_to_all(rows, axis, split_axis=0, concat_axis=0, tiled=True)]
    pallas_call x0 -> x5, Pallas kernels: none -> 16.1 us  [call(): pl.pallas_call(kernel, out_shape=outs, in_specs=[SM] * scalars + [VM] * (...]
    all_to_all x4 -> x2, starting transfers between devices: 40.2 us -> 28 us  [exchange(): return lax.all_to_all(rows, axis, split_axis=0, concat_axis=0, tiled=True)]
    dot_general x21 -> x0, matrix products: 11.1 us -> none  [the longest x6 2.53 us: attend(): jnp.einsum('...wvy,...ywj->...vwj', attention_probs, value_per_head)]
    ppermute x4 -> x1, starting transfers between devices: 14.1 us -> 4.57 us  [shards(): lax.ppermute(jnp.concatenate([emb, og], axis=1), 'grid', [(i + 1, i) for...]
  transfers between devices with their start and end apart: 10 -> 3, of which waited for: 8 -> 2; matrix products, arithmetic and copies ran while one was open for 2% -> 10% of each run, Pallas kernels for 0% -> 1%
where the time goes in v1:
time: 165 us; the launch traced here: 164 us
  blocking collectives  73.7 us (45%)
  starting transfers between devices  32.6 us (20%)
  local copies, waits for them, and re-layouts  21.3 us (13%)
  Pallas kernels  16.1 us (10%)
  waiting for transfers between devices  14.6 us (9%)
  other arithmetic  4.68 us (3%)
    all_to_all x3, blocking collectives, exchange(): return lax.all_to_all(rows, axis, split_axis=0, concat_axis=0, tiled=True)  73.7 us
    all_to_all x2, starting transfers between devices, exchange(): return lax.all_to_all(rows, axis, split_axis=0, concat_axis=0, tiled=True)  28 us
    pallas_call x5, Pallas kernels, call(): pl.pallas_call(kernel, out_shape=outs, in_specs=[SM] * scalars + [VM] * (...  16.1 us
    unnamed x56, local copies, waits for them, and re-layouts  15.4 us
    all_to_all x2, waiting for transfers between devices, exchange(): return lax.all_to_all(rows, axis, split_axis=0, concat_axis=0, tiled=True)  14.6 us
    ppermute x1, starting transfers between devices, shards(): lax.ppermute(jnp.concatenate([emb, og], axis=1), 'grid', [(i + 1, i) for...  4.57 us
  transfers between devices with their start and end apart: 3, of which 2 were waited for; matrix products, arithmetic and copies ran while one was open for 10% of the time, Pallas kernels for 1%

profile of v1, /device:TPU:8, one launch (start us, length us, event | category | flops | bytes accessed | tf_op | source)
XLA Modules:
  0.0 164.0 jit_solution(8224451077880099498)
XLA Ops:
  0.7 1.0 copy-done.9
  1.7 0.7 copy-done.16
  2.4 1.1 send_tokens.1
  3.5 18.7 %all-to-all-start = ((bf16[64,8,128]{2,1,0:T(8,128)(2,1)}), bf16[64,8,128]{2,1,0:T(8,128)(2,1)S(1)}, u32[]{:S(2)}, u32[]{:S(2)}) async-start(bf16[64,8,128]{2,1,0:T(8,128)(2,1)} %bitcast.5), calls=%async_computation | async-start | bytes 262144 | tf_op jit(solution)/shard_map/all_to_all | solution.py:259
  22.2 1.0 copy.39
  23.2 1.1 copy.41
  24.3 0.8 pad_maximum_fusion
  25.1 4.6 %collective-permute-start = (bf16[128,1024]{0,1:T(8,128)(2,1)}, bf16[128,1024]{0,1:T(8,128)(2,1)}, u32[]{:S(2)}, u32[]{:S(2)}) collective-permute-start(bf16[128,1024]{0,1:T(8,128)(2,1)} %pad_maximum_fusion), channel_id=1, source_target_pairs={{1,0},{2,1},{3,2},{4,3},{5,4},{6,5},{7,6},{8,7},{9,8},{10,9},{11,1... | collective-permute-start | bytes 786440 | tf_op jit(solution)/shard_map/ppermute | solution.py:313
  29.7 0.5 broadcast.124
  30.2 0.7 reduce.5
  31.0 0.1 slice_reduce_fusion
  31.3 0.2 convert_reduce_fusion.1
  32.2 0.1 min.33
  32.4 0.1 add.87
  32.6 0.1 min.36
  32.9 0.1 reshape_reshape.12.low1_ref
  33.1 0.1 reshape_reshape.13.high1_ref
  33.3 0.1 reshape_reshape.14.low2_ref
  33.6 0.1 reshape_reshape.15.high2_ref
  33.7 4.0 %all-to-all-done = bf16[64,8,128]{2,1,0:T(8,128)(2,1)S(1)} async-done(((bf16[64,8,128]{2,1,0:T(8,128)(2,1)}), bf16[64,8,128]{2,1,0:T(8,128)(2,1)S(1)}, u32[]{:S(2)}, u32[]{:S(2)}) %all-to-all-start) | async-done | bytes 131104 | tf_op jit(solution)/shard_map/all_to_all | solution.py:259
  37.7 2.2 %encode.1 = (bf16[512,256]{1,0:T(8,128)(2,1)}, f32[32,512]{1,0:T(8,128)S(1)}, bf16[32,1536]{1,0:T(8,128)(2,1)S(1)}, f32[256,32]{1,0:T(8,128)S(1)}) custom-call(bf16[512,128]{1,0:T(8,128)(2,1)S(1)} %bitcast.31, s32[1,512]{1,0:T(1,128)S(1)} %reshape_reshape.12.low1_ref, s32[1,512]{1,0:T(1,128)S(1)} %reshape_reshape.13.high1_ref, ...), custom_call_target="tpu_custom_call" | custom-call | tf_op jit(solution)/shard_map/encode/pallas_call | solution.py:247
  39.9 0.7 copy-done.10
  40.5 0.6 copy-done.12
  41.2 0.6 copy-done.14
  41.8 9.3 %all-to-all-start.1 = ((bf16[64,8,256]{2,1,0:T(8,128)(2,1)}), bf16[64,8,256]{2,1,0:T(8,128)(2,1)}, u32[]{:S(2)}, u32[]{:S(2)}) async-start(bf16[64,8,256]{2,1,0:T(8,128)(2,1)} %bitcast.7), calls=%async_computation.1 | async-start | bytes 524288 | tf_op jit(solution)/shard_map/all_to_all | solution.py:259
  51.2 0.1 copy.45.wid_col_ref
  51.3 0.9 copy.46.mask_ref
  52.2 2.1 %copy.42 = bf16[512,512]{0,1:T(8,128)(2,1)} copy(bf16[512,512]{1,0:T(8,128)(2,1)} %enc_out_ref.1) | data formatting | bytes 1048576 | tf_op args[6]
  54.3 0.7 copy.43
  55.0 0.2 convert_reduce_fusion.2
  55.2 0.6 pad_add_fusion.2.info_ref
  55.8 1.0 fusion.1
  56.8 1.8 %fusion = (bf16[512,256]{1,0:T(8,128)(2,1)S(1)}, bf16[256,512]{0,1:T(8,128)(2,1)}, bf16[512,256]{1,0:T(8,128)(2,1)}) fusion(bf16[128,512]{0,1:T(8,128)(2,1)S(1)} %get-tuple-element.25, bf16[128,512]{0,1:T(8,128)(2,1)} %bitcast.39, bf16[128,512]{0,1:T(8,128)(2,1)S(1)} %get-tuple-element.26, bf16[128,512]{0,1:T(8,128)(2,1)} %bitcast.37), kind=kLoop, calls=%fused_computation.28 | loop fusion | flops 1048576 | bytes 1310720 | tf_op jit(solution)/shard_map/transpose | solution.py:334
  58.6 1.8 %copy.44.og_ref = bf16[256,512]{1,0:T(8,128)(2,1)} copy(bf16[256,512]{0,1:T(8,128)(2,1)} %get-tuple-element.24) | data formatting | bytes 524288 | tf_op jit(solution)/shard_map/concatenate | solution.py:317
  60.4 10.6 %all-to-all-done.1 = bf16[64,8,256]{2,1,0:T(8,128)(2,1)} async-done(((bf16[64,8,256]{2,1,0:T(8,128)(2,1)}), bf16[64,8,256]{2,1,0:T(8,128)(2,1)}, u32[]{:S(2)}, u32[]{:S(2)}) %all-to-all-start.1) | async-done | bytes 262176 | tf_op jit(solution)/shard_map/all_to_all | solution.py:259
  71.1 1.0 copy-done.4
  72.1 0.9 copy-done.5
  73.1 0.9 copy-done.6
  74.0 0.9 copy-done.7
  75.0 1.0 copy-done.8
  76.0 0.7 copy-done.19
  76.7 0.7 copy-done.20
  77.3 9.2 %decode.1 = (bf16[512,256]{1,0:T(8,128)(2,1)S(1)}, bf16[8,512,128]{2,1,0:T(8,128)(2,1)S(1)}) custom-call(s32[13]{0:T(128)S(1)} %copy-done.20, bf16[512,256]{1,0:T(8,128)(2,1)} %bitcast.8.recv_ref, bf16[512,256]{1,0:T(8,128)(2,1)S(1)} %copy-done.5, bf16[256,512]{1,0:T(8,128)(2,1)S(1)} %copy-done.7, bf16[512,256]{1,0:T(8,128)(2,1)S(1)} %get-tuple-element.23.ogt_ref, ...), custom_call_target="tpu_custom_call" | custom-call | tf_op jit(solution)/shard_map/decode/pallas_call | solution.py:247
  86.6 20.3 %all_to_all.49.parts_ref = bf16[8,512,128]{2,1,0:T(8,128)(2,1)S(1)} all-to-all(bf16[8,512,128]{2,1,0:T(8,128)(2,1)S(1)} %get-tuple-element.14), channel_id=1, replica_groups=mesh['slide'=8,'grid'=64] {'slide'}, dimensions={0} | all-to-all | bytes 2097152 | tf_op jit(solution)/shard_map/all_to_all | solution.py:259
  107.0 26.8 %all_to_all.50 = bf16[64,8,256]{2,1,0:T(8,128)(2,1)S(1)} all-to-all(bf16[64,8,256]{2,1,0:T(8,128)(2,1)S(1)} %bitcast.32), channel_id=1, replica_groups=mesh['slide'=8,'grid'=64] {'grid'}, dimensions={0} | all-to-all | bytes 524288 | tf_op jit(solution)/shard_map/all_to_all | solution.py:259
  133.8 2.0 %encode_back.1 = bf16[512,256]{1,0:T(8,128)(2,1)S(1)} custom-call(bf16[512,256]{1,0:T(8,128)(2,1)S(1)} %bitcast.28, bf16[8,512,128]{2,1,0:T(8,128)(2,1)S(1)} %all_to_all.49.parts_ref, s32[1,512]{1,0:T(1,128)S(1)} %reshape_reshape.12.low1_ref, s32[1,512]{1,0:T(1,128)S(1)} %reshape_reshape.13.high1_ref, s32[1,512]{1,0:T(1,128)S(1)} %reshape_reshape.14.low2_ref, ...), custom_call_target="tpu_custom_call" | custom-call | tf_op jit(solution)/shard_map/encode_back/pallas_call | solution.py:247
  135.9 26.6 %all_to_all.51 = bf16[64,8,256]{2,1,0:T(8,128)(2,1)S(1)} all-to-all(bf16[64,8,256]{2,1,0:T(8,128)(2,1)S(1)} %bitcast.29), channel_id=1, replica_groups=mesh['slide'=8,'grid'=64] {'grid'}, dimensions={0} | all-to-all | bytes 524288 | tf_op jit(solution)/shard_map/all_to_all | solution.py:259
  162.5 1.6 finish.1
  (70 shorter events, 1.7 us)
Async XLA Ops:
  0.6 37.1 %copy-start.1 = (bf16[512,1536]{1,0:T(8,128)(2,1)S(1)}, bf16[512,1536]{1,0:T(8,128)(2,1)}, u32[]{:S(2)}) copy-start(bf16[512,1536]{1,0:T(8,128)(2,1)} %qkv_ref.5) | copy-start | bytes 4718596
  0.6 1.0 copy-start.9
  1.7 0.7 copy-start.16
  2.4 27.9 %copy-start.17 = (s32[1,2048]{1,0:T(1,128)S(1)}, s32[1,2048]{1,0:T(1,128)}, u32[]{:S(2)}) copy-start(s32[1,2048]{1,0:T(1,128)} %param.10) | copy-start | bytes 24580
  2.4 28.7 %copy-start.23 = (s32[1,8192]{1,0:T(1,128)S(1)}, s32[1,8192]{1,0:T(1,128)}, u32[]{:S(2)}) copy-start(s32[1,8192]{1,0:T(1,128)} %param.11) | copy-start | bytes 98308
  3.5 34.2 %all-to-all-start = ((bf16[64,8,128]{2,1,0:T(8,128)(2,1)}), bf16[64,8,128]{2,1,0:T(8,128)(2,1)S(1)}, u32[]{:S(2)}, u32[]{:S(2)}) async-start(bf16[64,8,128]{2,1,0:T(8,128)(2,1)} %bitcast.5), calls=%async_computation | async-start | bytes 262144 | tf_op jit(solution)/shard_map/all_to_all | solution.py:259
  23.2 10.0 %copy-start.21 = (bf16[1,128,512]{1,2,0:T(8,128)(2,1)}, bf16[1,128,512]{1,2,0:T(8,128)(2,1)S(1)}, u32[]{:S(2)}) copy-start(bf16[1,128,512]{1,2,0:T(8,128)(2,1)S(1)} %copy.39) | copy-start | bytes 393220
  24.3 13.4 %copy-start.22 = (bf16[1,128,512]{1,2,0:T(8,128)(2,1)}, bf16[1,128,512]{1,2,0:T(8,128)(2,1)S(1)}, u32[]{:S(2)}) copy-start(bf16[1,128,512]{1,2,0:T(8,128)(2,1)S(1)} %copy.41) | copy-start | bytes 393220
  25.1 30.7 %collective-permute-start = (bf16[128,1024]{0,1:T(8,128)(2,1)}, bf16[128,1024]{0,1:T(8,128)(2,1)}, u32[]{:S(2)}, u32[]{:S(2)}) collective-permute-start(bf16[128,1024]{0,1:T(8,128)(2,1)} %pad_maximum_fusion), channel_id=1, source_target_pairs={{1,0},{2,1},{3,2},{4,3},{5,4},{6,5},{7,6},{8,7},{9,8},{10,9},{11,1... | collective-permute-start | bytes 786440 | tf_op jit(solution)/shard_map/ppermute | solution.py:313
  32.9 18.4 %copy-start.24 = (f32[512]{0:T(512)S(1)}, f32[512]{0:T(512)}, u32[]{:S(2)}) copy-start(f32[512]{0:T(512)} %param.13) | copy-start | bytes 6148
  37.7 16.6 %copy-start = (bf16[512,1536]{1,0:T(8,128)(2,1)S(1)}, bf16[512,1536]{1,0:T(8,128)(2,1)}, u32[]{:S(2)}) copy-start(bf16[512,1536]{1,0:T(8,128)(2,1)} %qkv_ref.4) | copy-start | bytes 4718596
  39.9 0.7 copy-start.10
  40.5 0.6 copy-start.12
  41.2 0.6 copy-start.14
  41.8 29.3 %all-to-all-start.1 = ((bf16[64,8,256]{2,1,0:T(8,128)(2,1)}), bf16[64,8,256]{2,1,0:T(8,128)(2,1)}, u32[]{:S(2)}, u32[]{:S(2)}) async-start(bf16[64,8,256]{2,1,0:T(8,128)(2,1)} %bitcast.7), calls=%async_computation.1 | async-start | bytes 524288 | tf_op jit(solution)/shard_map/all_to_all | solution.py:259
  51.2 3.8 %copy-start.18 = (s32[256]{0:T(256)}, s32[256]{0:T(256)S(1)}, u32[]{:S(2)}) copy-start(s32[256]{0:T(256)S(1)} %pad_dynamic-slice_fusion) | copy-start | bytes 3076
  71.1 1.0 copy-start.4
  72.1 0.9 copy-start.5
  73.1 0.9 copy-start.6
  74.0 0.9 copy-start.7
  75.0 1.0 copy-start.8
  76.0 0.7 copy-start.19
  76.7 0.7 copy-start.20
  86.6 47.2 %copy-start.2 = (bf16[512,1536]{1,0:T(8,128)(2,1)S(1)}, bf16[512,1536]{1,0:T(8,128)(2,1)}, u32[]{:S(2)}) copy-start(bf16[512,1536]{1,0:T(8,128)(2,1)} %qkv_ref.5) | copy-start | bytes 4718596
  86.6 47.2 %copy-start.3 = (bf16[512,512]{1,0:T(8,128)(2,1)S(1)}, bf16[512,512]{1,0:T(8,128)(2,1)}, u32[]{:S(2)}) copy-start(bf16[512,512]{1,0:T(8,128)(2,1)} %enc_out_ref.1) | copy-start | bytes 1572868
  86.6 47.2 %copy-start.11 = (f32[256,32]{1,0:T(8,128)S(1)}, f32[256,32]{1,0:T(8,128)}, u32[]{:S(2)}) copy-start(f32[256,32]{1,0:T(8,128)} %copy-done.10) | copy-start | bytes 98308
  86.6 47.2 %copy-start.13 = (bf16[32,1536]{1,0:T(8,128)(2,1)S(1)}, bf16[32,1536]{1,0:T(8,128)(2,1)}, u32[]{:S(2)}) copy-start(bf16[32,1536]{1,0:T(8,128)(2,1)} %copy-done.12) | copy-start | bytes 294916
  86.6 47.2 %copy-start.15 = (f32[32,512]{1,0:T(8,128)S(1)}, f32[32,512]{1,0:T(8,128)}, u32[]{:S(2)}) copy-start(f32[32,512]{1,0:T(8,128)} %copy-done.14) | copy-start | bytes 196612

commit v2 on v1

v2 whole, which is shorter than its diff:
```python
import jax
import jax.numpy as jnp
from jax import lax
from jax.experimental import pallas as pl
from jax.experimental.pallas import tpu as pltpu
from jax.sharding import PartitionSpec as P

HEADS = 8
HEAD = 64
D = 512
TILE = 128
FRAME = 256
RUN = 32
GROUPS = 64
TOKENS = 32
EPS = 1e-06
SCALE = 0.125
NEG = -1e30
BF = jnp.bfloat16
F32 = jnp.float32
I32 = jnp.int32


def nn(a, b):
    return lax.dot_general(a, b, (((1,), (0,)), ((), ())), preferred_element_type=F32)


def nt(a, b):
    return lax.dot_general(a, b, (((1,), (1,)), ((), ())), preferred_element_type=F32)


def tn(a, b):
    return lax.dot_general(a, b, (((0,), (0,)), ((), ())), preferred_element_type=F32)


def iota(shape, dim):
    return lax.broadcasted_iota(I32, shape, dim)


def onehot(cond):
    return jnp.where(cond, 1.0, 0.0).astype(BF)


class Load:
    def __init__(self, source, held, sems, first, parts=1):
        self.held = held
        rows = held.shape[0] // parts
        spots = [slice(i * rows, (i + 1) * rows) for i in range(parts)]
        self.copies = [
            pltpu.make_async_copy(source.at[spot], held.at[spot], sems.at[first + i]) for i, spot in enumerate(spots)
        ]
        for copy in self.copies:
            copy.start()

    def __call__(self):
        for copy in self.copies:
            copy.wait()
        self.copies = []
        return self.held


def run_counts(visible_ref, limit):
    total = jnp.zeros(limit.shape, I32)
    for q in range(4):
        firsts = visible_ref[:, q * RUN : q * RUN + 1]
        total += jnp.sum(jnp.where(firsts < limit, 1, 0), axis=0, keepdims=True)
    return total


def frame_ranks(visible_ref, first, width):
    lane = iota((1, width), 1)
    limit = first + lane - (lane & (RUN - 1))
    seen = run_counts(visible_ref, limit)
    present = run_counts(visible_ref, limit + RUN) > seen
    return seen * RUN + (lane & (RUN - 1)), present


def own_slots(visible_ref, first):
    rank, present = frame_ranks(visible_ref, first, TILE)
    base = RUN * run_counts(visible_ref, jnp.broadcast_to(first, (1, TILE)))
    return jnp.where(present, (rank & (GROUPS - 1)) * 2 + ((rank - base) >> 6), -1)


def send_tokens_kernel(visible_hbm, emb_hbm, out_ref, visible_b, emb_b, sems):
    visible = Load(visible_hbm, visible_b, sems, 0)
    emb = Load(emb_hbm, emb_b, sems, 1)
    slot = own_slots(visible(), lax.axis_index("grid") * TILE)
    rows = iota((GROUPS * 8, TILE), 0)
    picks = [onehot(rows == slot * 4 + part) for part in range(4)]
    emb_ref = emb()
    total = jnp.zeros((GROUPS * 8, TILE), F32)
    for part in range(4):
        total += nn(picks[part], emb_ref[:, part * 128 : (part + 1) * 128])
    out_ref[...] = total.astype(BF)


def plan_kernel(visible_ref, wid_ref, enc_qkv_ref, marks_ref, enc_ref):
    enc_ref[...] = enc_qkv_ref[...]
    d = lax.axis_index("grid")
    first = d * TILE
    lane = iota((1, GROUPS * 8), 1)
    peer = lane >> 3
    start1 = RUN * run_counts(visible_ref, peer * TILE)
    stop1 = RUN * run_counts(visible_ref, peer * TILE + TILE)
    low1 = start1 + GROUPS * ((lane >> 2) & 1)
    marks_ref[0:1, :] = low1
    marks_ref[1:2, :] = jnp.minimum(low1 + GROUPS, stop1)

    wid = wid_ref[...]
    last = wid[:, TILE - 1 :]
    before = jnp.concatenate([jnp.full((1, 1), -1, I32), last[:-1]], axis=0)
    more = jnp.sum(jnp.where(wid == before, 1.0, 0.0), axis=1, keepdims=True).astype(I32)
    head = iota((GROUPS, 1), 0) * TILE + more
    rows = iota((GROUPS, GROUPS * 8), 0)
    begin = jnp.sum(jnp.where(rows == peer, head, 0), axis=0, keepdims=True)
    end = jnp.sum(jnp.where(rows == peer + 1, head, 0), axis=0, keepdims=True)
    end = jnp.where(peer == GROUPS - 1, GROUPS * TILE, end)

    def visible_below(tile):
        total = jnp.zeros(tile.shape, I32)
        for q in range(4):
            firsts = visible_ref[:, q * RUN : q * RUN + 1]
            total += jnp.sum(jnp.clip(tile - firsts, 0, RUN), axis=0, keepdims=True)
        return total

    start2, stop2 = visible_below(begin), visible_below(end)
    low2 = start2 + GROUPS * ((lane >> 1) & 3)
    marks_ref[2:3, :] = low2
    marks_ref[3:4, :] = jnp.minimum(low2 + GROUPS, stop2)
    marks_ref[4:8, :] = jnp.zeros((4, GROUPS * 8), I32)

    def mine(values):
        return jnp.sum(jnp.where(lane == d * 8, values.astype(F32), 0.0), axis=1, keepdims=True).astype(I32)

    start2, stop2, begin, end = mine(start2), mine(stop2), mine(begin), mine(end)
    rank, present = frame_ranks(visible_ref, first, FRAME)
    spot = iota((1, FRAME), 1)
    live = present & (rank >= start2) & (rank < stop2)
    owned = (first + spot >= begin) & (first + spot < end)
    marks_ref[4:5, :FRAME] = jnp.where(live, (rank & (GROUPS - 1)) * 4 + ((rank - start2) >> 6), -1)
    marks_ref[5:6, :FRAME] = jnp.where(owned, 1, 0)
    own = wid_ref[pl.ds(d, 1), :]
    after = wid_ref[pl.ds(jnp.minimum(d + 1, GROUPS - 1), 1), :]
    marks_ref[6:7, :FRAME] = jnp.where(owned, jnp.concatenate([own, after], axis=1), -1 - spot)
    marks_ref[7:8, :TILE] = own_slots(visible_ref, first)


OUT_T, BOTH, MORE, QKV, OG_ROWS, PACKED = 1536, 0, 512, 1024, 2560, 18432


def prepare_kernel(marks_ref, emb_ref, og_ref, halo_ref, proj_ref, enc_out_ref, qkv_ref, flipped_ref, packed_ref, held, sems):
    def ship(first, last, sem):
        copy = pltpu.make_async_copy(held.at[first:last], packed_ref.at[first:last], sems.at[sem])
        copy.start()
        return copy

    for i in range(3):
        held[QKV + i * D : QKV + (i + 1) * D, :] = qkv_ref[:, i * D : (i + 1) * D]
    copies = [ship(QKV, OG_ROWS, 0)]
    flipped_ref[:OUT_T, :] = qkv_ref[...].T
    flipped_ref[OUT_T:, :] = enc_out_ref[...].T
    owned = marks_ref[5:6, :FRAME] > 0
    held[OG_ROWS : OG_ROWS + TILE, :] = og_ref[...]
    held[OG_ROWS + TILE : OG_ROWS + FRAME, :] = halo_ref[:, D:]
    og_t = jnp.concatenate([og_ref[...].T, halo_ref[:, D:].T], axis=1).astype(F32)
    og_t = jnp.where(owned, og_t, 0.0).astype(BF)
    held[BOTH:MORE, :FRAME] = nn(proj_ref[...], og_t).astype(BF)
    held[BOTH:MORE, FRAME:] = og_t
    held[MORE : MORE + D, :FRAME] = jnp.concatenate([emb_ref[...].T, halo_ref[:, :D].T], axis=1)
    across = jnp.broadcast_to(marks_ref[6:7, :FRAME], (FRAME, FRAME))
    held[MORE : MORE + FRAME, FRAME:] = jnp.where(across == across.T, 0.0, NEG).astype(BF)
    held[MORE + FRAME : MORE + D, FRAME:] = jnp.zeros((FRAME, FRAME), BF)
    copies.append(ship(OG_ROWS, OG_ROWS + FRAME, 1))
    copies.append(ship(BOTH, QKV, 2))
    for copy in copies:
        copy.wait()


def per_head(rows):
    stacked = jnp.concatenate([rows] * HEADS, axis=0)
    shape = stacked.shape
    same = iota(shape, 0) // TOKENS == iota(shape, 1) // HEAD
    return jnp.where(same, stacked.astype(F32), 0.0).astype(BF)


def fold_heads(stacked):
    shape = stacked.shape
    same = iota(shape, 0) // TOKENS == iota(shape, 1) // HEAD
    kept = jnp.where(same, stacked, 0.0)
    total = kept[:TOKENS]
    for h in range(1, HEADS):
        total += kept[h * TOKENS : (h + 1) * TOKENS]
    return total


def group_match(bounds_ref, row):
    ranks = iota((TOKENS, GROUPS * 8), 0) * GROUPS + lax.axis_index("grid")
    return (ranks >= bounds_ref[row : row + 1, :]) & (ranks < bounds_ref[row + 1 : row + 2, :])


def encoder_probs(queries, keys):
    scores = nt(per_head(queries), keys) * SCALE
    weights = jnp.exp(scores - jnp.max(scores, axis=1, keepdims=True))
    return weights / jnp.sum(weights, axis=1, keepdims=True)


def encode_kernel(recv_ref, marks_ref, weight_ref, out_ref, kept_ref):
    match1 = group_match(marks_ref, 0)
    lanes = iota((TOKENS, GROUPS * 8), 1)
    recv = recv_ref[...]
    x = jnp.concatenate([nn(onehot(match1 & (lanes % 4 == part)), recv) for part in range(4)], axis=1)
    kept_ref[:TOKENS, :] = x.astype(BF)
    normed = (x * lax.rsqrt(jnp.mean(x * x, axis=1, keepdims=True) + EPS)).astype(BF)
    qkv = nn(normed, weight_ref[...]).astype(BF)
    for i in range(3):
        kept_ref[(i + 1) * TOKENS : (i + 2) * TOKENS, :] = qkv[:, i * D : (i + 1) * D]
    soft = encoder_probs(qkv[:, :D], qkv[:, D : 2 * D])
    context = fold_heads(nn(soft.astype(BF), qkv[:, 2 * D :])).astype(BF)
    match2 = group_match(marks_ref, 2)
    out = tn(onehot(match2 & (lanes % 2 == 0)), context[:, :256])
    out += tn(onehot(match2 & (lanes % 2 == 1)), context[:, 256:])
    out_ref[...] = out.astype(BF)


def decode_kernel(marks_ref, recv_ref, mask_ref, flipped_ref, packed, out_ref, keep_ref, send_ref, more_b, both_b, qkv_b, og_b, dqkv_ref, ctx_ref, sems):
    more = Load(packed.at[MORE:QKV], more_b, sems, 0)
    both = Load(packed.at[BOTH:MORE], both_b, sems, 1)
    qkv_w = Load(packed.at[QKV:OG_ROWS], qkv_b, sems, 2)
    og_rows = Load(packed.at[OG_ROWS : OG_ROWS + FRAME], og_b, sems, 3)
    slot = marks_ref[4:5, :FRAME]
    live = slot >= 0
    owned = marks_ref[5:6, :FRAME] > 0
    blank = jnp.broadcast_to(mask_ref[...], (TILE, D)).T[:, :1]
    rows = iota((GROUPS * 8, FRAME), 0)
    pick = [onehot(rows == slot * 2 + half) for half in range(2)]
    recv = recv_ref[...]
    ctx_enc = jnp.concatenate([tn(recv, pick[half]) for half in range(2)], axis=0).astype(BF)
    delta = nn(flipped_ref[OUT_T:, :], ctx_enc)
    x = jnp.where(live, (more()[:, :FRAME].astype(F32) + delta).astype(BF).astype(F32), blank)
    inv = lax.rsqrt(jnp.mean(x * x, axis=0, keepdims=True) + EPS)
    normed = (x * inv).astype(BF)
    qkv = nn(flipped_ref[:OUT_T, :], normed).astype(BF)
    keys = qkv[D : 2 * D].T
    vals = qkv[2 * D :].T
    bias_rows = more()[:FRAME, FRAME:].astype(F32)
    both_b = both()
    for h in range(HEADS):
        spot = slice(h * HEAD, (h + 1) * HEAD)
        q_t, k_t, v_t = qkv[spot], qkv[D + h * HEAD : D + (h + 1) * HEAD], qkv[2 * D + h * HEAD : 2 * D + (h + 1) * HEAD]
        d_t = both_b[spot, :FRAME]
        scores = nn(keys[:, spot], q_t) * SCALE + bias_rows
        weights = jnp.exp(scores - jnp.max(scores, axis=0, keepdims=True))
        probs = weights * (1.0 / jnp.sum(weights, axis=0, keepdims=True))
        probs_b = probs.astype(BF)
        ctx_ref[spot, :] = jnp.where(owned, nn(v_t, probs_b), 0.0).astype(BF)
        dprobs = nn(vals[:, spot], d_t).astype(BF).astype(F32)
        inner = jnp.sum(probs * dprobs, axis=0, keepdims=True)
        dscores = (probs * (dprobs - inner) * SCALE).astype(BF)
        dqkv_ref[spot, :] = nn(k_t, dscores).astype(BF)
        dqkv_ref[D + h * HEAD : D + (h + 1) * HEAD, :] = nt(q_t, dscores).astype(BF)
        dqkv_ref[2 * D + h * HEAD : 2 * D + (h + 1) * HEAD, :] = nt(d_t, probs_b).astype(BF)

    weight_ref = qkv_w()
    dnormed = nn(weight_ref[:D, :], dqkv_ref[:D, :])
    for i in range(1, 3):
        dnormed += nn(weight_ref[i * D : (i + 1) * D, :], dqkv_ref[i * D : (i + 1) * D, :])
    slope = inv * inv * inv * jnp.mean(x * dnormed, axis=0, keepdims=True)
    dx = (inv * dnormed - x * slope + both_b[:, FRAME:].astype(F32)).astype(BF)
    dx_rows = dx.T
    out = nn(pick[0], dx_rows[:, :256]) + nn(pick[1], dx_rows[:, 256:])
    out_ref[...] = out.astype(BF)

    me = lax.axis_index("slide")
    even = (me & 1) == 0
    grad_enc = nn(ctx_enc, dx_rows).astype(BF)
    grad_dec = nn(ctx_ref[...], og_rows()[...]).astype(BF)

    def block(s):
        spot = slice(s * 64, (s + 1) * 64)
        return jnp.concatenate([grad_enc[:, spot], grad_dec[:, spot]], axis=1)

    for m in range(4):
        low, high = block(2 * m), block(2 * m + 1)
        j = m ^ (me >> 1)
        keep_ref[j] = jnp.where(even, low, high)
        send_ref[j] = jnp.where(even, high, low)


def add_kernel(keep_ref, recv_ref, *outs):
    for j in range(4):
        outs[j][...] = (keep_ref[j].astype(F32) + recv_ref[j].astype(F32)).astype(BF)


def encode_back_kernel(marks_ref, recv_ref, enc_out_ref, weight_ref, kept_ref, part0, part1, part2, part3, out_ref):
    queries, keys, values = [kept_ref[i * TOKENS : (i + 1) * TOKENS, :] for i in range(1, 4)]
    probs = encoder_probs(queries, keys)
    match2 = group_match(marks_ref, 2)
    lanes = iota((TOKENS, GROUPS * 8), 1)
    recv = recv_ref[...]
    grad = jnp.concatenate(
        [nn(onehot(match2 & (lanes % 2 == half)), recv) for half in range(2)], axis=1
    )
    dctx = per_head(nt(grad.astype(BF), enc_out_ref[...]).astype(BF))
    dprobs = nt(dctx, values).astype(BF).astype(F32)
    inner = jnp.sum(probs * dprobs, axis=1, keepdims=True)
    dscores = (probs * (dprobs - inner) * SCALE).astype(BF)
    dq = fold_heads(nn(dscores, keys))
    dk = tn(dscores, per_head(queries))
    dv = tn(probs.astype(BF), dctx)
    dproj = jnp.concatenate([dq, dk, dv], axis=1).astype(BF)
    dnormed = nt(dproj, weight_ref[...]).astype(BF).astype(F32)
    x = kept_ref[:TOKENS, :].astype(F32)
    inv = lax.rsqrt(jnp.mean(x * x, axis=1, keepdims=True) + EPS)
    slope = inv * inv * inv * jnp.mean(x * dnormed, axis=1, keepdims=True)
    dtokens = (grad + (inv * dnormed - x * slope)).astype(BF)
    match1 = group_match(marks_ref, 0)
    out = jnp.zeros((GROUPS * 8, 128), F32)
    for part in range(4):
        out += tn(onehot(match1 & (lanes % 4 == part)), dtokens[:, part * 128 : (part + 1) * 128])
    out_ref[:, :128] = out.astype(BF)
    parts = [p[...].astype(F32) for p in (part0, part1, part2, part3)]
    out_ref[:, 128:] = (parts[0] + parts[1] + parts[2] + parts[3]).astype(BF)


def finish_kernel(marks_ref, recv_ref, tiles_ref, enc_ref, dec_ref):
    slot = jnp.broadcast_to(marks_ref[7:8, :TILE], (TILE, TILE)).T[:, 0:1]
    lanes = iota((TILE, GROUPS * 8), 1)
    recv = recv_ref[:, :128]
    for part in range(4):
        tiles_ref[:, part * 128 : (part + 1) * 128] = nn(onehot(lanes == slot * 4 + part), recv).astype(BF)
    rows = recv_ref[:, 128:].astype(F32).reshape(GROUPS, 8, 128)
    total = jnp.sum(rows, axis=0)
    enc_ref[...] = total[:, :64]
    dec_ref[...] = total[:, 64:]


VM = pl.BlockSpec(memory_space=pltpu.VMEM)
HERE = pl.BlockSpec(memory_space=pl.ANY)


def call(kernel, outs, args, name, scratch=(), limit=16, flops=10**8, sems=0):
    ins = [a if isinstance(a, tuple) else (a, VM) for a in args]
    held = [pltpu.VMEM(shape, dtype) for shape, dtype in scratch]
    return pl.pallas_call(
        kernel,
        out_shape=[jax.ShapeDtypeStruct(o[0], o[1]) for o in outs],
        in_specs=[place for _, place in ins],
        out_specs=[o[2] if len(o) > 2 else VM for o in outs],
        scratch_shapes=held + ([pltpu.SemaphoreType.DMA((sems,))] if sems else []),
        compiler_params=pltpu.CompilerParams(vmem_limit_bytes=limit * 1024 * 1024),
        cost_estimate=pl.CostEstimate(flops=flops, bytes_accessed=2 * 10**6, transcendentals=0),
        name=name,
    )(*[a for a, _ in ins])


def exchange(rows):
    return lax.all_to_all(rows, "grid", split_axis=0, concat_axis=0, tiled=True)


def swap(block, bit):
    return lax.ppermute(block, "slide", [(i, i ^ bit) for i in range(8)])


def shards(
    embeddings,
    visible,
    window_id,
    output_gradient,
    mask_token,
    enc_qkv,
    enc_out,
    dec_qkv,
    decoder_projected,
):
    emb = embeddings[0]
    og = output_gradient[0]
    ranks = visible.reshape(16, 128)
    (send1,) = call(
        send_tokens_kernel,
        [((GROUPS * 8, 128), BF)],
        ((ranks, HERE), (emb, HERE)),
        "send_tokens",
        scratch=[((16, 128), I32), ((TILE, D), BF)],
        sems=2,
        limit=62,
    )
    recv1 = exchange(send1)
    halo = lax.ppermute(
        jnp.concatenate([emb, og], axis=1), "grid", [(i + 1, i) for i in range(GROUPS - 1)]
    )
    recv1, halo = lax.optimization_barrier((recv1, halo))
    marks, enc = call(
        plan_kernel,
        [((8, GROUPS * 8), I32), ((D, 3 * D), BF)],
        (ranks, window_id.reshape(GROUPS, TILE), enc_qkv),
        "plan",
    )
    send2, kept = call(
        encode_kernel,
        [((GROUPS * 8, 256), BF), ((4 * TOKENS, D), BF)],
        (recv1, marks, enc),
        "encode",
    )
    recv2 = exchange(send2)
    flipped, packed = call(
        prepare_kernel,
        [((4 * D, D), BF), ((PACKED, D), BF, HERE)],
        (marks, emb, og, halo, decoder_projected, enc_out, dec_qkv),
        "prepare",
        scratch=[((OG_ROWS + FRAME, D), BF)],
        sems=3,
        limit=48,
    )
    send3, keep, send = call(
        decode_kernel,
        [((GROUPS * 8, 256), BF), ((4, D, 128), BF), ((4, D, 128), BF)],
        (marks, recv2, mask_token[None, :], flipped, (packed, HERE)),
        "decode",
        scratch=[
            ((D, D), BF),
            ((D, D), BF),
            ((3 * D, D), BF),
            ((FRAME, D), BF),
            ((3 * D, FRAME), BF),
            ((D, FRAME), BF),
        ],
        sems=4,
        limit=48,
        flops=2 * 10**9,
    )
    recv3 = exchange(send3)
    sums = call(add_kernel, [((D, 128), BF)] * 4, (keep, swap(send, 1)), "add_core")
    parts = [sums[0]] + [swap(sums[j], 2 * j) for j in range(1, 4)]
    (send4,) = call(
        encode_back_kernel,
        [((GROUPS * 8, 256), BF)],
        (marks, recv3, enc_out, enc_qkv, kept, *parts),
        "encode_back",
    )
    recv4 = exchange(send4)
    tiles, grad_enc, grad_dec = call(
        finish_kernel,
        [((TILE, D), BF), ((8, 64), F32), ((8, 64), F32)],
        (marks, recv4),
        "finish",
    )
    return tiles[None], grad_enc, grad_dec


def solution(mesh):
    placed = (
        P("slide", "grid", None),
        P("slide", None),
        P("slide", None),
        P("slide", "grid", None),
        P(),
        P(),
        P(),
        P(),
        P(),
    )
    return jax.shard_map(
        shards,
        mesh=mesh,
        in_specs=placed,
        out_specs=(P("slide", "grid", None), P("grid", "slide"), P("grid", "slide")),
        check_vma=False,
    )
```

time: 165 us -> 148 us (0.90)
  the two profiles are of different devices: /device:TPU:8 before, /device:TPU:4 now
where the time goes in v2:
time: 148 us
  starting transfers between devices  48.1 us (32%)
  waiting for transfers between devices  35.9 us (24%)
  blocking collectives  34.5 us (23%)
  Pallas kernels  19.7 us (13%)
  local copies, waits for them, and re-layouts  7.51 us (5%)
    all_to_all x3, starting transfers between devices, exchange(): return lax.all_to_all(rows, 'grid', split_axis=0, concat_axis=0, tiled=True)  35.7 us
    all_to_all x1, blocking collectives, exchange(): return lax.all_to_all(rows, 'grid', split_axis=0, concat_axis=0, tiled=True)  34.5 us
    all_to_all x3, waiting for transfers between devices, exchange(): return lax.all_to_all(rows, 'grid', split_axis=0, concat_axis=0, tiled=True)  21.1 us
    pallas_call x8, Pallas kernels, call(): pl.pallas_call(kernel, out_shape=[jax.ShapeDtypeStruct(o[0], o[1]) for o...  19.7 us
    ppermute x4, starting transfers between devices, swap(): return lax.ppermute(block, 'slide', [(i, i ^ bit) for i in range(8)])  11.1 us
    unnamed x24, local copies, waits for them, and re-layouts  7.51 us
    ppermute x4, waiting for transfers between devices, swap(): return lax.ppermute(block, 'slide', [(i, i ^ bit) for i in range(8)])  7.41 us
    ppermute x1, waiting for transfers between devices, shards(): lax.ppermute(jnp.concatenate([emb, og], axis=1), 'grid', [(i + 1, i) for...  7.38 us
  transfers between devices with their start and end apart: 8, of which 7 were waited for; matrix products, arithmetic and copies ran while one was open for 1% of the time, Pallas kernels for 2%

profile of v2, /device:TPU:4, one launch (start us, length us, event | category | flops | bytes accessed | tf_op | source)
XLA Modules:
  0.0 147.6 jit_solution(818375696811759316)
XLA Ops:
  0.6 1.9 %send_tokens.1 = bf16[512,128]{1,0:T(8,128)(2,1)} custom-call(s32[16,128]{1,0:T(8,128)} %bitcast.26, bf16[128,512]{1,0:T(8,128)(2,1)} %bitcast.17), custom_call_target="tpu_custom_call" | custom-call | flops 100000000 | bytes 2000000 | tf_op jit(solution)/shard_map/send_tokens/pallas_call | solution.py:344
  2.5 18.7 %all-to-all-start = ((bf16[64,8,128]{2,1,0:T(8,128)(2,1)}), bf16[64,8,128]{2,1,0:T(8,128)(2,1)S(1)}, u32[]{:S(2)}, u32[]{:S(2)}) async-start(bf16[64,8,128]{2,1,0:T(8,128)(2,1)} %bitcast.29), calls=%async_computation | async-start | bytes 262144 | tf_op jit(solution)/shard_map/all_to_all | solution.py:357
  21.3 1.0 pad_maximum_fusion
  22.3 1.3 collective-permute-start
  23.6 0.0 copy-start
  23.6 1.4 copy-done
  25.0 0.0 copy-start.8
  25.0 0.8 copy-done.8
  25.7 0.0 copy-start.9
  25.7 0.7 copy-done.9
  26.4 0.0 copy-start.2
  26.4 0.0 copy-start.4
  26.4 0.0 copy-start.5
  26.4 0.5 plan.1
  27.0 7.4 %collective-permute-done.halo_ref = bf16[128,1024]{1,0:T(8,128)(2,1)S(1)} collective-permute-done((bf16[128,1024]{1,0:T(8,128)(2,1)S(1)}, bf16[128,1024]{1,0:T(8,128)(2,1)S(1)}, u32[]{:S(2)}, u32[]{:S(2)}) %collective-permute-start) | collective-permute-done | bytes 262176 | tf_op jit(solution)/shard_map/ppermute | solution.py:388
  34.3 3.3 %all-to-all-done = bf16[64,8,128]{2,1,0:T(8,128)(2,1)S(1)} async-done(((bf16[64,8,128]{2,1,0:T(8,128)(2,1)}), bf16[64,8,128]{2,1,0:T(8,128)(2,1)S(1)}, u32[]{:S(2)}, u32[]{:S(2)}) %all-to-all-start) | async-done | bytes 131104 | tf_op jit(solution)/shard_map/all_to_all | solution.py:357
  37.6 2.2 %encode.1 = (bf16[512,256]{1,0:T(8,128)(2,1)}, bf16[128,512]{1,0:T(8,128)(2,1)S(1)}) custom-call(bf16[512,128]{1,0:T(8,128)(2,1)S(1)} %bitcast.22, s32[8,512]{1,0:T(8,128)S(1)} %get-tuple-element.21.marks_ref, bf16[512,1536]{1,0:T(8,128)(2,1)S(1)} %get-tuple-element.23.weight_ref), custom_call_target="tpu_custom_call" | custom-call | flops 100000000 | bytes 2000000 | tf_op jit(solution)/shard_map/encode/pallas_call | solution.py:344
  39.8 10.6 %all-to-all-start.1 = ((bf16[64,8,256]{2,1,0:T(8,128)(2,1)}), bf16[64,8,256]{2,1,0:T(8,128)(2,1)S(1)}, u32[]{:S(2)}, u32[]{:S(2)}) async-start(bf16[64,8,256]{2,1,0:T(8,128)(2,1)} %bitcast.6), calls=%async_computation.1 | async-start | bytes 524288 | tf_op jit(solution)/shard_map/all_to_all | solution.py:357
  50.3 0.0 copy-done.2
  50.4 0.0 copy-done.4
  50.4 0.0 copy-done.5
  50.4 0.0 copy-start.3
  50.4 1.4 copy-done.3
  51.8 0.0 copy-start.6
  51.8 1.0 copy-done.6
  52.8 2.2 %prepare.1 = (bf16[2048,512]{1,0:T(8,128)(2,1)S(1)}, bf16[18432,512]{1,0:T(8,128)(2,1)}) custom-call(s32[8,512]{1,0:T(8,128)S(1)} %get-tuple-element.21.marks_ref, bf16[128,512]{1,0:T(8,128)(2,1)S(1)} %bitcast.19, bf16[128,512]{1,0:T(8,128)(2,1)S(1)} %bitcast.21, bf16[128,1024]{1,0:T(8,128)(2,1)S(1)} %collective-permute-done.halo_ref, ...), custom_call_target="tpu_custom_call" | custom-call | flops 100000000 | bytes 2000000 | tf_op jit(solution)/shard_map/prepare/pallas_call | solution.py:344
  55.0 16.3 %all-to-all-done.1 = bf16[64,8,256]{2,1,0:T(8,128)(2,1)S(1)} async-done(((bf16[64,8,256]{2,1,0:T(8,128)(2,1)}), bf16[64,8,256]{2,1,0:T(8,128)(2,1)S(1)}, u32[]{:S(2)}, u32[]{:S(2)}) %all-to-all-start.1) | async-done | bytes 262176 | tf_op jit(solution)/shard_map/all_to_all | solution.py:357
  71.3 0.0 copy-start.10
  71.3 0.7 copy-done.10
  72.0 9.9 %decode.1 = (bf16[512,256]{1,0:T(8,128)(2,1)S(1)}, bf16[4,512,128]{2,1,0:T(8,128)(2,1)S(1)}, bf16[4,512,128]{2,1,0:T(8,128)(2,1)S(1)}) custom-call(s32[8,512]{1,0:T(8,128)S(1)} %get-tuple-element.21.marks_ref, bf16[512,256]{1,0:T(8,128)(2,1)S(1)} %bitcast.14, f32[1,512]{1,0:T(1,128)S(1)} %bitcast.28, bf16[2048,512]{1,0:T(8,128)(2,1)S(1)} %get-tuple-element.26.flipped_ref, ...), custom_call_target="tpu_custom_call" | custom-call | flops 2000000000 | bytes 2000000 | tf_op jit(solution)/shard_map/decode/pallas_call | solution.py:344
  81.9 0.0 copy-start.11
  81.9 0.8 copy-done.11
  82.7 0.7 copy-done.7
  83.4 6.4 %all-to-all-start.2 = ((bf16[64,8,256]{2,1,0:T(8,128)(2,1)}), bf16[64,8,256]{2,1,0:T(8,128)(2,1)S(1)}, u32[]{:S(2)}, u32[]{:S(2)}) async-start(bf16[64,8,256]{2,1,0:T(8,128)(2,1)} %bitcast.23), calls=%async_computation.2 | async-start | bytes 524288 | tf_op jit(solution)/shard_map/all_to_all | solution.py:357
  89.8 1.9 %collective-permute-start.1 = (bf16[4,512,128]{2,1,0:T(8,128)(2,1)}, bf16[4,512,128]{2,1,0:T(8,128)(2,1)S(1)}, u32[]{:S(2)}, u32[]{:S(2)}) collective-permute-start(bf16[4,512,128]{2,1,0:T(8,128)(2,1)} %copy-done.11), channel_id=1, source_target_pairs={{0,64},{64,0},{128,192},{192,128},{256,320},{320,256},{384,448},{4... | collective-permute-start | bytes 1572872 | tf_op jit(solution)/shard_map/ppermute | solution.py:361
  91.8 2.1 %collective-permute-done.1.recv_ref = bf16[4,512,128]{2,1,0:T(8,128)(2,1)S(1)} collective-permute-done((bf16[4,512,128]{2,1,0:T(8,128)(2,1)}, bf16[4,512,128]{2,1,0:T(8,128)(2,1)S(1)}, u32[]{:S(2)}, u32[]{:S(2)}) %collective-permute-start.1) | collective-permute-done | bytes 524320 | tf_op jit(solution)/shard_map/ppermute | solution.py:361
  93.9 0.1 add_core.1
  94.0 3.1 %collective-permute-start.2 = (bf16[512,128]{1,0:T(8,128)(2,1)S(1)}, bf16[512,128]{1,0:T(8,128)(2,1)S(1)}, u32[]{:S(2)}, u32[]{:S(2)}) collective-permute-start(bf16[512,128]{1,0:T(8,128)(2,1)S(1)} %get-tuple-element.33), channel_id=1, source_target_pairs={{0,128},{64,192},{128,0},{192,64},{256,384},{320,448},{384,256},{4... | collective-permute-start | bytes 393224 | tf_op jit(solution)/shard_map/ppermute | solution.py:361
  97.1 2.7 %collective-permute-start.3 = (bf16[512,128]{1,0:T(8,128)(2,1)S(1)}, bf16[512,128]{1,0:T(8,128)(2,1)S(1)}, u32[]{:S(2)}, u32[]{:S(2)}) collective-permute-start(bf16[512,128]{1,0:T(8,128)(2,1)S(1)} %get-tuple-element.34), channel_id=1, source_target_pairs={{0,256},{64,320},{128,384},{192,448},{256,0},{320,64},{384,128},{4... | collective-permute-start | bytes 393224 | tf_op jit(solution)/shard_map/ppermute | solution.py:361
  99.8 3.4 %collective-permute-start.4 = (bf16[512,128]{1,0:T(8,128)(2,1)S(1)}, bf16[512,128]{1,0:T(8,128)(2,1)S(1)}, u32[]{:S(2)}, u32[]{:S(2)}) collective-permute-start(bf16[512,128]{1,0:T(8,128)(2,1)S(1)} %get-tuple-element.35), channel_id=1, source_target_pairs={{0,384},{64,448},{128,256},{192,320},{256,128},{320,192},{384,0},{... | collective-permute-start | bytes 393224 | tf_op jit(solution)/shard_map/ppermute | solution.py:361
  103.2 0.0 collective-permute-done.2.part1
  103.2 2.6 %collective-permute-done.3.part2 = bf16[512,128]{1,0:T(8,128)(2,1)S(1)} collective-permute-done((bf16[512,128]{1,0:T(8,128)(2,1)S(1)}, bf16[512,128]{1,0:T(8,128)(2,1)S(1)}, u32[]{:S(2)}, u32[]{:S(2)}) %collective-permute-start.3) | collective-permute-done | bytes 131104 | tf_op jit(solution)/shard_map/ppermute | solution.py:361
  105.8 2.7 %collective-permute-done.4.part3 = bf16[512,128]{1,0:T(8,128)(2,1)S(1)} collective-permute-done((bf16[512,128]{1,0:T(8,128)(2,1)S(1)}, bf16[512,128]{1,0:T(8,128)(2,1)S(1)}, u32[]{:S(2)}, u32[]{:S(2)}) %collective-permute-start.4) | collective-permute-done | bytes 131104 | tf_op jit(solution)/shard_map/ppermute | solution.py:361
  108.5 1.5 %all-to-all-done.2 = bf16[64,8,256]{2,1,0:T(8,128)(2,1)S(1)} async-done(((bf16[64,8,256]{2,1,0:T(8,128)(2,1)}), bf16[64,8,256]{2,1,0:T(8,128)(2,1)S(1)}, u32[]{:S(2)}, u32[]{:S(2)}) %all-to-all-start.2) | async-done | bytes 262176 | tf_op jit(solution)/shard_map/all_to_all | solution.py:357
  110.1 0.0 copy-done.1
  110.1 2.0 %encode_back.1 = bf16[512,256]{1,0:T(8,128)(2,1)S(1)} custom-call(s32[8,512]{1,0:T(8,128)S(1)} %get-tuple-element.21.marks_ref, bf16[512,256]{1,0:T(8,128)(2,1)S(1)} %bitcast.15, bf16[512,512]{1,0:T(8,128)(2,1)S(1)} %copy-done.2, bf16[512,1536]{1,0:T(8,128)(2,1)S(1)} %copy-done.1, bf16[128,512]{1,0:T(8,128)(2,1)S(1)} %get-tuple-element.29.kept_ref, ...), custom_call_target="tpu_custom_call" | custom-call | flops 100000000 | bytes 2000000 | tf_op jit(solution)/shard_map/encode_back/pallas_call | solution.py:344
  112.0 34.5 %all_to_all.45 = bf16[64,8,256]{2,1,0:T(8,128)(2,1)S(1)} all-to-all(bf16[64,8,256]{2,1,0:T(8,128)(2,1)S(1)} %bitcast.16), channel_id=1, replica_groups=mesh['slide'=8,'grid'=64] {'grid'}, dimensions={0} | all-to-all | bytes 524288 | tf_op jit(solution)/shard_map/all_to_all | solution.py:357
  146.6 1.1 finish.1
  (2 shorter events, 0.0 us)
Async XLA Ops:
  2.5 35.1 %all-to-all-start = ((bf16[64,8,128]{2,1,0:T(8,128)(2,1)}), bf16[64,8,128]{2,1,0:T(8,128)(2,1)S(1)}, u32[]{:S(2)}, u32[]{:S(2)}) async-start(bf16[64,8,128]{2,1,0:T(8,128)(2,1)} %bitcast.29), calls=%async_computation | async-start | bytes 262144 | tf_op jit(solution)/shard_map/all_to_all | solution.py:357
  22.3 12.1 %collective-permute-start = (bf16[128,1024]{1,0:T(8,128)(2,1)S(1)}, bf16[128,1024]{1,0:T(8,128)(2,1)S(1)}, u32[]{:S(2)}, u32[]{:S(2)}) collective-permute-start(bf16[128,1024]{1,0:T(8,128)(2,1)S(1)} %pad_maximum_fusion), channel_id=1, source_target_pairs={{1,0},{2,1},{3,2},{4,3},{5,4},{6,5},{7,6},{8,7},{9,8},{10,9},{11,1... | collective-permute-start | bytes 786440 | tf_op jit(solution)/shard_map/ppermute | solution.py:388
  23.6 1.4 copy-start
  25.0 0.8 copy-start.8
  25.7 0.7 copy-start.9
  26.4 23.9 %copy-start.2 = (bf16[512,512]{1,0:T(8,128)(2,1)S(1)}, bf16[512,512]{1,0:T(8,128)(2,1)}, u32[]{:S(2)}) copy-start(bf16[512,512]{1,0:T(8,128)(2,1)} %enc_out_ref.3) | copy-start | bytes 1572868
  26.4 23.9 %copy-start.4 = (bf16[1,128,512]{2,1,0:T(8,128)(2,1)S(1)}, bf16[1,128,512]{2,1,0:T(8,128)(2,1)}, u32[]{:S(2)}) copy-start(bf16[1,128,512]{2,1,0:T(8,128)(2,1)} %param.9) | copy-start | bytes 393220
  26.4 23.9 %copy-start.5 = (bf16[1,128,512]{2,1,0:T(8,128)(2,1)S(1)}, bf16[1,128,512]{2,1,0:T(8,128)(2,1)}, u32[]{:S(2)}) copy-start(bf16[1,128,512]{2,1,0:T(8,128)(2,1)} %param.12) | copy-start | bytes 393220
  39.8 31.5 %all-to-all-start.1 = ((bf16[64,8,256]{2,1,0:T(8,128)(2,1)}), bf16[64,8,256]{2,1,0:T(8,128)(2,1)S(1)}, u32[]{:S(2)}, u32[]{:S(2)}) async-start(bf16[64,8,256]{2,1,0:T(8,128)(2,1)} %bitcast.6), calls=%async_computation.1 | async-start | bytes 524288 | tf_op jit(solution)/shard_map/all_to_all | solution.py:357
  50.4 1.4 copy-start.3
  51.8 1.0 copy-start.6
  71.3 0.7 copy-start.10
  81.9 0.8 copy-start.11
  82.7 0.7 copy-start.7
  82.7 27.4 %copy-start.1 = (bf16[512,1536]{1,0:T(8,128)(2,1)S(1)}, bf16[512,1536]{1,0:T(8,128)(2,1)}, u32[]{:S(2)}) copy-start(bf16[512,1536]{1,0:T(8,128)(2,1)} %weight_ref.1) | copy-start | bytes 4718596
  83.4 26.7 %all-to-all-start.2 = ((bf16[64,8,256]{2,1,0:T(8,128)(2,1)}), bf16[64,8,256]{2,1,0:T(8,128)(2,1)S(1)}, u32[]{:S(2)}, u32[]{:S(2)}) async-start(bf16[64,8,256]{2,1,0:T(8,128)(2,1)} %bitcast.23), calls=%async_computation.2 | async-start | bytes 524288 | tf_op jit(solution)/shard_map/all_to_all | solution.py:357
  89.8 4.0 %collective-permute-start.1 = (bf16[4,512,128]{2,1,0:T(8,128)(2,1)}, bf16[4,512,128]{2,1,0:T(8,128)(2,1)S(1)}, u32[]{:S(2)}, u32[]{:S(2)}) collective-permute-start(bf16[4,512,128]{2,1,0:T(8,128)(2,1)} %copy-done.11), channel_id=1, source_target_pairs={{0,64},{64,0},{128,192},{192,128},{256,320},{320,256},{384,448},{4... | collective-permute-start | bytes 1572872 | tf_op jit(solution)/shard_map/ppermute | solution.py:361
  94.0 9.2 %collective-permute-start.2 = (bf16[512,128]{1,0:T(8,128)(2,1)S(1)}, bf16[512,128]{1,0:T(8,128)(2,1)S(1)}, u32[]{:S(2)}, u32[]{:S(2)}) collective-permute-start(bf16[512,128]{1,0:T(8,128)(2,1)S(1)} %get-tuple-element.33), channel_id=1, source_target_pairs={{0,128},{64,192},{128,0},{192,64},{256,384},{320,448},{384,256},{4... | collective-permute-start | bytes 393224 | tf_op jit(solution)/shard_map/ppermute | solution.py:361
  97.1 8.8 %collective-permute-start.3 = (bf16[512,128]{1,0:T(8,128)(2,1)S(1)}, bf16[512,128]{1,0:T(8,128)(2,1)S(1)}, u32[]{:S(2)}, u32[]{:S(2)}) collective-permute-start(bf16[512,128]{1,0:T(8,128)(2,1)S(1)} %get-tuple-element.34), channel_id=1, source_target_pairs={{0,256},{64,320},{128,384},{192,448},{256,0},{320,64},{384,128},{4... | collective-permute-start | bytes 393224 | tf_op jit(solution)/shard_map/ppermute | solution.py:361
  99.8 8.7 %collective-permute-start.4 = (bf16[512,128]{1,0:T(8,128)(2,1)S(1)}, bf16[512,128]{1,0:T(8,128)(2,1)S(1)}, u32[]{:S(2)}, u32[]{:S(2)}) collective-permute-start(bf16[512,128]{1,0:T(8,128)(2,1)S(1)} %get-tuple-element.35), channel_id=1, source_target_pairs={{0,384},{64,448},{128,256},{192,320},{256,128},{320,192},{384,0},{... | collective-permute-start | bytes 393224 | tf_op jit(solution)/shard_map/ppermute | solution.py:361

commit v3 on v2

--- a/solution.py
+++ b/solution.py
@@ -81,20 +81,27 @@
     return jnp.where(present, (rank & (GROUPS - 1)) * 2 + ((rank - base) >> 6), -1)
 
 
-def send_tokens_kernel(visible_hbm, emb_hbm, out_ref, visible_b, emb_b, sems):
+def send_tokens_kernel(visible_hbm, emb_hbm, og_hbm, out_ref, pair_hbm, visible_b, emb_b, og_b, sems):
     visible = Load(visible_hbm, visible_b, sems, 0)
     emb = Load(emb_hbm, emb_b, sems, 1)
+    og = Load(og_hbm, og_b, sems, 2)
     slot = own_slots(visible(), lax.axis_index("grid") * TILE)
     rows = iota((GROUPS * 8, TILE), 0)
     picks = [onehot(rows == slot * 4 + part) for part in range(4)]
     emb_ref = emb()
+    ship_emb = pltpu.make_async_copy(emb_ref, pair_hbm.at[:, :D], sems.at[3])
+    ship_emb.start()
+    ship_og = pltpu.make_async_copy(og(), pair_hbm.at[:, D:], sems.at[4])
+    ship_og.start()
     total = jnp.zeros((GROUPS * 8, TILE), F32)
     for part in range(4):
         total += nn(picks[part], emb_ref[:, part * 128 : (part + 1) * 128])
     out_ref[...] = total.astype(BF)
-
-
-def plan_kernel(visible_ref, wid_ref, enc_qkv_ref, marks_ref, enc_ref):
+    ship_emb.wait()
+    ship_og.wait()
+
+
+def plan_kernel(visible_ref, wid_ref, enc_qkv_ref, mask_ref, halo_ref, marks_ref, enc_ref):
     enc_ref[...] = enc_qkv_ref[...]
     d = lax.axis_index("grid")
     first = d * TILE
@@ -103,8 +110,8 @@
     start1 = RUN * run_counts(visible_ref, peer * TILE)
     stop1 = RUN * run_counts(visible_ref, peer * TILE + TILE)
     low1 = start1 + GROUPS * ((lane >> 2) & 1)
-    marks_ref[0:1, :] = low1
-    marks_ref[1:2, :] = jnp.minimum(low1 + GROUPS, stop1)
+    marks_ref[0:1, :] = low1.astype(F32)
+    marks_ref[1:2, :] = jnp.minimum(low1 + GROUPS, stop1).astype(F32)
 
     wid = wid_ref[...]
     last = wid[:, TILE - 1 :]
@@ -125,9 +132,10 @@
 
     start2, stop2 = visible_below(begin), visible_below(end)
     low2 = start2 + GROUPS * ((lane >> 1) & 3)
-    marks_ref[2:3, :] = low2
-    marks_ref[3:4, :] = jnp.minimum(low2 + GROUPS, stop2)
-    marks_ref[4:8, :] = jnp.zeros((4, GROUPS * 8), I32)
+    marks_ref[2:3, :] = low2.astype(F32)
+    marks_ref[3:4, :] = jnp.minimum(low2 + GROUPS, stop2).astype(F32)
+    marks_ref[4:8, :] = jnp.zeros((4, GROUPS * 8), F32)
+    marks_ref[8:16, :] = jnp.broadcast_to(mask_ref[...], (8, D))
 
     def mine(values):
         return jnp.sum(jnp.where(lane == d * 8, values.astype(F32), 0.0), axis=1, keepdims=True).astype(I32)
@@ -137,26 +145,29 @@
     spot = iota((1, FRAME), 1)
     live = present & (rank >= start2) & (rank < stop2)
     owned = (first + spot >= begin) & (first + spot < end)
-    marks_ref[4:5, :FRAME] = jnp.where(live, (rank & (GROUPS - 1)) * 4 + ((rank - start2) >> 6), -1)
-    marks_ref[5:6, :FRAME] = jnp.where(owned, 1, 0)
+    marks_ref[4:5, :FRAME] = jnp.where(live, (rank & (GROUPS - 1)) * 4 + ((rank - start2) >> 6), -1).astype(F32)
+    marks_ref[5:6, :FRAME] = jnp.where(owned, 1.0, 0.0)
     own = wid_ref[pl.ds(d, 1), :]
     after = wid_ref[pl.ds(jnp.minimum(d + 1, GROUPS - 1), 1), :]
-    marks_ref[6:7, :FRAME] = jnp.where(owned, jnp.concatenate([own, after], axis=1), -1 - spot)
-    marks_ref[7:8, :TILE] = own_slots(visible_ref, first)
-
-
-OUT_T, BOTH, MORE, QKV, OG_ROWS, PACKED = 1536, 0, 512, 1024, 2560, 18432
-
-
-def prepare_kernel(marks_ref, emb_ref, og_ref, halo_ref, proj_ref, enc_out_ref, qkv_ref, flipped_ref, packed_ref, held, sems):
-    def ship(first, last, sem):
-        copy = pltpu.make_async_copy(held.at[first:last], packed_ref.at[first:last], sems.at[sem])
-        copy.start()
-        return copy
-
-    for i in range(3):
-        held[QKV + i * D : QKV + (i + 1) * D, :] = qkv_ref[:, i * D : (i + 1) * D]
-    copies = [ship(QKV, OG_ROWS, 0)]
+    marks_ref[6:7, :FRAME] = jnp.where(owned, jnp.concatenate([own, after], axis=1), -1 - spot).astype(F32)
+    marks_ref[7:8, :TILE] = own_slots(visible_ref, first).astype(F32)
+
+
+OUT_T, BOTH, MORE, OG_ROWS, OWN, QKV, ENC_OUT, ENC_QKV, PACKED = 1536, 0, 512, 1024, 1280, 1280, 2816, 3328, 18432
+
+
+def blocks(weight_ref, out_ref, first, sems, sem):
+    copies = []
+    for i in range(weight_ref.shape[1] // D):
+        rows = out_ref.at[first + i * D : first + (i + 1) * D]
+        copies.append(pltpu.make_async_copy(weight_ref.at[:, i * D : (i + 1) * D], rows, sems.at[sem + i]))
+        copies[-1].start()
+    return copies
+
+
+def prepare_kernel(marks_ref, emb_ref, og_ref, halo_ref, proj_ref, enc_out_ref, qkv_ref, enc_qkv_ref, flipped_ref, packed_ref, held, sems):
+    copies = blocks(qkv_ref, packed_ref, QKV, sems, 0)
+    copies += blocks(enc_out_ref, packed_ref, ENC_OUT, sems, 4) + blocks(enc_qkv_ref, packed_ref, ENC_QKV, sems, 5)
     flipped_ref[:OUT_T, :] = qkv_ref[...].T
     flipped_ref[OUT_T:, :] = enc_out_ref[...].T
     owned = marks_ref[5:6, :FRAME] > 0
@@ -170,8 +181,8 @@
     across = jnp.broadcast_to(marks_ref[6:7, :FRAME], (FRAME, FRAME))
     held[MORE : MORE + FRAME, FRAME:] = jnp.where(across == across.T, 0.0, NEG).astype(BF)
     held[MORE + FRAME : MORE + D, FRAME:] = jnp.zeros((FRAME, FRAME), BF)
-    copies.append(ship(OG_ROWS, OG_ROWS + FRAME, 1))
-    copies.append(ship(BOTH, QKV, 2))
+    copies.append(pltpu.make_async_copy(held, packed_ref.at[:OWN], sems.at[3]))
+    copies[-1].start()
     for copy in copies:
         copy.wait()
 
@@ -193,9 +204,10 @@
     return total
 
 
-def group_match(bounds_ref, row):
+def group_match(marks_ref, row):
     ranks = iota((TOKENS, GROUPS * 8), 0) * GROUPS + lax.axis_index("grid")
-    return (ranks >= bounds_ref[row : row + 1, :]) & (ranks < bounds_ref[row + 1 : row + 2, :])
+    low, high = marks_ref[row : row + 1, :].astype(I32), marks_ref[row + 1 : row + 2, :].astype(I32)
+    return (ranks >= low) & (ranks < high)
 
 
 def encoder_probs(queries, keys):
@@ -204,7 +216,7 @@
     return weights / jnp.sum(weights, axis=1, keepdims=True)
 
 
-def encode_kernel(recv_ref, marks_ref, weight_ref, out_ref, kept_ref):
+def encode_kernel(recv_ref, marks_ref, weight_ref, out_ref, store, kept_ref, sems):
     match1 = group_match(marks_ref, 0)
     lanes = iota((TOKENS, GROUPS * 8), 1)
     recv = recv_ref[...]
@@ -214,23 +226,26 @@
     qkv = nn(normed, weight_ref[...]).astype(BF)
     for i in range(3):
         kept_ref[(i + 1) * TOKENS : (i + 2) * TOKENS, :] = qkv[:, i * D : (i + 1) * D]
+    keep = pltpu.make_async_copy(kept_ref, store.at[: 4 * TOKENS], sems.at[0])
+    keep.start()
     soft = encoder_probs(qkv[:, :D], qkv[:, D : 2 * D])
     context = fold_heads(nn(soft.astype(BF), qkv[:, 2 * D :])).astype(BF)
     match2 = group_match(marks_ref, 2)
     out = tn(onehot(match2 & (lanes % 2 == 0)), context[:, :256])
     out += tn(onehot(match2 & (lanes % 2 == 1)), context[:, 256:])
     out_ref[...] = out.astype(BF)
-
-
-def decode_kernel(marks_ref, recv_ref, mask_ref, flipped_ref, packed, out_ref, keep_ref, send_ref, more_b, both_b, qkv_b, og_b, dqkv_ref, ctx_ref, sems):
-    more = Load(packed.at[MORE:QKV], more_b, sems, 0)
+    keep.wait()
+
+
+def decode_kernel(marks_ref, recv_ref, flipped_ref, packed, out_hbm, keep_ref, send_ref, out_ref, more_b, both_b, qkv_b, og_b, dqkv_ref, ctx_ref, sems):
+    more = Load(packed.at[MORE:OG_ROWS], more_b, sems, 0)
     both = Load(packed.at[BOTH:MORE], both_b, sems, 1)
-    qkv_w = Load(packed.at[QKV:OG_ROWS], qkv_b, sems, 2)
-    og_rows = Load(packed.at[OG_ROWS : OG_ROWS + FRAME], og_b, sems, 3)
-    slot = marks_ref[4:5, :FRAME]
+    qkv_w = Load(packed.at[QKV : QKV + 3 * D], qkv_b, sems, 2)
+    og_rows = Load(packed.at[OG_ROWS:OWN], og_b, sems, 3)
+    slot = marks_ref[4:5, :FRAME].astype(I32)
     live = slot >= 0
     owned = marks_ref[5:6, :FRAME] > 0
-    blank = jnp.broadcast_to(mask_ref[...], (TILE, D)).T[:, :1]
+    blank = jnp.broadcast_to(marks_ref[8:9, :], (TILE, D)).T[:, :1]
     rows = iota((GROUPS * 8, FRAME), 0)
     pick = [onehot(rows == slot * 2 + half) for half in range(2)]
     recv = recv_ref[...]
@@ -269,6 +284,8 @@
     dx_rows = dx.T
     out = nn(pick[0], dx_rows[:, :256]) + nn(pick[1], dx_rows[:, 256:])
     out_ref[...] = out.astype(BF)
+    ship = pltpu.make_async_copy(out_ref, out_hbm, sems.at[4])
+    ship.start()
 
     me = lax.axis_index("slide")
     even = (me & 1) == 0
@@ -284,6 +301,7 @@
         j = m ^ (me >> 1)
         keep_ref[j] = jnp.where(even, low, high)
         send_ref[j] = jnp.where(even, high, low)
+    ship.wait()
 
 
 def add_kernel(keep_ref, recv_ref, *outs):
@@ -291,24 +309,31 @@
         outs[j][...] = (keep_ref[j].astype(F32) + recv_ref[j].astype(F32)).astype(BF)
 
 
-def encode_back_kernel(marks_ref, recv_ref, enc_out_ref, weight_ref, kept_ref, part0, part1, part2, part3, out_ref):
-    queries, keys, values = [kept_ref[i * TOKENS : (i + 1) * TOKENS, :] for i in range(1, 4)]
-    probs = encoder_probs(queries, keys)
+def encode_back_kernel(marks_ref, recv_ref, packed, store, out_ref, enc_out_b, kept_b, weight_b, sems):
+    enc_out = Load(packed.at[ENC_OUT:ENC_QKV], enc_out_b, sems, 0, 2)
+    kept = Load(store.at[: 4 * TOKENS], kept_b, sems, 2)
+    weight = Load(packed.at[ENC_QKV : ENC_QKV + 3 * D], weight_b, sems, 3, 3)
     match2 = group_match(marks_ref, 2)
     lanes = iota((TOKENS, GROUPS * 8), 1)
     recv = recv_ref[...]
     grad = jnp.concatenate(
         [nn(onehot(match2 & (lanes % 2 == half)), recv) for half in range(2)], axis=1
     )
-    dctx = per_head(nt(grad.astype(BF), enc_out_ref[...]).astype(BF))
+    dctx = per_head(nt(grad.astype(BF), enc_out()[...]).astype(BF))
+    kept_ref = kept()
+    queries, keys, values = [kept_ref[i * TOKENS : (i + 1) * TOKENS, :] for i in range(1, 4)]
+    probs = encoder_probs(queries, keys)
     dprobs = nt(dctx, values).astype(BF).astype(F32)
     inner = jnp.sum(probs * dprobs, axis=1, keepdims=True)
     dscores = (probs * (dprobs - inner) * SCALE).astype(BF)
     dq = fold_heads(nn(dscores, keys))
     dk = tn(dscores, per_head(queries))
     dv = tn(probs.astype(BF), dctx)
-    dproj = jnp.concatenate([dq, dk, dv], axis=1).astype(BF)
-    dnormed = nt(dproj, weight_ref[...]).astype(BF).astype(F32)
+    weight_ref = weight()
+    dnormed = nt(dq.astype(BF), weight_ref[:D, :])
+    dnormed += nt(dk.astype(BF), weight_ref[D : 2 * D, :])
+    dnormed += nt(dv.astype(BF), weight_ref[2 * D :, :])
+    dnormed = dnormed.astype(BF).astype(F32)
     x = kept_ref[:TOKENS, :].astype(F32)
     inv = lax.rsqrt(jnp.mean(x * x, axis=1, keepdims=True) + EPS)
     slope = inv * inv * inv * jnp.mean(x * dnormed, axis=1, keepdims=True)
@@ -317,13 +342,17 @@
     out = jnp.zeros((GROUPS * 8, 128), F32)
     for part in range(4):
         out += tn(onehot(match1 & (lanes % 4 == part)), dtokens[:, part * 128 : (part + 1) * 128])
-    out_ref[:, :128] = out.astype(BF)
+    out_ref[...] = out.astype(BF)
+
+
+def join_kernel(tokens_ref, part0, part1, part2, part3, out_ref):
+    out_ref[:, :128] = tokens_ref[...]
     parts = [p[...].astype(F32) for p in (part0, part1, part2, part3)]
     out_ref[:, 128:] = (parts[0] + parts[1] + parts[2] + parts[3]).astype(BF)
 
 
 def finish_kernel(marks_ref, recv_ref, tiles_ref, enc_ref, dec_ref):
-    slot = jnp.broadcast_to(marks_ref[7:8, :TILE], (TILE, TILE)).T[:, 0:1]
+    slot = jnp.broadcast_to(marks_ref[7:8, :TILE], (TILE, TILE)).T[:, 0:1].astype(I32)
     lanes = iota((TILE, GROUPS * 8), 1)
     recv = recv_ref[:, :128]
     for part in range(4):
@@ -375,48 +404,50 @@
     emb = embeddings[0]
     og = output_gradient[0]
     ranks = visible.reshape(16, 128)
-    (send1,) = call(
+    send1, pair = call(
         send_tokens_kernel,
-        [((GROUPS * 8, 128), BF)],
-        ((ranks, HERE), (emb, HERE)),
+        [((GROUPS * 8, 128), BF), ((TILE, 2 * D), BF, HERE)],
+        ((ranks, HERE), (emb, HERE), (og, HERE)),
         "send_tokens",
-        scratch=[((16, 128), I32), ((TILE, D), BF)],
-        sems=2,
+        scratch=[((16, 128), I32), ((TILE, D), BF), ((TILE, D), BF)],
+        sems=5,
         limit=62,
     )
+    halo = lax.ppermute(pair, "grid", [(i + 1, i) for i in range(GROUPS - 1)])
     recv1 = exchange(send1)
-    halo = lax.ppermute(
-        jnp.concatenate([emb, og], axis=1), "grid", [(i + 1, i) for i in range(GROUPS - 1)]
-    )
-    recv1, halo = lax.optimization_barrier((recv1, halo))
     marks, enc = call(
         plan_kernel,
-        [((8, GROUPS * 8), I32), ((D, 3 * D), BF)],
-        (ranks, window_id.reshape(GROUPS, TILE), enc_qkv),
+        [((16, GROUPS * 8), F32), ((D, 3 * D), BF)],
+        (ranks, window_id.reshape(GROUPS, TILE), enc_qkv, mask_token[None, :], (halo, HERE)),
         "plan",
+        flops=4 * 10**9,
     )
     send2, kept = call(
         encode_kernel,
-        [((GROUPS * 8, 256), BF), ((4 * TOKENS, D), BF)],
+        [((GROUPS * 8, 256), BF), ((PACKED, D), BF, HERE)],
         (recv1, marks, enc),
         "encode",
+        scratch=[((4 * TOKENS, D), BF)],
+        sems=1,
+        limit=40,
     )
     recv2 = exchange(send2)
     flipped, packed = call(
         prepare_kernel,
         [((4 * D, D), BF), ((PACKED, D), BF, HERE)],
-        (marks, emb, og, halo, decoder_projected, enc_out, dec_qkv),
+        (marks, emb, og, halo, decoder_projected, enc_out, dec_qkv, enc_qkv),
         "prepare",
-        scratch=[((OG_ROWS + FRAME, D), BF)],
-        sems=3,
-        limit=48,
+        scratch=[((OWN, D), BF)],
+        sems=8,
+        limit=40,
     )
     send3, keep, send = call(
         decode_kernel,
-        [((GROUPS * 8, 256), BF), ((4, D, 128), BF), ((4, D, 128), BF)],
-        (marks, recv2, mask_token[None, :], flipped, (packed, HERE)),
+        [((GROUPS * 8, 256), BF, HERE), ((4, D, 128), BF), ((4, D, 128), BF)],
+        (marks, recv2, flipped, (packed, HERE)),
         "decode",
         scratch=[
+            ((GROUPS * 8, 256), BF),
             ((D, D), BF),
             ((D, D), BF),
             ((3 * D, D), BF),
@@ -424,19 +455,24 @@
             ((3 * D, FRAME), BF),
             ((D, FRAME), BF),
         ],
-        sems=4,
+        sems=5,
         limit=48,
         flops=2 * 10**9,
     )
     recv3 = exchange(send3)
     sums = call(add_kernel, [((D, 128), BF)] * 4, (keep, swap(send, 1)), "add_core")
     parts = [sums[0]] + [swap(sums[j], 2 * j) for j in range(1, 4)]
-    (send4,) = call(
+    (back,) = call(
         encode_back_kernel,
-        [((GROUPS * 8, 256), BF)],
-        (marks, recv3, enc_out, enc_qkv, kept, *parts),
+        [((GROUPS * 8, 128), BF)],
+        (marks, recv3, (packed, HERE), (kept, HERE)),
         "encode_back",
-    )
+        scratch=[((D, D), BF), ((4 * TOKENS, D), BF), ((3 * D, D), BF)],
+        sems=6,
+        limit=48,
+        flops=2 * 10**9,
+    )
+    (send4,) = call(join_kernel, [((GROUPS * 8, 256), BF)], (back, *parts), "join")
     recv4 = exchange(send4)
     tiles, grad_enc, grad_dec = call(
         finish_kernel,

time: 148 us -> 142 us (0.959)
  starting transfers between devices: 48.1 us -> 44.4 us
  waiting for transfers between devices: 35.9 us -> 32.7 us
  blocking collectives: 34.5 us -> 31.4 us
  Pallas kernels: 19.7 us -> 22.4 us
  local copies, waits for them, and re-layouts: 7.51 us -> 9.22 us
    all_to_all x3, waiting for transfers between devices: 21.1 us -> 30.8 us  [exchange(): return lax.all_to_all(rows, 'grid', split_axis=0, concat_axis=0, tiled=True)]
    ppermute x1, waiting for transfers between devices: 7.38 us -> 0.01 us  [shards(): halo = lax.ppermute(pair, 'grid', [(i + 1, i) for i in range(GROUPS - 1)])]
    ppermute x4, waiting for transfers between devices: 7.41 us -> 1.88 us  [swap(): return lax.ppermute(block, 'slide', [(i, i ^ bit) for i in range(8)])]
    all_to_all x3, starting transfers between devices: 35.7 us -> 31.9 us  [exchange(): return lax.all_to_all(rows, 'grid', split_axis=0, concat_axis=0, tiled=True)]
    all_to_all x1, blocking collectives: 34.5 us -> 31.4 us  [exchange(): return lax.all_to_all(rows, 'grid', split_axis=0, concat_axis=0, tiled=True)]
    pallas_call x8 -> x9, Pallas kernels: 19.7 us -> 22.4 us  [call(): pl.pallas_call(kernel, out_shape=[jax.ShapeDtypeStruct(o[0], o[1]) for o...]
    unnamed x24, local copies, waits for them, and re-layouts: 7.51 us -> 9.22 us
  transfers between devices with their start and end apart: 8 -> 8, of which waited for: 7 -> 4; matrix products, arithmetic and copies ran while one was open for 1% -> 0% of each run, Pallas kernels for 2% -> 5%
where the time goes in v3:
time: 142 us; the launch traced here: 141 us
  starting transfers between devices  44.4 us (31%)
  waiting for transfers between devices  32.7 us (23%)
  blocking collectives  31.4 us (22%)
  Pallas kernels  22.4 us (16%)
  local copies, waits for them, and re-layouts  9.22 us (6%)
    all_to_all x3, starting transfers between devices, exchange(): return lax.all_to_all(rows, 'grid', split_axis=0, concat_axis=0, tiled=True)  31.9 us
    all_to_all x1, blocking collectives, exchange(): return lax.all_to_all(rows, 'grid', split_axis=0, concat_axis=0, tiled=True)  31.4 us
    all_to_all x3, waiting for transfers between devices, exchange(): return lax.all_to_all(rows, 'grid', split_axis=0, concat_axis=0, tiled=True)  30.8 us
    pallas_call x9, Pallas kernels, call(): pl.pallas_call(kernel, out_shape=[jax.ShapeDtypeStruct(o[0], o[1]) for o...  22.4 us
    ppermute x4, starting transfers between devices, swap(): return lax.ppermute(block, 'slide', [(i, i ^ bit) for i in range(8)])  11.1 us
    unnamed x24, local copies, waits for them, and re-layouts  9.22 us
  transfers between devices with their start and end apart: 8, of which 4 were waited for; matrix products, arithmetic and copies ran while one was open for 0% of the time, Pallas kernels for 5%

profile of v3, /device:TPU:4, one launch (start us, length us, event | category | flops | bytes accessed | tf_op | source)
XLA Modules:
  0.0 140.9 jit_solution(15321859649798105248)
XLA Ops:
  0.6 2.4 %send_tokens.1 = (bf16[512,128]{1,0:T(8,128)(2,1)}, bf16[128,1024]{1,0:T(8,128)(2,1)}) custom-call(s32[16,128]{1,0:T(8,128)} %bitcast.24, bf16[128,512]{1,0:T(8,128)(2,1)} %bitcast.19, bf16[128,512]{1,0:T(8,128)(2,1)} %bitcast.21), custom_call_target="tpu_custom_call" | custom-call | flops 100000000 | bytes 2000000 | tf_op jit(solution)/shard_map/send_tokens/pallas_call | solution.py:373
  3.0 1.3 collective-permute-start
  4.3 19.9 %all-to-all-start = ((bf16[64,8,128]{2,1,0:T(8,128)(2,1)}), bf16[64,8,128]{2,1,0:T(8,128)(2,1)S(1)}, u32[]{:S(2)}, u32[]{:S(2)}) async-start(bf16[64,8,128]{2,1,0:T(8,128)(2,1)} %bitcast.27), calls=%async_computation | async-start | bytes 262144 | tf_op jit(solution)/shard_map/all_to_all | solution.py:386
  24.2 0.0 collective-permute-done.halo_ref
  24.2 0.0 copy-start.5
  24.2 0.0 copy-start
  24.2 1.5 %copy-done = bf16[512,1536]{1,0:T(8,128)(2,1)S(1)} copy-done((bf16[512,1536]{1,0:T(8,128)(2,1)S(1)}, bf16[512,1536]{1,0:T(8,128)(2,1)}, u32[]{:S(2)}) %copy-start) | copy-done | bytes 1572888
  25.7 0.0 copy-start.9
  25.7 0.8 copy-done.9
  26.5 0.0 copy-start.10
  26.5 0.7 copy-done.10
  27.2 0.0 copy-start.11
  27.2 0.7 copy-done.11
  27.9 0.5 plan.1
  28.4 0.0 copy-done.5
  28.4 0.0 copy-start.3
  28.4 0.0 copy-start.4
  28.4 11.9 %all-to-all-done = bf16[64,8,128]{2,1,0:T(8,128)(2,1)S(1)} async-done(((bf16[64,8,128]{2,1,0:T(8,128)(2,1)}), bf16[64,8,128]{2,1,0:T(8,128)(2,1)S(1)}, u32[]{:S(2)}, u32[]{:S(2)}) %all-to-all-start) | async-done | bytes 131104 | tf_op jit(solution)/shard_map/all_to_all | solution.py:386
  40.3 2.4 %encode.1 = (bf16[512,256]{1,0:T(8,128)(2,1)}, bf16[18432,512]{1,0:T(8,128)(2,1)}) custom-call(bf16[512,128]{1,0:T(8,128)(2,1)S(1)} %bitcast.17, f32[16,512]{1,0:T(8,128)S(1)} %get-tuple-element.22.marks_ref, bf16[512,1536]{1,0:T(8,128)(2,1)S(1)} %get-tuple-element.24.weight_ref), custom_call_target="tpu_custom_call" | custom-call | flops 100000000 | bytes 2000000 | tf_op jit(solution)/shard_map/encode/pallas_call | solution.py:373
  42.8 5.5 %all-to-all-start.1 = ((bf16[64,8,256]{2,1,0:T(8,128)(2,1)}), bf16[64,8,256]{2,1,0:T(8,128)(2,1)S(1)}, u32[]{:S(2)}, u32[]{:S(2)}) async-start(bf16[64,8,256]{2,1,0:T(8,128)(2,1)} %bitcast.7), calls=%async_computation.1 | async-start | bytes 524288 | tf_op jit(solution)/shard_map/all_to_all | solution.py:386
  48.3 0.0 copy-done.3
  48.3 0.0 copy-done.4
  48.3 0.0 copy-start.1
  48.3 1.4 copy-done.1
  49.7 0.0 copy-start.2
  49.7 1.4 copy-done.2
  51.2 0.0 copy-start.6
  51.2 0.9 copy-done.6
  52.1 0.9 copy-done.7
  53.0 0.9 copy-done.8
  53.9 2.7 %prepare.1 = (bf16[2048,512]{1,0:T(8,128)(2,1)S(1)}, bf16[18432,512]{1,0:T(8,128)(2,1)}) custom-call(f32[16,512]{1,0:T(8,128)S(1)} %get-tuple-element.22.marks_ref, bf16[128,512]{1,0:T(8,128)(2,1)S(1)} %bitcast.20, bf16[128,512]{1,0:T(8,128)(2,1)S(1)} %bitcast.22, bf16[128,1024]{1,0:T(8,128)(2,1)S(1)} %copy-done.6, bf16[512,512]{1,0:T(8,128)(2,1)S(1)} %copy-done.3, ...), custom_call_target="tpu_custom_call" | custom-call | flops 100000000 | bytes 2000000 | tf_op jit(solution)/shard_map/prepare/pallas_call | solution.py:373
  56.6 12.2 %all-to-all-done.1 = bf16[64,8,256]{2,1,0:T(8,128)(2,1)S(1)} async-done(((bf16[64,8,256]{2,1,0:T(8,128)(2,1)}), bf16[64,8,256]{2,1,0:T(8,128)(2,1)S(1)}, u32[]{:S(2)}, u32[]{:S(2)}) %all-to-all-start.1) | async-done | bytes 262176 | tf_op jit(solution)/shard_map/all_to_all | solution.py:386
  68.8 9.9 %decode.1 = (bf16[512,256]{1,0:T(8,128)(2,1)}, bf16[4,512,128]{2,1,0:T(8,128)(2,1)S(1)}, bf16[4,512,128]{2,1,0:T(8,128)(2,1)S(1)}) custom-call(f32[16,512]{1,0:T(8,128)S(1)} %get-tuple-element.22.marks_ref, bf16[512,256]{1,0:T(8,128)(2,1)S(1)} %bitcast.16, bf16[2048,512]{1,0:T(8,128)(2,1)S(1)} %get-tuple-element.26.flipped_ref, ...), custom_call_target="tpu_custom_call" | custom-call | flops 2000000000 | bytes 2000000 | tf_op jit(solution)/shard_map/decode/pallas_call | solution.py:373
  78.7 6.5 %all-to-all-start.2 = ((bf16[64,8,256]{2,1,0:T(8,128)(2,1)}), bf16[64,8,256]{2,1,0:T(8,128)(2,1)S(1)}, u32[]{:S(2)}, u32[]{:S(2)}) async-start(bf16[64,8,256]{2,1,0:T(8,128)(2,1)} %bitcast.9), calls=%async_computation.2 | async-start | bytes 524288 | tf_op jit(solution)/shard_map/all_to_all | solution.py:386
  85.2 1.9 %collective-permute-start.1 = (bf16[4,512,128]{2,1,0:T(8,128)(2,1)S(1)}, bf16[4,512,128]{2,1,0:T(8,128)(2,1)S(1)}, u32[]{:S(2)}, u32[]{:S(2)}) collective-permute-start(bf16[4,512,128]{2,1,0:T(8,128)(2,1)S(1)} %get-tuple-element.31), channel_id=1, source_target_pairs={{0,64},{64,0},{128,192},{192,128},{256,320},{320,256},{384,448},{4... | collective-permute-start | bytes 1572872 | tf_op jit(solution)/shard_map/ppermute | solution.py:390
  87.1 1.9 %collective-permute-done.1.recv_ref = bf16[4,512,128]{2,1,0:T(8,128)(2,1)S(1)} collective-permute-done((bf16[4,512,128]{2,1,0:T(8,128)(2,1)S(1)}, bf16[4,512,128]{2,1,0:T(8,128)(2,1)S(1)}, u32[]{:S(2)}, u32[]{:S(2)}) %collective-permute-start.1) | collective-permute-done | bytes 524320 | tf_op jit(solution)/shard_map/ppermute | solution.py:390
  89.0 0.1 add_core.1
  89.1 3.1 %collective-permute-start.2 = (bf16[512,128]{1,0:T(8,128)(2,1)S(1)}, bf16[512,128]{1,0:T(8,128)(2,1)S(1)}, u32[]{:S(2)}, u32[]{:S(2)}) collective-permute-start(bf16[512,128]{1,0:T(8,128)(2,1)S(1)} %get-tuple-element.33), channel_id=1, source_target_pairs={{0,128},{64,192},{128,0},{192,64},{256,384},{320,448},{384,256},{4... | collective-permute-start | bytes 393224 | tf_op jit(solution)/shard_map/ppermute | solution.py:390
  92.2 2.7 %collective-permute-start.3 = (bf16[512,128]{1,0:T(8,128)(2,1)S(1)}, bf16[512,128]{1,0:T(8,128)(2,1)S(1)}, u32[]{:S(2)}, u32[]{:S(2)}) collective-permute-start(bf16[512,128]{1,0:T(8,128)(2,1)S(1)} %get-tuple-element.34), channel_id=1, source_target_pairs={{0,256},{64,320},{128,384},{192,448},{256,0},{320,64},{384,128},{4... | collective-permute-start | bytes 393224 | tf_op jit(solution)/shard_map/ppermute | solution.py:390
  94.9 3.4 %collective-permute-start.4 = (bf16[512,128]{1,0:T(8,128)(2,1)S(1)}, bf16[512,128]{1,0:T(8,128)(2,1)S(1)}, u32[]{:S(2)}, u32[]{:S(2)}) collective-permute-start(bf16[512,128]{1,0:T(8,128)(2,1)S(1)} %get-tuple-element.35), channel_id=1, source_target_pairs={{0,384},{64,448},{128,256},{192,320},{256,128},{320,192},{384,0},{... | collective-permute-start | bytes 393224 | tf_op jit(solution)/shard_map/ppermute | solution.py:390
  98.3 6.7 %all-to-all-done.2 = bf16[64,8,256]{2,1,0:T(8,128)(2,1)S(1)} async-done(((bf16[64,8,256]{2,1,0:T(8,128)(2,1)}), bf16[64,8,256]{2,1,0:T(8,128)(2,1)S(1)}, u32[]{:S(2)}, u32[]{:S(2)}) %all-to-all-start.2) | async-done | bytes 262176 | tf_op jit(solution)/shard_map/all_to_all | solution.py:386
  105.0 3.3 %encode_back.1.tokens_ref = bf16[512,128]{1,0:T(8,128)(2,1)S(1)} custom-call(f32[16,512]{1,0:T(8,128)S(1)} %get-tuple-element.22.marks_ref, bf16[512,256]{1,0:T(8,128)(2,1)S(1)} %bitcast.14, bf16[18432,512]{1,0:T(8,128)(2,1)} %get-tuple-element.27.packed, bf16[18432,512]{1,0:T(8,128)(2,1)} %get-tuple-element.29.store), custom_call_target="tpu_custom_call" | custom-call | flops 2000000000 | bytes 2000000 | tf_op jit(solution)/shard_map/encode_back/pallas_call | solution.py:373
  108.3 0.0 collective-permute-done.2.part1
  108.3 0.0 collective-permute-done.3.part2
  108.3 0.0 collective-permute-done.4.part3
  108.3 0.1 join.1
  108.4 31.4 %all_to_all.44 = bf16[64,8,256]{2,1,0:T(8,128)(2,1)S(1)} all-to-all(bf16[64,8,256]{2,1,0:T(8,128)(2,1)S(1)} %bitcast.15), channel_id=1, replica_groups=mesh['slide'=8,'grid'=64] {'grid'}, dimensions={0} | all-to-all | bytes 524288 | tf_op jit(solution)/shard_map/all_to_all | solution.py:386
  139.8 1.1 finish.1
  (2 shorter events, 0.0 us)
Async XLA Ops:
  3.0 21.2 %collective-permute-start = (bf16[128,1024]{1,0:T(8,128)(2,1)}, bf16[128,1024]{1,0:T(8,128)(2,1)S(1)}, u32[]{:S(2)}, u32[]{:S(2)}) collective-permute-start(bf16[128,1024]{1,0:T(8,128)(2,1)} %get-tuple-element.21), channel_id=1, source_target_pairs={{1,0},{2,1},{3,2},{4,3},{5,4},{6,5},{7,6},{8,7},{9,8},{10,9},{11,1... | collective-permute-start | bytes 786440 | tf_op jit(solution)/shard_map/ppermute | solution.py:416
  4.3 36.1 %all-to-all-start = ((bf16[64,8,128]{2,1,0:T(8,128)(2,1)}), bf16[64,8,128]{2,1,0:T(8,128)(2,1)S(1)}, u32[]{:S(2)}, u32[]{:S(2)}) async-start(bf16[64,8,128]{2,1,0:T(8,128)(2,1)} %bitcast.27), calls=%async_computation | async-start | bytes 262144 | tf_op jit(solution)/shard_map/all_to_all | solution.py:386
  24.2 4.2 %copy-start.5 = (bf16[128,1024]{1,0:T(8,128)(2,1)}, bf16[128,1024]{1,0:T(8,128)(2,1)S(1)}, u32[]{:S(2)}) copy-start(bf16[128,1024]{1,0:T(8,128)(2,1)S(1)} %collective-permute-done.halo_ref) | copy-start | bytes 786436
  24.2 1.5 %copy-start = (bf16[512,1536]{1,0:T(8,128)(2,1)S(1)}, bf16[512,1536]{1,0:T(8,128)(2,1)}, u32[]{:S(2)}) copy-start(bf16[512,1536]{1,0:T(8,128)(2,1)} %enc_qkv_ref.3) | copy-start | bytes 4718596
  25.7 0.8 copy-start.9
  26.5 0.7 copy-start.10
  27.2 0.7 copy-start.11
  28.4 19.9 %copy-start.3 = (bf16[512,512]{1,0:T(8,128)(2,1)S(1)}, bf16[512,512]{1,0:T(8,128)(2,1)}, u32[]{:S(2)}) copy-start(bf16[512,512]{1,0:T(8,128)(2,1)} %proj_ref.1) | copy-start | bytes 1572868
  28.4 19.9 %copy-start.4 = (bf16[512,512]{1,0:T(8,128)(2,1)S(1)}, bf16[512,512]{1,0:T(8,128)(2,1)}, u32[]{:S(2)}) copy-start(bf16[512,512]{1,0:T(8,128)(2,1)} %enc_out_ref.1) | copy-start | bytes 1572868
  42.8 26.0 %all-to-all-start.1 = ((bf16[64,8,256]{2,1,0:T(8,128)(2,1)}), bf16[64,8,256]{2,1,0:T(8,128)(2,1)S(1)}, u32[]{:S(2)}, u32[]{:S(2)}) async-start(bf16[64,8,256]{2,1,0:T(8,128)(2,1)} %bitcast.7), calls=%async_computation.1 | async-start | bytes 524288 | tf_op jit(solution)/shard_map/all_to_all | solution.py:386
  48.3 1.4 %copy-start.1 = (bf16[512,1536]{1,0:T(8,128)(2,1)S(1)}, bf16[512,1536]{1,0:T(8,128)(2,1)}, u32[]{:S(2)}) copy-start(bf16[512,1536]{1,0:T(8,128)(2,1)} %enc_qkv_ref.3) | copy-start | bytes 4718596
  49.7 1.4 copy-start.2
  51.2 0.9 copy-start.6
  52.1 0.9 copy-start.7
  53.0 0.9 copy-start.8
  78.7 26.3 %all-to-all-start.2 = ((bf16[64,8,256]{2,1,0:T(8,128)(2,1)}), bf16[64,8,256]{2,1,0:T(8,128)(2,1)S(1)}, u32[]{:S(2)}, u32[]{:S(2)}) async-start(bf16[64,8,256]{2,1,0:T(8,128)(2,1)} %bitcast.9), calls=%async_computation.2 | async-start | bytes 524288 | tf_op jit(solution)/shard_map/all_to_all | solution.py:386
  85.2 3.8 %collective-permute-start.1 = (bf16[4,512,128]{2,1,0:T(8,128)(2,1)S(1)}, bf16[4,512,128]{2,1,0:T(8,128)(2,1)S(1)}, u32[]{:S(2)}, u32[]{:S(2)}) collective-permute-start(bf16[4,512,128]{2,1,0:T(8,128)(2,1)S(1)} %get-tuple-element.31), channel_id=1, source_target_pairs={{0,64},{64,0},{128,192},{192,128},{256,320},{320,256},{384,448},{4... | collective-permute-start | bytes 1572872 | tf_op jit(solution)/shard_map/ppermute | solution.py:390
  89.1 19.2 %collective-permute-start.2 = (bf16[512,128]{1,0:T(8,128)(2,1)S(1)}, bf16[512,128]{1,0:T(8,128)(2,1)S(1)}, u32[]{:S(2)}, u32[]{:S(2)}) collective-permute-start(bf16[512,128]{1,0:T(8,128)(2,1)S(1)} %get-tuple-element.33), channel_id=1, source_target_pairs={{0,128},{64,192},{128,0},{192,64},{256,384},{320,448},{384,256},{4... | collective-permute-start | bytes 393224 | tf_op jit(solution)/shard_map/ppermute | solution.py:390
  92.2 16.1 %collective-permute-start.3 = (bf16[512,128]{1,0:T(8,128)(2,1)S(1)}, bf16[512,128]{1,0:T(8,128)(2,1)S(1)}, u32[]{:S(2)}, u32[]{:S(2)}) collective-permute-start(bf16[512,128]{1,0:T(8,128)(2,1)S(1)} %get-tuple-element.34), channel_id=1, source_target_pairs={{0,256},{64,320},{128,384},{192,448},{256,0},{320,64},{384,128},{4... | collective-permute-start | bytes 393224 | tf_op jit(solution)/shard_map/ppermute | solution.py:390
  94.9 13.4 %collective-permute-start.4 = (bf16[512,128]{1,0:T(8,128)(2,1)S(1)}, bf16[512,128]{1,0:T(8,128)(2,1)S(1)}, u32[]{:S(2)}, u32[]{:S(2)}) collective-permute-start(bf16[512,128]{1,0:T(8,128)(2,1)S(1)} %get-tuple-element.35), channel_id=1, source_target_pairs={{0,384},{64,448},{128,256},{192,320},{256,128},{320,192},{384,0},{... | collective-permute-start | bytes 393224 | tf_op jit(solution)/shard_map/ppermute | solution.py:390

commit v4 on v3

--- a/solution.py
+++ b/solution.py
@@ -15,6 +15,7 @@
 TOKENS = 32
 EPS = 1e-06
 SCALE = 0.125
+LOG2E = 1.4426950408889634
 NEG = -1e30
 BF = jnp.bfloat16
 F32 = jnp.float32
@@ -254,26 +255,38 @@
     x = jnp.where(live, (more()[:, :FRAME].astype(F32) + delta).astype(BF).astype(F32), blank)
     inv = lax.rsqrt(jnp.mean(x * x, axis=0, keepdims=True) + EPS)
     normed = (x * inv).astype(BF)
-    qkv = nn(flipped_ref[:OUT_T, :], normed).astype(BF)
-    keys = qkv[D : 2 * D].T
-    vals = qkv[2 * D :].T
+    keys_t = nn(flipped_ref[D : 2 * D, :], normed).astype(BF)
+    keys = keys_t.T
+    vals_t = nn(flipped_ref[2 * D : OUT_T, :], normed).astype(BF)
+    vals = vals_t.T
+    qkv = (nn(flipped_ref[:D, :], normed).astype(BF), keys_t, vals_t)
     bias_rows = more()[:FRAME, FRAME:].astype(F32)
     both_b = both()
-    for h in range(HEADS):
-        spot = slice(h * HEAD, (h + 1) * HEAD)
-        q_t, k_t, v_t = qkv[spot], qkv[D + h * HEAD : D + (h + 1) * HEAD], qkv[2 * D + h * HEAD : 2 * D + (h + 1) * HEAD]
-        d_t = both_b[spot, :FRAME]
-        scores = nn(keys[:, spot], q_t) * SCALE + bias_rows
-        weights = jnp.exp(scores - jnp.max(scores, axis=0, keepdims=True))
-        probs = weights * (1.0 / jnp.sum(weights, axis=0, keepdims=True))
-        probs_b = probs.astype(BF)
-        ctx_ref[spot, :] = jnp.where(owned, nn(v_t, probs_b), 0.0).astype(BF)
-        dprobs = nn(vals[:, spot], d_t).astype(BF).astype(F32)
-        inner = jnp.sum(probs * dprobs, axis=0, keepdims=True)
-        dscores = (probs * (dprobs - inner) * SCALE).astype(BF)
-        dqkv_ref[spot, :] = nn(k_t, dscores).astype(BF)
-        dqkv_ref[D + h * HEAD : D + (h + 1) * HEAD, :] = nt(q_t, dscores).astype(BF)
-        dqkv_ref[2 * D + h * HEAD : 2 * D + (h + 1) * HEAD, :] = nt(d_t, probs_b).astype(BF)
+    for first in range(0, HEADS, 8):
+        group = range(first, first + 8)
+        q, k, v, d = {}, {}, {}, {}
+        for h in group:
+            spot = slice(h * HEAD, (h + 1) * HEAD)
+            q[h], k[h], v[h] = [block[spot] for block in qkv]
+            d[h] = both_b[spot, :FRAME]
+        scores = {h: nn(keys[:, h * HEAD : (h + 1) * HEAD], q[h]) for h in group}
+        dprobs = {h: nn(vals[:, h * HEAD : (h + 1) * HEAD], d[h]) for h in group}
+        probs = {}
+        for h in group:
+            logits = scores[h] * (SCALE * LOG2E) + bias_rows
+            weights = jnp.exp2(logits - jnp.max(logits, axis=0, keepdims=True))
+            probs[h] = weights * (1.0 / jnp.sum(weights, axis=0, keepdims=True))
+        probs_b = {h: probs[h].astype(BF) for h in group}
+        context = {h: nn(v[h], probs_b[h]) for h in group}
+        dscores = {}
+        for h in group:
+            ctx_ref[h * HEAD : (h + 1) * HEAD, :] = jnp.where(owned, context[h], 0.0).astype(BF)
+            inner = jnp.sum(context[h] * d[h].astype(F32), axis=0, keepdims=True)
+            dscores[h] = (probs[h] * (dprobs[h] - inner)).astype(BF)
+        for h in group:
+            dqkv_ref[h * HEAD : (h + 1) * HEAD, :] = (nn(k[h], dscores[h]) * SCALE).astype(BF)
+            dqkv_ref[D + h * HEAD : D + (h + 1) * HEAD, :] = (nt(q[h], dscores[h]) * SCALE).astype(BF)
+            dqkv_ref[2 * D + h * HEAD : 2 * D + (h + 1) * HEAD, :] = nt(d[h], probs_b[h]).astype(BF)
 
     weight_ref = qkv_w()
     dnormed = nn(weight_ref[:D, :], dqkv_ref[:D, :])

time: 142 us -> 138 us (0.972)
  Pallas kernels: 22.4 us -> 18.9 us
    pallas_call x9, Pallas kernels: 22.4 us -> 18.9 us  [call(): pl.pallas_call(kernel, out_shape=[jax.ShapeDtypeStruct(o[0], o[1]) for o...]
where the time goes in v4:
time: 138 us; the launch traced here: 137 us
  starting transfers between devices  44.4 us (32%)
  waiting for transfers between devices  32.6 us (24%)
  blocking collectives  31.4 us (23%)
  Pallas kernels  18.9 us (14%)
  local copies, waits for them, and re-layouts  9.22 us (7%)
    all_to_all x3, starting transfers between devices, exchange(): return lax.all_to_all(rows, 'grid', split_axis=0, concat_axis=0, tiled=True)  31.9 us
    all_to_all x1, blocking collectives, exchange(): return lax.all_to_all(rows, 'grid', split_axis=0, concat_axis=0, tiled=True)  31.4 us
    all_to_all x3, waiting for transfers between devices, exchange(): return lax.all_to_all(rows, 'grid', split_axis=0, concat_axis=0, tiled=True)  30.8 us
    pallas_call x9, Pallas kernels, call(): pl.pallas_call(kernel, out_shape=[jax.ShapeDtypeStruct(o[0], o[1]) for o...  18.9 us
    ppermute x4, starting transfers between devices, swap(): return lax.ppermute(block, 'slide', [(i, i ^ bit) for i in range(8)])  11.1 us
    unnamed x24, local copies, waits for them, and re-layouts  9.22 us
  transfers between devices with their start and end apart: 8, of which 4 were waited for; matrix products, arithmetic and copies ran while one was open for 0% of the time, Pallas kernels for 5%

profile of v4, /device:TPU:4, one launch (start us, length us, event | category | flops | bytes accessed | tf_op | source)
XLA Modules:
  0.0 137.4 jit_solution(8006795846241113849)
XLA Ops:
  0.6 2.4 %send_tokens.1 = (bf16[512,128]{1,0:T(8,128)(2,1)}, bf16[128,1024]{1,0:T(8,128)(2,1)}) custom-call(s32[16,128]{1,0:T(8,128)} %bitcast.24, bf16[128,512]{1,0:T(8,128)(2,1)} %bitcast.19, bf16[128,512]{1,0:T(8,128)(2,1)} %bitcast.21), custom_call_target="tpu_custom_call" | custom-call | flops 100000000 | bytes 2000000 | tf_op jit(solution)/shard_map/send_tokens/pallas_call | solution.py:386
  3.0 1.3 collective-permute-start
  4.3 19.9 %all-to-all-start = ((bf16[64,8,128]{2,1,0:T(8,128)(2,1)}), bf16[64,8,128]{2,1,0:T(8,128)(2,1)S(1)}, u32[]{:S(2)}, u32[]{:S(2)}) async-start(bf16[64,8,128]{2,1,0:T(8,128)(2,1)} %bitcast.27), calls=%async_computation | async-start | bytes 262144 | tf_op jit(solution)/shard_map/all_to_all | solution.py:399
  24.2 0.0 collective-permute-done.halo_ref
  24.2 0.0 copy-start.5
  24.2 0.0 copy-start
  24.2 1.5 %copy-done = bf16[512,1536]{1,0:T(8,128)(2,1)S(1)} copy-done((bf16[512,1536]{1,0:T(8,128)(2,1)S(1)}, bf16[512,1536]{1,0:T(8,128)(2,1)}, u32[]{:S(2)}) %copy-start) | copy-done | bytes 1572888
  25.7 0.0 copy-start.9
  25.7 0.8 copy-done.9
  26.5 0.0 copy-start.10
  26.5 0.7 copy-done.10
  27.2 0.0 copy-start.11
  27.2 0.7 copy-done.11
  27.9 0.5 plan.1
  28.4 0.0 copy-done.5
  28.4 0.0 copy-start.3
  28.4 0.0 copy-start.4
  28.4 11.9 %all-to-all-done = bf16[64,8,128]{2,1,0:T(8,128)(2,1)S(1)} async-done(((bf16[64,8,128]{2,1,0:T(8,128)(2,1)}), bf16[64,8,128]{2,1,0:T(8,128)(2,1)S(1)}, u32[]{:S(2)}, u32[]{:S(2)}) %all-to-all-start) | async-done | bytes 131104 | tf_op jit(solution)/shard_map/all_to_all | solution.py:399
  40.3 2.4 %encode.1 = (bf16[512,256]{1,0:T(8,128)(2,1)}, bf16[18432,512]{1,0:T(8,128)(2,1)}) custom-call(bf16[512,128]{1,0:T(8,128)(2,1)S(1)} %bitcast.17, f32[16,512]{1,0:T(8,128)S(1)} %get-tuple-element.22.marks_ref, bf16[512,1536]{1,0:T(8,128)(2,1)S(1)} %get-tuple-element.24.weight_ref), custom_call_target="tpu_custom_call" | custom-call | flops 100000000 | bytes 2000000 | tf_op jit(solution)/shard_map/encode/pallas_call | solution.py:386
  42.8 5.5 %all-to-all-start.1 = ((bf16[64,8,256]{2,1,0:T(8,128)(2,1)}), bf16[64,8,256]{2,1,0:T(8,128)(2,1)S(1)}, u32[]{:S(2)}, u32[]{:S(2)}) async-start(bf16[64,8,256]{2,1,0:T(8,128)(2,1)} %bitcast.7), calls=%async_computation.1 | async-start | bytes 524288 | tf_op jit(solution)/shard_map/all_to_all | solution.py:399
  48.3 0.0 copy-done.3
  48.3 0.0 copy-done.4
  48.3 0.0 copy-start.1
  48.3 1.4 %copy-done.1 = bf16[512,1536]{1,0:T(8,128)(2,1)S(1)} copy-done((bf16[512,1536]{1,0:T(8,128)(2,1)S(1)}, bf16[512,1536]{1,0:T(8,128)(2,1)}, u32[]{:S(2)}) %copy-start.1) | copy-done | bytes 1572888
  49.7 0.0 copy-start.2
  49.7 1.4 %copy-done.2 = bf16[512,1536]{1,0:T(8,128)(2,1)S(1)} copy-done((bf16[512,1536]{1,0:T(8,128)(2,1)S(1)}, bf16[512,1536]{1,0:T(8,128)(2,1)}, u32[]{:S(2)}) %copy-start.2) | copy-done | bytes 1572888
  51.1 0.0 copy-start.6
  51.2 0.9 copy-done.6
  52.1 0.9 copy-done.7
  53.0 0.9 copy-done.8
  53.9 2.7 %prepare.1 = (bf16[2048,512]{1,0:T(8,128)(2,1)S(1)}, bf16[18432,512]{1,0:T(8,128)(2,1)}) custom-call(f32[16,512]{1,0:T(8,128)S(1)} %get-tuple-element.22.marks_ref, bf16[128,512]{1,0:T(8,128)(2,1)S(1)} %bitcast.20, bf16[128,512]{1,0:T(8,128)(2,1)S(1)} %bitcast.22, bf16[128,1024]{1,0:T(8,128)(2,1)S(1)} %copy-done.6, bf16[512,512]{1,0:T(8,128)(2,1)S(1)} %copy-done.3, ...), custom_call_target="tpu_custom_call" | custom-call | flops 100000000 | bytes 2000000 | tf_op jit(solution)/shard_map/prepare/pallas_call | solution.py:386
  56.6 12.2 %all-to-all-done.1 = bf16[64,8,256]{2,1,0:T(8,128)(2,1)S(1)} async-done(((bf16[64,8,256]{2,1,0:T(8,128)(2,1)}), bf16[64,8,256]{2,1,0:T(8,128)(2,1)S(1)}, u32[]{:S(2)}, u32[]{:S(2)}) %all-to-all-start.1) | async-done | bytes 262176 | tf_op jit(solution)/shard_map/all_to_all | solution.py:399
  68.8 6.4 %decode.1 = (bf16[512,256]{1,0:T(8,128)(2,1)}, bf16[4,512,128]{2,1,0:T(8,128)(2,1)S(1)}, bf16[4,512,128]{2,1,0:T(8,128)(2,1)S(1)}) custom-call(f32[16,512]{1,0:T(8,128)S(1)} %get-tuple-element.22.marks_ref, bf16[512,256]{1,0:T(8,128)(2,1)S(1)} %bitcast.16, bf16[2048,512]{1,0:T(8,128)(2,1)S(1)} %get-tuple-element.26.flipped_ref, ...), custom_call_target="tpu_custom_call" | custom-call | flops 2000000000 | bytes 2000000 | tf_op jit(solution)/shard_map/decode/pallas_call | solution.py:386
  75.2 6.5 %all-to-all-start.2 = ((bf16[64,8,256]{2,1,0:T(8,128)(2,1)}), bf16[64,8,256]{2,1,0:T(8,128)(2,1)S(1)}, u32[]{:S(2)}, u32[]{:S(2)}) async-start(bf16[64,8,256]{2,1,0:T(8,128)(2,1)} %bitcast.9), calls=%async_computation.2 | async-start | bytes 524288 | tf_op jit(solution)/shard_map/all_to_all | solution.py:399
  81.7 1.9 %collective-permute-start.1 = (bf16[4,512,128]{2,1,0:T(8,128)(2,1)S(1)}, bf16[4,512,128]{2,1,0:T(8,128)(2,1)S(1)}, u32[]{:S(2)}, u32[]{:S(2)}) collective-permute-start(bf16[4,512,128]{2,1,0:T(8,128)(2,1)S(1)} %get-tuple-element.31), channel_id=1, source_target_pairs={{0,64},{64,0},{128,192},{192,128},{256,320},{320,256},{384,448},{4... | collective-permute-start | bytes 1572872 | tf_op jit(solution)/shard_map/ppermute | solution.py:403
  83.6 1.9 %collective-permute-done.1.recv_ref = bf16[4,512,128]{2,1,0:T(8,128)(2,1)S(1)} collective-permute-done((bf16[4,512,128]{2,1,0:T(8,128)(2,1)S(1)}, bf16[4,512,128]{2,1,0:T(8,128)(2,1)S(1)}, u32[]{:S(2)}, u32[]{:S(2)}) %collective-permute-start.1) | collective-permute-done | bytes 524320 | tf_op jit(solution)/shard_map/ppermute | solution.py:403
  85.5 0.1 add_core.1
  85.6 3.1 %collective-permute-start.2 = (bf16[512,128]{1,0:T(8,128)(2,1)S(1)}, bf16[512,128]{1,0:T(8,128)(2,1)S(1)}, u32[]{:S(2)}, u32[]{:S(2)}) collective-permute-start(bf16[512,128]{1,0:T(8,128)(2,1)S(1)} %get-tuple-element.33), channel_id=1, source_target_pairs={{0,128},{64,192},{128,0},{192,64},{256,384},{320,448},{384,256},{4... | collective-permute-start | bytes 393224 | tf_op jit(solution)/shard_map/ppermute | solution.py:403
  88.7 2.7 %collective-permute-start.3 = (bf16[512,128]{1,0:T(8,128)(2,1)S(1)}, bf16[512,128]{1,0:T(8,128)(2,1)S(1)}, u32[]{:S(2)}, u32[]{:S(2)}) collective-permute-start(bf16[512,128]{1,0:T(8,128)(2,1)S(1)} %get-tuple-element.34), channel_id=1, source_target_pairs={{0,256},{64,320},{128,384},{192,448},{256,0},{320,64},{384,128},{4... | collective-permute-start | bytes 393224 | tf_op jit(solution)/shard_map/ppermute | solution.py:403
  91.5 3.4 %collective-permute-start.4 = (bf16[512,128]{1,0:T(8,128)(2,1)S(1)}, bf16[512,128]{1,0:T(8,128)(2,1)S(1)}, u32[]{:S(2)}, u32[]{:S(2)}) collective-permute-start(bf16[512,128]{1,0:T(8,128)(2,1)S(1)} %get-tuple-element.35), channel_id=1, source_target_pairs={{0,384},{64,448},{128,256},{192,320},{256,128},{320,192},{384,0},{... | collective-permute-start | bytes 393224 | tf_op jit(solution)/shard_map/ppermute | solution.py:403
  94.9 6.6 %all-to-all-done.2 = bf16[64,8,256]{2,1,0:T(8,128)(2,1)S(1)} async-done(((bf16[64,8,256]{2,1,0:T(8,128)(2,1)}), bf16[64,8,256]{2,1,0:T(8,128)(2,1)S(1)}, u32[]{:S(2)}, u32[]{:S(2)}) %all-to-all-start.2) | async-done | bytes 262176 | tf_op jit(solution)/shard_map/all_to_all | solution.py:399
  101.5 3.3 %encode_back.1.tokens_ref = bf16[512,128]{1,0:T(8,128)(2,1)S(1)} custom-call(f32[16,512]{1,0:T(8,128)S(1)} %get-tuple-element.22.marks_ref, bf16[512,256]{1,0:T(8,128)(2,1)S(1)} %bitcast.14, bf16[18432,512]{1,0:T(8,128)(2,1)} %get-tuple-element.27.packed, bf16[18432,512]{1,0:T(8,128)(2,1)} %get-tuple-element.29.store), custom_call_target="tpu_custom_call" | custom-call | flops 2000000000 | bytes 2000000 | tf_op jit(solution)/shard_map/encode_back/pallas_call | solution.py:386
  104.8 0.0 collective-permute-done.2.part1
  104.8 0.0 collective-permute-done.3.part2
  104.8 0.0 collective-permute-done.4.part3
  104.8 0.1 join.1
  104.9 31.4 %all_to_all.44 = bf16[64,8,256]{2,1,0:T(8,128)(2,1)S(1)} all-to-all(bf16[64,8,256]{2,1,0:T(8,128)(2,1)S(1)} %bitcast.15), channel_id=1, replica_groups=mesh['slide'=8,'grid'=64] {'grid'}, dimensions={0} | all-to-all | bytes 524288 | tf_op jit(solution)/shard_map/all_to_all | solution.py:399
  136.3 1.1 finish.1
  (2 shorter events, 0.0 us)
Async XLA Ops:
  3.0 21.2 %collective-permute-start = (bf16[128,1024]{1,0:T(8,128)(2,1)}, bf16[128,1024]{1,0:T(8,128)(2,1)S(1)}, u32[]{:S(2)}, u32[]{:S(2)}) collective-permute-start(bf16[128,1024]{1,0:T(8,128)(2,1)} %get-tuple-element.21), channel_id=1, source_target_pairs={{1,0},{2,1},{3,2},{4,3},{5,4},{6,5},{7,6},{8,7},{9,8},{10,9},{11,1... | collective-permute-start | bytes 786440 | tf_op jit(solution)/shard_map/ppermute | solution.py:429
  4.3 36.1 %all-to-all-start = ((bf16[64,8,128]{2,1,0:T(8,128)(2,1)}), bf16[64,8,128]{2,1,0:T(8,128)(2,1)S(1)}, u32[]{:S(2)}, u32[]{:S(2)}) async-start(bf16[64,8,128]{2,1,0:T(8,128)(2,1)} %bitcast.27), calls=%async_computation | async-start | bytes 262144 | tf_op jit(solution)/shard_map/all_to_all | solution.py:399
  24.2 4.2 %copy-start.5 = (bf16[128,1024]{1,0:T(8,128)(2,1)}, bf16[128,1024]{1,0:T(8,128)(2,1)S(1)}, u32[]{:S(2)}) copy-start(bf16[128,1024]{1,0:T(8,128)(2,1)S(1)} %collective-permute-done.halo_ref) | copy-start | bytes 786436
  24.2 1.5 %copy-start = (bf16[512,1536]{1,0:T(8,128)(2,1)S(1)}, bf16[512,1536]{1,0:T(8,128)(2,1)}, u32[]{:S(2)}) copy-start(bf16[512,1536]{1,0:T(8,128)(2,1)} %enc_qkv_ref.3) | copy-start | bytes 4718596
  25.7 0.8 copy-start.9
  26.5 0.7 copy-start.10
  27.2 0.7 copy-start.11
  28.4 19.9 %copy-start.3 = (bf16[512,512]{1,0:T(8,128)(2,1)S(1)}, bf16[512,512]{1,0:T(8,128)(2,1)}, u32[]{:S(2)}) copy-start(bf16[512,512]{1,0:T(8,128)(2,1)} %proj_ref.1) | copy-start | bytes 1572868
  28.4 19.9 %copy-start.4 = (bf16[512,512]{1,0:T(8,128)(2,1)S(1)}, bf16[512,512]{1,0:T(8,128)(2,1)}, u32[]{:S(2)}) copy-start(bf16[512,512]{1,0:T(8,128)(2,1)} %enc_out_ref.1) | copy-start | bytes 1572868
  42.8 26.0 %all-to-all-start.1 = ((bf16[64,8,256]{2,1,0:T(8,128)(2,1)}), bf16[64,8,256]{2,1,0:T(8,128)(2,1)S(1)}, u32[]{:S(2)}, u32[]{:S(2)}) async-start(bf16[64,8,256]{2,1,0:T(8,128)(2,1)} %bitcast.7), calls=%async_computation.1 | async-start | bytes 524288 | tf_op jit(solution)/shard_map/all_to_all | solution.py:399
  48.3 1.4 %copy-start.1 = (bf16[512,1536]{1,0:T(8,128)(2,1)S(1)}, bf16[512,1536]{1,0:T(8,128)(2,1)}, u32[]{:S(2)}) copy-start(bf16[512,1536]{1,0:T(8,128)(2,1)} %enc_qkv_ref.3) | copy-start | bytes 4718596
  49.7 1.4 %copy-start.2 = (bf16[512,1536]{1,0:T(8,128)(2,1)S(1)}, bf16[512,1536]{1,0:T(8,128)(2,1)}, u32[]{:S(2)}) copy-start(bf16[512,1536]{1,0:T(8,128)(2,1)} %qkv_ref.1) | copy-start | bytes 4718596
  51.1 0.9 copy-start.6
  52.1 0.9 copy-start.7
  53.0 0.9 copy-start.8
  75.2 26.3 %all-to-all-start.2 = ((bf16[64,8,256]{2,1,0:T(8,128)(2,1)}), bf16[64,8,256]{2,1,0:T(8,128)(2,1)S(1)}, u32[]{:S(2)}, u32[]{:S(2)}) async-start(bf16[64,8,256]{2,1,0:T(8,128)(2,1)} %bitcast.9), calls=%async_computation.2 | async-start | bytes 524288 | tf_op jit(solution)/shard_map/all_to_all | solution.py:399
  81.7 3.8 %collective-permute-start.1 = (bf16[4,512,128]{2,1,0:T(8,128)(2,1)S(1)}, bf16[4,512,128]{2,1,0:T(8,128)(2,1)S(1)}, u32[]{:S(2)}, u32[]{:S(2)}) collective-permute-start(bf16[4,512,128]{2,1,0:T(8,128)(2,1)S(1)} %get-tuple-element.31), channel_id=1, source_target_pairs={{0,64},{64,0},{128,192},{192,128},{256,320},{320,256},{384,448},{4... | collective-permute-start | bytes 1572872 | tf_op jit(solution)/shard_map/ppermute | solution.py:403
  85.6 19.2 %collective-permute-start.2 = (bf16[512,128]{1,0:T(8,128)(2,1)S(1)}, bf16[512,128]{1,0:T(8,128)(2,1)S(1)}, u32[]{:S(2)}, u32[]{:S(2)}) collective-permute-start(bf16[512,128]{1,0:T(8,128)(2,1)S(1)} %get-tuple-element.33), channel_id=1, source_target_pairs={{0,128},{64,192},{128,0},{192,64},{256,384},{320,448},{384,256},{4... | collective-permute-start | bytes 393224 | tf_op jit(solution)/shard_map/ppermute | solution.py:403
  88.7 16.1 %collective-permute-start.3 = (bf16[512,128]{1,0:T(8,128)(2,1)S(1)}, bf16[512,128]{1,0:T(8,128)(2,1)S(1)}, u32[]{:S(2)}, u32[]{:S(2)}) collective-permute-start(bf16[512,128]{1,0:T(8,128)(2,1)S(1)} %get-tuple-element.34), channel_id=1, source_target_pairs={{0,256},{64,320},{128,384},{192,448},{256,0},{320,64},{384,128},{4... | collective-permute-start | bytes 393224 | tf_op jit(solution)/shard_map/ppermute | solution.py:403
  91.5 13.4 %collective-permute-start.4 = (bf16[512,128]{1,0:T(8,128)(2,1)S(1)}, bf16[512,128]{1,0:T(8,128)(2,1)S(1)}, u32[]{:S(2)}, u32[]{:S(2)}) collective-permute-start(bf16[512,128]{1,0:T(8,128)(2,1)S(1)} %get-tuple-element.35), channel_id=1, source_target_pairs={{0,384},{64,448},{128,256},{192,320},{256,128},{320,192},{384,0},{... | collective-permute-start | bytes 393224 | tf_op jit(solution)/shard_map/ppermute | solution.py:403

commit v5 on v4

--- a/solution.py
+++ b/solution.py
@@ -82,22 +82,25 @@
     return jnp.where(present, (rank & (GROUPS - 1)) * 2 + ((rank - base) >> 6), -1)
 
 
-def send_tokens_kernel(visible_hbm, emb_hbm, og_hbm, out_ref, pair_hbm, visible_b, emb_b, og_b, sems):
+def send_tokens_kernel(visible_hbm, emb_hbm, og_hbm, out_hbm, pair_hbm, visible_b, emb_b, og_b, out_ref, sems):
+    og = Load(og_hbm, og_b, sems, 2)
+    emb = Load(emb_hbm, emb_b, sems, 1)
     visible = Load(visible_hbm, visible_b, sems, 0)
-    emb = Load(emb_hbm, emb_b, sems, 1)
-    og = Load(og_hbm, og_b, sems, 2)
+    ship_og = pltpu.make_async_copy(og(), pair_hbm.at[:, D:], sems.at[4])
+    ship_og.start()
+    emb_ref = emb()
+    ship_emb = pltpu.make_async_copy(emb_ref, pair_hbm.at[:, :D], sems.at[3])
+    ship_emb.start()
     slot = own_slots(visible(), lax.axis_index("grid") * TILE)
     rows = iota((GROUPS * 8, TILE), 0)
     picks = [onehot(rows == slot * 4 + part) for part in range(4)]
-    emb_ref = emb()
-    ship_emb = pltpu.make_async_copy(emb_ref, pair_hbm.at[:, :D], sems.at[3])
-    ship_emb.start()
-    ship_og = pltpu.make_async_copy(og(), pair_hbm.at[:, D:], sems.at[4])
-    ship_og.start()
     total = jnp.zeros((GROUPS * 8, TILE), F32)
     for part in range(4):
         total += nn(picks[part], emb_ref[:, part * 128 : (part + 1) * 128])
     out_ref[...] = total.astype(BF)
+    ship_out = pltpu.make_async_copy(out_ref, out_hbm, sems.at[5])
+    ship_out.start()
+    ship_out.wait()
     ship_emb.wait()
     ship_og.wait()
 
@@ -317,22 +320,25 @@
     ship.wait()
 
 
-def add_kernel(keep_ref, recv_ref, *outs):
+def fetch_kernel(packed, enc_out_ref, sems):
+    Load(packed.at[ENC_OUT:ENC_QKV], enc_out_ref, sems, 0, 4)()
+
+
+def add_kernel(keep_ref, recv_ref, fetched, *outs):
     for j in range(4):
         outs[j][...] = (keep_ref[j].astype(F32) + recv_ref[j].astype(F32)).astype(BF)
 
 
-def encode_back_kernel(marks_ref, recv_ref, packed, store, out_ref, enc_out_b, kept_b, weight_b, sems):
-    enc_out = Load(packed.at[ENC_OUT:ENC_QKV], enc_out_b, sems, 0, 2)
-    kept = Load(store.at[: 4 * TOKENS], kept_b, sems, 2)
-    weight = Load(packed.at[ENC_QKV : ENC_QKV + 3 * D], weight_b, sems, 3, 3)
+def encode_back_kernel(marks_ref, recv_ref, enc_out_ref, packed, store, out_ref, kept_b, weight_b, sems):
+    kept = Load(store.at[: 4 * TOKENS], kept_b, sems, 0)
+    weight = Load(packed.at[ENC_QKV : ENC_QKV + 3 * D], weight_b, sems, 1, 3)
     match2 = group_match(marks_ref, 2)
     lanes = iota((TOKENS, GROUPS * 8), 1)
     recv = recv_ref[...]
     grad = jnp.concatenate(
         [nn(onehot(match2 & (lanes % 2 == half)), recv) for half in range(2)], axis=1
     )
-    dctx = per_head(nt(grad.astype(BF), enc_out()[...]).astype(BF))
+    dctx = per_head(nt(grad.astype(BF), enc_out_ref[...]).astype(BF))
     kept_ref = kept()
     queries, keys, values = [kept_ref[i * TOKENS : (i + 1) * TOKENS, :] for i in range(1, 4)]
     probs = encoder_probs(queries, keys)
@@ -419,11 +425,11 @@
     ranks = visible.reshape(16, 128)
     send1, pair = call(
         send_tokens_kernel,
-        [((GROUPS * 8, 128), BF), ((TILE, 2 * D), BF, HERE)],
+        [((GROUPS * 8, 128), BF, HERE), ((TILE, 2 * D), BF, HERE)],
         ((ranks, HERE), (emb, HERE), (og, HERE)),
         "send_tokens",
-        scratch=[((16, 128), I32), ((TILE, D), BF), ((TILE, D), BF)],
-        sems=5,
+        scratch=[((16, 128), I32), ((TILE, D), BF), ((TILE, D), BF), ((GROUPS * 8, 128), BF)],
+        sems=6,
         limit=62,
     )
     halo = lax.ppermute(pair, "grid", [(i + 1, i) for i in range(GROUPS - 1)])
@@ -473,15 +479,17 @@
         flops=2 * 10**9,
     )
     recv3 = exchange(send3)
-    sums = call(add_kernel, [((D, 128), BF)] * 4, (keep, swap(send, 1)), "add_core")
-    parts = [sums[0]] + [swap(sums[j], 2 * j) for j in range(1, 4)]
+    part = swap(send, 1)
+    (enc_out_b,) = call(fetch_kernel, [((D, D), BF)], ((packed, HERE),), "fetch", sems=4, limit=40)
+    sums = call(add_kernel, [((D, 128), BF)] * 4, (keep, part, (enc_out_b, HERE)), "add_core")
+    parts = [sums[0]] + [swap(sums[j], 2 * j) for j in (2, 1, 3)]
     (back,) = call(
         encode_back_kernel,
         [((GROUPS * 8, 128), BF)],
-        (marks, recv3, (packed, HERE), (kept, HERE)),
+        (marks, recv3, enc_out_b, (packed, HERE), (kept, HERE)),
         "encode_back",
-        scratch=[((D, D), BF), ((4 * TOKENS, D), BF), ((3 * D, D), BF)],
-        sems=6,
+        scratch=[((4 * TOKENS, D), BF), ((3 * D, D), BF)],
+        sems=4,
         limit=48,
         flops=2 * 10**9,
     )

time: 138 us -> 137 us (level)
  the two profiles are of different devices: /device:TPU:4 before, /device:TPU:8 now
where the time goes in v5:
time: 137 us; the launch traced here: 136 us
  starting transfers between devices  46.1 us (34%)
  blocking collectives  31.2 us (23%)
  waiting for transfers between devices  29.7 us (22%)
  Pallas kernels  19.4 us (14%)
  local copies, waits for them, and re-layouts  9.22 us (7%)
    all_to_all x1, blocking collectives, exchange(): return lax.all_to_all(rows, 'grid', split_axis=0, concat_axis=0, tiled=True)  31.2 us
    all_to_all x3, waiting for transfers between devices, exchange(): return lax.all_to_all(rows, 'grid', split_axis=0, concat_axis=0, tiled=True)  28.9 us
    all_to_all x3, starting transfers between devices, exchange(): return lax.all_to_all(rows, 'grid', split_axis=0, concat_axis=0, tiled=True)  23 us
    pallas_call x10, Pallas kernels, call(): pl.pallas_call(kernel, out_shape=[jax.ShapeDtypeStruct(o[0], o[1]) for o...  19.4 us
    ppermute x4, starting transfers between devices, swap(): return lax.ppermute(block, 'slide', [(i, i ^ bit) for i in range(8)])  11.8 us
    ppermute x1, starting transfers between devices, shards(): halo = lax.ppermute(pair, 'grid', [(i + 1, i) for i in range(GROUPS - 1)])  11.3 us
    unnamed x24, local copies, waits for them, and re-layouts  9.22 us
  transfers between devices with their start and end apart: 8, of which 4 were waited for; matrix products, arithmetic and copies ran while one was open for 0% of the time, Pallas kernels for 5%

profile of v5, /device:TPU:8, one launch (start us, length us, event | category | flops | bytes accessed | tf_op | source)
XLA Modules:
  0.0 136.4 jit_solution(7462065558279714250)
XLA Ops:
  0.6 2.1 %send_tokens.1 = (bf16[512,128]{1,0:T(8,128)(2,1)}, bf16[128,1024]{1,0:T(8,128)(2,1)}) custom-call(s32[16,128]{1,0:T(8,128)} %bitcast.24, bf16[128,512]{1,0:T(8,128)(2,1)} %bitcast.19, bf16[128,512]{1,0:T(8,128)(2,1)} %bitcast.21), custom_call_target="tpu_custom_call" | custom-call | flops 100000000 | bytes 2000000 | tf_op jit(solution)/shard_map/send_tokens/pallas_call | solution.py:392
  2.7 11.3 %collective-permute-start = (bf16[128,1024]{1,0:T(8,128)(2,1)}, bf16[128,1024]{1,0:T(8,128)(2,1)S(1)}, u32[]{:S(2)}, u32[]{:S(2)}) collective-permute-start(bf16[128,1024]{1,0:T(8,128)(2,1)} %get-tuple-element.21), channel_id=1, source_target_pairs={{1,0},{2,1},{3,2},{4,3},{5,4},{6,5},{7,6},{8,7},{9,8},{10,9},{11,1... | collective-permute-start | bytes 786440 | tf_op jit(solution)/shard_map/ppermute | solution.py:435
  14.0 9.9 %all-to-all-start = ((bf16[64,8,128]{2,1,0:T(8,128)(2,1)}), bf16[64,8,128]{2,1,0:T(8,128)(2,1)S(1)}, u32[]{:S(2)}, u32[]{:S(2)}) async-start(bf16[64,8,128]{2,1,0:T(8,128)(2,1)} %bitcast.27), calls=%async_computation | async-start | bytes 262144 | tf_op jit(solution)/shard_map/all_to_all | solution.py:405
  24.0 0.0 collective-permute-done.halo_ref
  24.0 0.0 copy-start.5
  24.0 0.0 copy-start
  24.0 1.5 %copy-done = bf16[512,1536]{1,0:T(8,128)(2,1)S(1)} copy-done((bf16[512,1536]{1,0:T(8,128)(2,1)S(1)}, bf16[512,1536]{1,0:T(8,128)(2,1)}, u32[]{:S(2)}) %copy-start) | copy-done | bytes 1572888
  25.5 0.0 copy-start.9
  25.5 0.8 copy-done.9
  26.3 0.0 copy-start.10
  26.3 0.7 copy-done.10
  27.0 0.0 copy-start.11
  27.0 0.7 copy-done.11
  27.6 0.5 plan.1
  28.2 0.0 copy-done.5
  28.2 0.0 copy-start.3
  28.2 0.0 copy-start.4
  28.2 11.0 %all-to-all-done = bf16[64,8,128]{2,1,0:T(8,128)(2,1)S(1)} async-done(((bf16[64,8,128]{2,1,0:T(8,128)(2,1)}), bf16[64,8,128]{2,1,0:T(8,128)(2,1)S(1)}, u32[]{:S(2)}, u32[]{:S(2)}) %all-to-all-start) | async-done | bytes 131104 | tf_op jit(solution)/shard_map/all_to_all | solution.py:405
  39.2 2.4 %encode.1 = (bf16[512,256]{1,0:T(8,128)(2,1)}, bf16[18432,512]{1,0:T(8,128)(2,1)}) custom-call(bf16[512,128]{1,0:T(8,128)(2,1)S(1)} %bitcast.17, f32[16,512]{1,0:T(8,128)S(1)} %get-tuple-element.22.marks_ref, bf16[512,1536]{1,0:T(8,128)(2,1)S(1)} %get-tuple-element.24.weight_ref), custom_call_target="tpu_custom_call" | custom-call | flops 100000000 | bytes 2000000 | tf_op jit(solution)/shard_map/encode/pallas_call | solution.py:392
  41.6 6.4 %all-to-all-start.1 = ((bf16[64,8,256]{2,1,0:T(8,128)(2,1)}), bf16[64,8,256]{2,1,0:T(8,128)(2,1)S(1)}, u32[]{:S(2)}, u32[]{:S(2)}) async-start(bf16[64,8,256]{2,1,0:T(8,128)(2,1)} %bitcast.7), calls=%async_computation.1 | async-start | bytes 524288 | tf_op jit(solution)/shard_map/all_to_all | solution.py:405
  48.1 0.0 copy-done.3
  48.1 0.0 copy-done.4
  48.1 0.0 copy-start.1
  48.1 1.4 %copy-done.1 = bf16[512,1536]{1,0:T(8,128)(2,1)S(1)} copy-done((bf16[512,1536]{1,0:T(8,128)(2,1)S(1)}, bf16[512,1536]{1,0:T(8,128)(2,1)}, u32[]{:S(2)}) %copy-start.1) | copy-done | bytes 1572888
  49.5 0.0 copy-start.2
  49.5 1.4 %copy-done.2 = bf16[512,1536]{1,0:T(8,128)(2,1)S(1)} copy-done((bf16[512,1536]{1,0:T(8,128)(2,1)S(1)}, bf16[512,1536]{1,0:T(8,128)(2,1)}, u32[]{:S(2)}) %copy-start.2) | copy-done | bytes 1572888
  50.9 0.9 copy-done.6
  51.9 0.9 copy-done.7
  52.8 0.9 copy-done.8
  53.7 2.7 %prepare.1 = (bf16[2048,512]{1,0:T(8,128)(2,1)S(1)}, bf16[18432,512]{1,0:T(8,128)(2,1)}) custom-call(f32[16,512]{1,0:T(8,128)S(1)} %get-tuple-element.22.marks_ref, bf16[128,512]{1,0:T(8,128)(2,1)S(1)} %bitcast.20, bf16[128,512]{1,0:T(8,128)(2,1)S(1)} %bitcast.22, bf16[128,1024]{1,0:T(8,128)(2,1)S(1)} %copy-done.6, bf16[512,512]{1,0:T(8,128)(2,1)S(1)} %copy-done.3, ...), custom_call_target="tpu_custom_call" | custom-call | flops 100000000 | bytes 2000000 | tf_op jit(solution)/shard_map/prepare/pallas_call | solution.py:392
  56.3 12.1 %all-to-all-done.1 = bf16[64,8,256]{2,1,0:T(8,128)(2,1)S(1)} async-done(((bf16[64,8,256]{2,1,0:T(8,128)(2,1)}), bf16[64,8,256]{2,1,0:T(8,128)(2,1)S(1)}, u32[]{:S(2)}, u32[]{:S(2)}) %all-to-all-start.1) | async-done | bytes 262176 | tf_op jit(solution)/shard_map/all_to_all | solution.py:405
  68.4 6.4 %decode.1 = (bf16[512,256]{1,0:T(8,128)(2,1)}, bf16[4,512,128]{2,1,0:T(8,128)(2,1)S(1)}, bf16[4,512,128]{2,1,0:T(8,128)(2,1)S(1)}) custom-call(f32[16,512]{1,0:T(8,128)S(1)} %get-tuple-element.22.marks_ref, bf16[512,256]{1,0:T(8,128)(2,1)S(1)} %bitcast.16, bf16[2048,512]{1,0:T(8,128)(2,1)S(1)} %get-tuple-element.26.flipped_ref, ...), custom_call_target="tpu_custom_call" | custom-call | flops 2000000000 | bytes 2000000 | tf_op jit(solution)/shard_map/decode/pallas_call | solution.py:392
  74.9 6.6 %all-to-all-start.2 = ((bf16[64,8,256]{2,1,0:T(8,128)(2,1)}), bf16[64,8,256]{2,1,0:T(8,128)(2,1)S(1)}, u32[]{:S(2)}, u32[]{:S(2)}) async-start(bf16[64,8,256]{2,1,0:T(8,128)(2,1)} %bitcast.9), calls=%async_computation.2 | async-start | bytes 524288 | tf_op jit(solution)/shard_map/all_to_all | solution.py:405
  81.5 1.9 %collective-permute-start.1 = (bf16[4,512,128]{2,1,0:T(8,128)(2,1)S(1)}, bf16[4,512,128]{2,1,0:T(8,128)(2,1)S(1)}, u32[]{:S(2)}, u32[]{:S(2)}) collective-permute-start(bf16[4,512,128]{2,1,0:T(8,128)(2,1)S(1)} %get-tuple-element.31), channel_id=1, source_target_pairs={{0,64},{64,0},{128,192},{192,128},{256,320},{320,256},{384,448},{4... | collective-permute-start | bytes 1572872 | tf_op jit(solution)/shard_map/ppermute | solution.py:409
  83.4 1.1 fetch.1.enc_out_ref.fetched
  84.5 0.7 collective-permute-done.1.recv_ref
  85.3 0.1 add_core.1
  85.4 4.9 %collective-permute-start.2 = (bf16[512,128]{1,0:T(8,128)(2,1)S(1)}, bf16[512,128]{1,0:T(8,128)(2,1)S(1)}, u32[]{:S(2)}, u32[]{:S(2)}) collective-permute-start(bf16[512,128]{1,0:T(8,128)(2,1)S(1)} %get-tuple-element.33), channel_id=1, source_target_pairs={{0,256},{64,320},{128,384},{192,448},{256,0},{320,64},{384,128},{4... | collective-permute-start | bytes 393224 | tf_op jit(solution)/shard_map/ppermute | solution.py:409
  90.3 2.5 %collective-permute-start.3 = (bf16[512,128]{1,0:T(8,128)(2,1)S(1)}, bf16[512,128]{1,0:T(8,128)(2,1)S(1)}, u32[]{:S(2)}, u32[]{:S(2)}) collective-permute-start(bf16[512,128]{1,0:T(8,128)(2,1)S(1)} %get-tuple-element.34), channel_id=1, source_target_pairs={{0,128},{64,192},{128,0},{192,64},{256,384},{320,448},{384,256},{4... | collective-permute-start | bytes 393224 | tf_op jit(solution)/shard_map/ppermute | solution.py:409
  92.8 2.5 %collective-permute-start.4 = (bf16[512,128]{1,0:T(8,128)(2,1)S(1)}, bf16[512,128]{1,0:T(8,128)(2,1)S(1)}, u32[]{:S(2)}, u32[]{:S(2)}) collective-permute-start(bf16[512,128]{1,0:T(8,128)(2,1)S(1)} %get-tuple-element.35), channel_id=1, source_target_pairs={{0,384},{64,448},{128,256},{192,320},{256,128},{320,192},{384,0},{... | collective-permute-start | bytes 393224 | tf_op jit(solution)/shard_map/ppermute | solution.py:409
  95.3 5.8 %all-to-all-done.2 = bf16[64,8,256]{2,1,0:T(8,128)(2,1)S(1)} async-done(((bf16[64,8,256]{2,1,0:T(8,128)(2,1)}), bf16[64,8,256]{2,1,0:T(8,128)(2,1)S(1)}, u32[]{:S(2)}, u32[]{:S(2)}) %all-to-all-start.2) | async-done | bytes 262176 | tf_op jit(solution)/shard_map/all_to_all | solution.py:405
  101.2 2.8 %encode_back.1.tokens_ref = bf16[512,128]{1,0:T(8,128)(2,1)S(1)} custom-call(f32[16,512]{1,0:T(8,128)S(1)} %get-tuple-element.22.marks_ref, bf16[512,256]{1,0:T(8,128)(2,1)S(1)} %bitcast.14, bf16[512,512]{1,0:T(8,128)(2,1)S(1)} %fetch.1.enc_out_ref.fetched, bf16[18432,512]{1,0:T(8,128)(2,1)} %get-tuple-element.27.packed, ...), custom_call_target="tpu_custom_call" | custom-call | flops 2000000000 | bytes 2000000 | tf_op jit(solution)/shard_map/encode_back/pallas_call | solution.py:392
  104.0 0.0 collective-permute-done.2.part1
  104.0 0.0 collective-permute-done.3.part2
  104.0 0.0 collective-permute-done.4.part3
  104.0 0.1 join.1
  104.1 31.2 %all_to_all.44 = bf16[64,8,256]{2,1,0:T(8,128)(2,1)S(1)} all-to-all(bf16[64,8,256]{2,1,0:T(8,128)(2,1)S(1)} %bitcast.15), channel_id=1, replica_groups=mesh['slide'=8,'grid'=64] {'grid'}, dimensions={0} | all-to-all | bytes 524288 | tf_op jit(solution)/shard_map/all_to_all | solution.py:405
  135.3 1.1 finish.1
  (3 shorter events, 0.0 us)
Async XLA Ops:
  2.7 21.2 %collective-permute-start = (bf16[128,1024]{1,0:T(8,128)(2,1)}, bf16[128,1024]{1,0:T(8,128)(2,1)S(1)}, u32[]{:S(2)}, u32[]{:S(2)}) collective-permute-start(bf16[128,1024]{1,0:T(8,128)(2,1)} %get-tuple-element.21), channel_id=1, source_target_pairs={{1,0},{2,1},{3,2},{4,3},{5,4},{6,5},{7,6},{8,7},{9,8},{10,9},{11,1... | collective-permute-start | bytes 786440 | tf_op jit(solution)/shard_map/ppermute | solution.py:435
  14.0 25.2 %all-to-all-start = ((bf16[64,8,128]{2,1,0:T(8,128)(2,1)}), bf16[64,8,128]{2,1,0:T(8,128)(2,1)S(1)}, u32[]{:S(2)}, u32[]{:S(2)}) async-start(bf16[64,8,128]{2,1,0:T(8,128)(2,1)} %bitcast.27), calls=%async_computation | async-start | bytes 262144 | tf_op jit(solution)/shard_map/all_to_all | solution.py:405
  24.0 4.2 %copy-start.5 = (bf16[128,1024]{1,0:T(8,128)(2,1)}, bf16[128,1024]{1,0:T(8,128)(2,1)S(1)}, u32[]{:S(2)}) copy-start(bf16[128,1024]{1,0:T(8,128)(2,1)S(1)} %collective-permute-done.halo_ref) | copy-start | bytes 786436
  24.0 1.5 %copy-start = (bf16[512,1536]{1,0:T(8,128)(2,1)S(1)}, bf16[512,1536]{1,0:T(8,128)(2,1)}, u32[]{:S(2)}) copy-start(bf16[512,1536]{1,0:T(8,128)(2,1)} %enc_qkv_ref.3) | copy-start | bytes 4718596
  25.5 0.8 copy-start.9
  26.3 0.7 copy-start.10
  27.0 0.7 copy-start.11
  28.2 19.9 %copy-start.3 = (bf16[512,512]{1,0:T(8,128)(2,1)S(1)}, bf16[512,512]{1,0:T(8,128)(2,1)}, u32[]{:S(2)}) copy-start(bf16[512,512]{1,0:T(8,128)(2,1)} %proj_ref.1) | copy-start | bytes 1572868
  28.2 19.9 %copy-start.4 = (bf16[512,512]{1,0:T(8,128)(2,1)S(1)}, bf16[512,512]{1,0:T(8,128)(2,1)}, u32[]{:S(2)}) copy-start(bf16[512,512]{1,0:T(8,128)(2,1)} %enc_out_ref.1) | copy-start | bytes 1572868
  41.6 26.8 %all-to-all-start.1 = ((bf16[64,8,256]{2,1,0:T(8,128)(2,1)}), bf16[64,8,256]{2,1,0:T(8,128)(2,1)S(1)}, u32[]{:S(2)}, u32[]{:S(2)}) async-start(bf16[64,8,256]{2,1,0:T(8,128)(2,1)} %bitcast.7), calls=%async_computation.1 | async-start | bytes 524288 | tf_op jit(solution)/shard_map/all_to_all | solution.py:405
  48.1 1.4 %copy-start.1 = (bf16[512,1536]{1,0:T(8,128)(2,1)S(1)}, bf16[512,1536]{1,0:T(8,128)(2,1)}, u32[]{:S(2)}) copy-start(bf16[512,1536]{1,0:T(8,128)(2,1)} %enc_qkv_ref.3) | copy-start | bytes 4718596
  49.5 1.4 %copy-start.2 = (bf16[512,1536]{1,0:T(8,128)(2,1)S(1)}, bf16[512,1536]{1,0:T(8,128)(2,1)}, u32[]{:S(2)}) copy-start(bf16[512,1536]{1,0:T(8,128)(2,1)} %qkv_ref.1) | copy-start | bytes 4718596
  50.9 0.9 copy-start.6
  51.9 0.9 copy-start.7
  52.8 0.9 copy-start.8
  74.9 26.3 %all-to-all-start.2 = ((bf16[64,8,256]{2,1,0:T(8,128)(2,1)}), bf16[64,8,256]{2,1,0:T(8,128)(2,1)S(1)}, u32[]{:S(2)}, u32[]{:S(2)}) async-start(bf16[64,8,256]{2,1,0:T(8,128)(2,1)} %bitcast.9), calls=%async_computation.2 | async-start | bytes 524288 | tf_op jit(solution)/shard_map/all_to_all | solution.py:405
  81.5 3.8 %collective-permute-start.1 = (bf16[4,512,128]{2,1,0:T(8,128)(2,1)S(1)}, bf16[4,512,128]{2,1,0:T(8,128)(2,1)S(1)}, u32[]{:S(2)}, u32[]{:S(2)}) collective-permute-start(bf16[4,512,128]{2,1,0:T(8,128)(2,1)S(1)} %get-tuple-element.31), channel_id=1, source_target_pairs={{0,64},{64,0},{128,192},{192,128},{256,320},{320,256},{384,448},{4... | collective-permute-start | bytes 1572872 | tf_op jit(solution)/shard_map/ppermute | solution.py:409
  85.4 18.6 %collective-permute-start.2 = (bf16[512,128]{1,0:T(8,128)(2,1)S(1)}, bf16[512,128]{1,0:T(8,128)(2,1)S(1)}, u32[]{:S(2)}, u32[]{:S(2)}) collective-permute-start(bf16[512,128]{1,0:T(8,128)(2,1)S(1)} %get-tuple-element.33), channel_id=1, source_target_pairs={{0,256},{64,320},{128,384},{192,448},{256,0},{320,64},{384,128},{4... | collective-permute-start | bytes 393224 | tf_op jit(solution)/shard_map/ppermute | solution.py:409
  90.3 13.7 %collective-permute-start.3 = (bf16[512,128]{1,0:T(8,128)(2,1)S(1)}, bf16[512,128]{1,0:T(8,128)(2,1)S(1)}, u32[]{:S(2)}, u32[]{:S(2)}) collective-permute-start(bf16[512,128]{1,0:T(8,128)(2,1)S(1)} %get-tuple-element.34), channel_id=1, source_target_pairs={{0,128},{64,192},{128,0},{192,64},{256,384},{320,448},{384,256},{4... | collective-permute-start | bytes 393224 | tf_op jit(solution)/shard_map/ppermute | solution.py:409
  92.8 11.2 %collective-permute-start.4 = (bf16[512,128]{1,0:T(8,128)(2,1)S(1)}, bf16[512,128]{1,0:T(8,128)(2,1)S(1)}, u32[]{:S(2)}, u32[]{:S(2)}) collective-permute-start(bf16[512,128]{1,0:T(8,128)(2,1)S(1)} %get-tuple-element.35), channel_id=1, source_target_pairs={{0,384},{64,448},{128,256},{192,320},{256,128},{320,192},{384,0},{... | collective-permute-start | bytes 393224 | tf_op jit(solution)/shard_map/ppermute | solution.py:409

commit v6 on v5

--- a/solution.py
+++ b/solution.py
@@ -320,8 +320,8 @@
     ship.wait()
 
 
-def fetch_kernel(packed, enc_out_ref, sems):
-    Load(packed.at[ENC_OUT:ENC_QKV], enc_out_ref, sems, 0, 4)()
+def fetch_kernel(packed, first_ref, sems):
+    Load(packed.at[ENC_OUT : ENC_QKV + D], first_ref, sems, 0, 4)()
 
 
 def add_kernel(keep_ref, recv_ref, fetched, *outs):
@@ -329,16 +329,16 @@
         outs[j][...] = (keep_ref[j].astype(F32) + recv_ref[j].astype(F32)).astype(BF)
 
 
-def encode_back_kernel(marks_ref, recv_ref, enc_out_ref, packed, store, out_ref, kept_b, weight_b, sems):
+def encode_back_kernel(marks_ref, recv_ref, first_ref, packed, store, out_ref, kept_b, weight_b, sems):
     kept = Load(store.at[: 4 * TOKENS], kept_b, sems, 0)
-    weight = Load(packed.at[ENC_QKV : ENC_QKV + 3 * D], weight_b, sems, 1, 3)
+    weight = Load(packed.at[ENC_QKV + D : ENC_QKV + 3 * D], weight_b, sems, 1, 2)
     match2 = group_match(marks_ref, 2)
     lanes = iota((TOKENS, GROUPS * 8), 1)
     recv = recv_ref[...]
     grad = jnp.concatenate(
         [nn(onehot(match2 & (lanes % 2 == half)), recv) for half in range(2)], axis=1
     )
-    dctx = per_head(nt(grad.astype(BF), enc_out_ref[...]).astype(BF))
+    dctx = per_head(nt(grad.astype(BF), first_ref[:D, :]).astype(BF))
     kept_ref = kept()
     queries, keys, values = [kept_ref[i * TOKENS : (i + 1) * TOKENS, :] for i in range(1, 4)]
     probs = encoder_probs(queries, keys)
@@ -348,10 +348,10 @@
     dq = fold_heads(nn(dscores, keys))
     dk = tn(dscores, per_head(queries))
     dv = tn(probs.astype(BF), dctx)
+    dnormed = nt(dq.astype(BF), first_ref[D:, :])
     weight_ref = weight()
-    dnormed = nt(dq.astype(BF), weight_ref[:D, :])
-    dnormed += nt(dk.astype(BF), weight_ref[D : 2 * D, :])
-    dnormed += nt(dv.astype(BF), weight_ref[2 * D :, :])
+    dnormed += nt(dk.astype(BF), weight_ref[:D, :])
+    dnormed += nt(dv.astype(BF), weight_ref[D:, :])
     dnormed = dnormed.astype(BF).astype(F32)
     x = kept_ref[:TOKENS, :].astype(F32)
     inv = lax.rsqrt(jnp.mean(x * x, axis=1, keepdims=True) + EPS)
@@ -480,16 +480,16 @@
     )
     recv3 = exchange(send3)
     part = swap(send, 1)
-    (enc_out_b,) = call(fetch_kernel, [((D, D), BF)], ((packed, HERE),), "fetch", sems=4, limit=40)
-    sums = call(add_kernel, [((D, 128), BF)] * 4, (keep, part, (enc_out_b, HERE)), "add_core")
+    (first_b,) = call(fetch_kernel, [((2 * D, D), BF)], ((packed, HERE),), "fetch", sems=4, limit=40)
+    sums = call(add_kernel, [((D, 128), BF)] * 4, (keep, part, (first_b, HERE)), "add_core")
     parts = [sums[0]] + [swap(sums[j], 2 * j) for j in (2, 1, 3)]
     (back,) = call(
         encode_back_kernel,
         [((GROUPS * 8, 128), BF)],
-        (marks, recv3, enc_out_b, (packed, HERE), (kept, HERE)),
+        (marks, recv3, first_b, (packed, HERE), (kept, HERE)),
         "encode_back",
-        scratch=[((4 * TOKENS, D), BF), ((3 * D, D), BF)],
-        sems=4,
+        scratch=[((4 * TOKENS, D), BF), ((2 * D, D), BF)],
+        sems=3,
         limit=48,
         flops=2 * 10**9,
     )

time: 137 us -> 137 us (level)
  no operation moved by 1% of the time
where the time goes in v6:
time: 137 us; the launch traced here: 136 us
  starting transfers between devices  46.1 us (34%)
  blocking collectives  31.2 us (23%)
  waiting for transfers between devices  29.6 us (22%)
  Pallas kernels  19.4 us (14%)
  local copies, waits for them, and re-layouts  9.22 us (7%)
    all_to_all x1, blocking collectives, exchange(): return lax.all_to_all(rows, 'grid', split_axis=0, concat_axis=0, tiled=True)  31.2 us
    all_to_all x3, waiting for transfers between devices, exchange(): return lax.all_to_all(rows, 'grid', split_axis=0, concat_axis=0, tiled=True)  28.9 us
    all_to_all x3, starting transfers between devices, exchange(): return lax.all_to_all(rows, 'grid', split_axis=0, concat_axis=0, tiled=True)  23 us
    pallas_call x10, Pallas kernels, call(): pl.pallas_call(kernel, out_shape=[jax.ShapeDtypeStruct(o[0], o[1]) for o...  19.4 us
    ppermute x4, starting transfers between devices, swap(): return lax.ppermute(block, 'slide', [(i, i ^ bit) for i in range(8)])  11.8 us
    ppermute x1, starting transfers between devices, shards(): halo = lax.ppermute(pair, 'grid', [(i + 1, i) for i in range(GROUPS - 1)])  11.3 us
    unnamed x24, local copies, waits for them, and re-layouts  9.22 us
  transfers between devices with their start and end apart: 8, of which 4 were waited for; matrix products, arithmetic and copies ran while one was open for 0% of the time, Pallas kernels for 5%

profile of v6, /device:TPU:8, one launch (start us, length us, event | category | flops | bytes accessed | tf_op | source)
XLA Modules:
  0.0 136.4 jit_solution(1091573786182982102)
XLA Ops:
  0.6 2.1 %send_tokens.1 = (bf16[512,128]{1,0:T(8,128)(2,1)}, bf16[128,1024]{1,0:T(8,128)(2,1)}) custom-call(s32[16,128]{1,0:T(8,128)} %bitcast.24, bf16[128,512]{1,0:T(8,128)(2,1)} %bitcast.19, bf16[128,512]{1,0:T(8,128)(2,1)} %bitcast.21), custom_call_target="tpu_custom_call" | custom-call | flops 100000000 | bytes 2000000 | tf_op jit(solution)/shard_map/send_tokens/pallas_call | solution.py:392
  2.7 11.3 %collective-permute-start = (bf16[128,1024]{1,0:T(8,128)(2,1)}, bf16[128,1024]{1,0:T(8,128)(2,1)S(1)}, u32[]{:S(2)}, u32[]{:S(2)}) collective-permute-start(bf16[128,1024]{1,0:T(8,128)(2,1)} %get-tuple-element.21), channel_id=1, source_target_pairs={{1,0},{2,1},{3,2},{4,3},{5,4},{6,5},{7,6},{8,7},{9,8},{10,9},{11,1... | collective-permute-start | bytes 786440 | tf_op jit(solution)/shard_map/ppermute | solution.py:435
  14.0 9.9 %all-to-all-start = ((bf16[64,8,128]{2,1,0:T(8,128)(2,1)}), bf16[64,8,128]{2,1,0:T(8,128)(2,1)S(1)}, u32[]{:S(2)}, u32[]{:S(2)}) async-start(bf16[64,8,128]{2,1,0:T(8,128)(2,1)} %bitcast.27), calls=%async_computation | async-start | bytes 262144 | tf_op jit(solution)/shard_map/all_to_all | solution.py:405
  24.0 0.0 collective-permute-done.halo_ref
  24.0 0.0 copy-start.5
  24.0 0.0 copy-start
  24.0 1.5 %copy-done = bf16[512,1536]{1,0:T(8,128)(2,1)S(1)} copy-done((bf16[512,1536]{1,0:T(8,128)(2,1)S(1)}, bf16[512,1536]{1,0:T(8,128)(2,1)}, u32[]{:S(2)}) %copy-start) | copy-done | bytes 1572888
  25.5 0.0 copy-start.9
  25.5 0.8 copy-done.9
  26.3 0.0 copy-start.10
  26.3 0.7 copy-done.10
  27.0 0.0 copy-start.11
  27.0 0.7 copy-done.11
  27.6 0.5 plan.1
  28.2 0.0 copy-done.5
  28.2 0.0 copy-start.3
  28.2 0.0 copy-start.4
  28.2 11.0 %all-to-all-done = bf16[64,8,128]{2,1,0:T(8,128)(2,1)S(1)} async-done(((bf16[64,8,128]{2,1,0:T(8,128)(2,1)}), bf16[64,8,128]{2,1,0:T(8,128)(2,1)S(1)}, u32[]{:S(2)}, u32[]{:S(2)}) %all-to-all-start) | async-done | bytes 131104 | tf_op jit(solution)/shard_map/all_to_all | solution.py:405
  39.2 2.4 %encode.1 = (bf16[512,256]{1,0:T(8,128)(2,1)}, bf16[18432,512]{1,0:T(8,128)(2,1)}) custom-call(bf16[512,128]{1,0:T(8,128)(2,1)S(1)} %bitcast.17, f32[16,512]{1,0:T(8,128)S(1)} %get-tuple-element.22.marks_ref, bf16[512,1536]{1,0:T(8,128)(2,1)S(1)} %get-tuple-element.24.weight_ref), custom_call_target="tpu_custom_call" | custom-call | flops 100000000 | bytes 2000000 | tf_op jit(solution)/shard_map/encode/pallas_call | solution.py:392
  41.6 6.4 %all-to-all-start.1 = ((bf16[64,8,256]{2,1,0:T(8,128)(2,1)}), bf16[64,8,256]{2,1,0:T(8,128)(2,1)S(1)}, u32[]{:S(2)}, u32[]{:S(2)}) async-start(bf16[64,8,256]{2,1,0:T(8,128)(2,1)} %bitcast.7), calls=%async_computation.1 | async-start | bytes 524288 | tf_op jit(solution)/shard_map/all_to_all | solution.py:405
  48.1 0.0 copy-done.3
  48.1 0.0 copy-done.4
  48.1 0.0 copy-start.1
  48.1 1.4 %copy-done.1 = bf16[512,1536]{1,0:T(8,128)(2,1)S(1)} copy-done((bf16[512,1536]{1,0:T(8,128)(2,1)S(1)}, bf16[512,1536]{1,0:T(8,128)(2,1)}, u32[]{:S(2)}) %copy-start.1) | copy-done | bytes 1572888
  49.5 0.0 copy-start.2
  49.5 1.4 %copy-done.2 = bf16[512,1536]{1,0:T(8,128)(2,1)S(1)} copy-done((bf16[512,1536]{1,0:T(8,128)(2,1)S(1)}, bf16[512,1536]{1,0:T(8,128)(2,1)}, u32[]{:S(2)}) %copy-start.2) | copy-done | bytes 1572888
  50.9 0.9 copy-done.6
  51.9 0.9 copy-done.7
  52.8 0.9 copy-done.8
  53.7 2.7 %prepare.1 = (bf16[2048,512]{1,0:T(8,128)(2,1)S(1)}, bf16[18432,512]{1,0:T(8,128)(2,1)}) custom-call(f32[16,512]{1,0:T(8,128)S(1)} %get-tuple-element.22.marks_ref, bf16[128,512]{1,0:T(8,128)(2,1)S(1)} %bitcast.20, bf16[128,512]{1,0:T(8,128)(2,1)S(1)} %bitcast.22, bf16[128,1024]{1,0:T(8,128)(2,1)S(1)} %copy-done.6, bf16[512,512]{1,0:T(8,128)(2,1)S(1)} %copy-done.3, ...), custom_call_target="tpu_custom_call" | custom-call | flops 100000000 | bytes 2000000 | tf_op jit(solution)/shard_map/prepare/pallas_call | solution.py:392
  56.3 12.1 %all-to-all-done.1 = bf16[64,8,256]{2,1,0:T(8,128)(2,1)S(1)} async-done(((bf16[64,8,256]{2,1,0:T(8,128)(2,1)}), bf16[64,8,256]{2,1,0:T(8,128)(2,1)S(1)}, u32[]{:S(2)}, u32[]{:S(2)}) %all-to-all-start.1) | async-done | bytes 262176 | tf_op jit(solution)/shard_map/all_to_all | solution.py:405
  68.4 6.4 %decode.1 = (bf16[512,256]{1,0:T(8,128)(2,1)}, bf16[4,512,128]{2,1,0:T(8,128)(2,1)S(1)}, bf16[4,512,128]{2,1,0:T(8,128)(2,1)S(1)}) custom-call(f32[16,512]{1,0:T(8,128)S(1)} %get-tuple-element.22.marks_ref, bf16[512,256]{1,0:T(8,128)(2,1)S(1)} %bitcast.16, bf16[2048,512]{1,0:T(8,128)(2,1)S(1)} %get-tuple-element.26.flipped_ref, ...), custom_call_target="tpu_custom_call" | custom-call | flops 2000000000 | bytes 2000000 | tf_op jit(solution)/shard_map/decode/pallas_call | solution.py:392
  74.9 6.6 %all-to-all-start.2 = ((bf16[64,8,256]{2,1,0:T(8,128)(2,1)}), bf16[64,8,256]{2,1,0:T(8,128)(2,1)S(1)}, u32[]{:S(2)}, u32[]{:S(2)}) async-start(bf16[64,8,256]{2,1,0:T(8,128)(2,1)} %bitcast.9), calls=%async_computation.2 | async-start | bytes 524288 | tf_op jit(solution)/shard_map/all_to_all | solution.py:405
  81.5 1.9 %collective-permute-start.1 = (bf16[4,512,128]{2,1,0:T(8,128)(2,1)S(1)}, bf16[4,512,128]{2,1,0:T(8,128)(2,1)S(1)}, u32[]{:S(2)}, u32[]{:S(2)}) collective-permute-start(bf16[4,512,128]{2,1,0:T(8,128)(2,1)S(1)} %get-tuple-element.31), channel_id=1, source_target_pairs={{0,64},{64,0},{128,192},{192,128},{256,320},{320,256},{384,448},{4... | collective-permute-start | bytes 1572872 | tf_op jit(solution)/shard_map/ppermute | solution.py:409
  83.4 1.2 fetch.1.first_ref.fetched
  84.6 0.6 collective-permute-done.1.recv_ref
  85.3 0.1 add_core.1
  85.4 4.9 %collective-permute-start.2 = (bf16[512,128]{1,0:T(8,128)(2,1)S(1)}, bf16[512,128]{1,0:T(8,128)(2,1)S(1)}, u32[]{:S(2)}, u32[]{:S(2)}) collective-permute-start(bf16[512,128]{1,0:T(8,128)(2,1)S(1)} %get-tuple-element.33), channel_id=1, source_target_pairs={{0,256},{64,320},{128,384},{192,448},{256,0},{320,64},{384,128},{4... | collective-permute-start | bytes 393224 | tf_op jit(solution)/shard_map/ppermute | solution.py:409
  90.3 2.5 %collective-permute-start.3 = (bf16[512,128]{1,0:T(8,128)(2,1)S(1)}, bf16[512,128]{1,0:T(8,128)(2,1)S(1)}, u32[]{:S(2)}, u32[]{:S(2)}) collective-permute-start(bf16[512,128]{1,0:T(8,128)(2,1)S(1)} %get-tuple-element.34), channel_id=1, source_target_pairs={{0,128},{64,192},{128,0},{192,64},{256,384},{320,448},{384,256},{4... | collective-permute-start | bytes 393224 | tf_op jit(solution)/shard_map/ppermute | solution.py:409
  92.8 2.5 %collective-permute-start.4 = (bf16[512,128]{1,0:T(8,128)(2,1)S(1)}, bf16[512,128]{1,0:T(8,128)(2,1)S(1)}, u32[]{:S(2)}, u32[]{:S(2)}) collective-permute-start(bf16[512,128]{1,0:T(8,128)(2,1)S(1)} %get-tuple-element.35), channel_id=1, source_target_pairs={{0,384},{64,448},{128,256},{192,320},{256,128},{320,192},{384,0},{... | collective-permute-start | bytes 393224 | tf_op jit(solution)/shard_map/ppermute | solution.py:409
  95.3 5.8 %all-to-all-done.2 = bf16[64,8,256]{2,1,0:T(8,128)(2,1)S(1)} async-done(((bf16[64,8,256]{2,1,0:T(8,128)(2,1)}), bf16[64,8,256]{2,1,0:T(8,128)(2,1)S(1)}, u32[]{:S(2)}, u32[]{:S(2)}) %all-to-all-start.2) | async-done | bytes 262176 | tf_op jit(solution)/shard_map/all_to_all | solution.py:405
  101.2 2.8 %encode_back.1.tokens_ref = bf16[512,128]{1,0:T(8,128)(2,1)S(1)} custom-call(f32[16,512]{1,0:T(8,128)S(1)} %get-tuple-element.22.marks_ref, bf16[512,256]{1,0:T(8,128)(2,1)S(1)} %bitcast.14, bf16[1024,512]{1,0:T(8,128)(2,1)S(1)} %fetch.1.first_ref.fetched, bf16[18432,512]{1,0:T(8,128)(2,1)} %get-tuple-element.27.packed, ...), custom_call_target="tpu_custom_call" | custom-call | flops 2000000000 | bytes 2000000 | tf_op jit(solution)/shard_map/encode_back/pallas_call | solution.py:392
  104.0 0.0 collective-permute-done.2.part1
  104.0 0.0 collective-permute-done.3.part2
  104.0 0.0 collective-permute-done.4.part3
  104.0 0.1 join.1
  104.1 31.2 %all_to_all.44 = bf16[64,8,256]{2,1,0:T(8,128)(2,1)S(1)} all-to-all(bf16[64,8,256]{2,1,0:T(8,128)(2,1)S(1)} %bitcast.15), channel_id=1, replica_groups=mesh['slide'=8,'grid'=64] {'grid'}, dimensions={0} | all-to-all | bytes 524288 | tf_op jit(solution)/shard_map/all_to_all | solution.py:405
  135.3 1.1 finish.1
  (3 shorter events, 0.0 us)
Async XLA Ops:
  2.7 21.2 %collective-permute-start = (bf16[128,1024]{1,0:T(8,128)(2,1)}, bf16[128,1024]{1,0:T(8,128)(2,1)S(1)}, u32[]{:S(2)}, u32[]{:S(2)}) collective-permute-start(bf16[128,1024]{1,0:T(8,128)(2,1)} %get-tuple-element.21), channel_id=1, source_target_pairs={{1,0},{2,1},{3,2},{4,3},{5,4},{6,5},{7,6},{8,7},{9,8},{10,9},{11,1... | collective-permute-start | bytes 786440 | tf_op jit(solution)/shard_map/ppermute | solution.py:435
  14.0 25.2 %all-to-all-start = ((bf16[64,8,128]{2,1,0:T(8,128)(2,1)}), bf16[64,8,128]{2,1,0:T(8,128)(2,1)S(1)}, u32[]{:S(2)}, u32[]{:S(2)}) async-start(bf16[64,8,128]{2,1,0:T(8,128)(2,1)} %bitcast.27), calls=%async_computation | async-start | bytes 262144 | tf_op jit(solution)/shard_map/all_to_all | solution.py:405
  24.0 4.2 %copy-start.5 = (bf16[128,1024]{1,0:T(8,128)(2,1)}, bf16[128,1024]{1,0:T(8,128)(2,1)S(1)}, u32[]{:S(2)}) copy-start(bf16[128,1024]{1,0:T(8,128)(2,1)S(1)} %collective-permute-done.halo_ref) | copy-start | bytes 786436
  24.0 1.5 %copy-start = (bf16[512,1536]{1,0:T(8,128)(2,1)S(1)}, bf16[512,1536]{1,0:T(8,128)(2,1)}, u32[]{:S(2)}) copy-start(bf16[512,1536]{1,0:T(8,128)(2,1)} %enc_qkv_ref.3) | copy-start | bytes 4718596
  25.5 0.8 copy-start.9
  26.3 0.7 copy-start.10
  27.0 0.7 copy-start.11
  28.2 19.9 %copy-start.3 = (bf16[512,512]{1,0:T(8,128)(2,1)S(1)}, bf16[512,512]{1,0:T(8,128)(2,1)}, u32[]{:S(2)}) copy-start(bf16[512,512]{1,0:T(8,128)(2,1)} %proj_ref.1) | copy-start | bytes 1572868
  28.2 19.9 %copy-start.4 = (bf16[512,512]{1,0:T(8,128)(2,1)S(1)}, bf16[512,512]{1,0:T(8,128)(2,1)}, u32[]{:S(2)}) copy-start(bf16[512,512]{1,0:T(8,128)(2,1)} %enc_out_ref.1) | copy-start | bytes 1572868
  41.6 26.8 %all-to-all-start.1 = ((bf16[64,8,256]{2,1,0:T(8,128)(2,1)}), bf16[64,8,256]{2,1,0:T(8,128)(2,1)S(1)}, u32[]{:S(2)}, u32[]{:S(2)}) async-start(bf16[64,8,256]{2,1,0:T(8,128)(2,1)} %bitcast.7), calls=%async_computation.1 | async-start | bytes 524288 | tf_op jit(solution)/shard_map/all_to_all | solution.py:405
  48.1 1.4 %copy-start.1 = (bf16[512,1536]{1,0:T(8,128)(2,1)S(1)}, bf16[512,1536]{1,0:T(8,128)(2,1)}, u32[]{:S(2)}) copy-start(bf16[512,1536]{1,0:T(8,128)(2,1)} %enc_qkv_ref.3) | copy-start | bytes 4718596
  49.5 1.4 %copy-start.2 = (bf16[512,1536]{1,0:T(8,128)(2,1)S(1)}, bf16[512,1536]{1,0:T(8,128)(2,1)}, u32[]{:S(2)}) copy-start(bf16[512,1536]{1,0:T(8,128)(2,1)} %qkv_ref.1) | copy-start | bytes 4718596
  50.9 0.9 copy-start.6
  51.9 0.9 copy-start.7
  52.8 0.9 copy-start.8
  74.9 26.3 %all-to-all-start.2 = ((bf16[64,8,256]{2,1,0:T(8,128)(2,1)}), bf16[64,8,256]{2,1,0:T(8,128)(2,1)S(1)}, u32[]{:S(2)}, u32[]{:S(2)}) async-start(bf16[64,8,256]{2,1,0:T(8,128)(2,1)} %bitcast.9), calls=%async_computation.2 | async-start | bytes 524288 | tf_op jit(solution)/shard_map/all_to_all | solution.py:405
  81.5 3.8 %collective-permute-start.1 = (bf16[4,512,128]{2,1,0:T(8,128)(2,1)S(1)}, bf16[4,512,128]{2,1,0:T(8,128)(2,1)S(1)}, u32[]{:S(2)}, u32[]{:S(2)}) collective-permute-start(bf16[4,512,128]{2,1,0:T(8,128)(2,1)S(1)} %get-tuple-element.31), channel_id=1, source_target_pairs={{0,64},{64,0},{128,192},{192,128},{256,320},{320,256},{384,448},{4... | collective-permute-start | bytes 1572872 | tf_op jit(solution)/shard_map/ppermute | solution.py:409
  85.4 18.6 %collective-permute-start.2 = (bf16[512,128]{1,0:T(8,128)(2,1)S(1)}, bf16[512,128]{1,0:T(8,128)(2,1)S(1)}, u32[]{:S(2)}, u32[]{:S(2)}) collective-permute-start(bf16[512,128]{1,0:T(8,128)(2,1)S(1)} %get-tuple-element.33), channel_id=1, source_target_pairs={{0,256},{64,320},{128,384},{192,448},{256,0},{320,64},{384,128},{4... | collective-permute-start | bytes 393224 | tf_op jit(solution)/shard_map/ppermute | solution.py:409
  90.3 13.6 %collective-permute-start.3 = (bf16[512,128]{1,0:T(8,128)(2,1)S(1)}, bf16[512,128]{1,0:T(8,128)(2,1)S(1)}, u32[]{:S(2)}, u32[]{:S(2)}) collective-permute-start(bf16[512,128]{1,0:T(8,128)(2,1)S(1)} %get-tuple-element.34), channel_id=1, source_target_pairs={{0,128},{64,192},{128,0},{192,64},{256,384},{320,448},{384,256},{4... | collective-permute-start | bytes 393224 | tf_op jit(solution)/shard_map/ppermute | solution.py:409
  92.8 11.1 %collective-permute-start.4 = (bf16[512,128]{1,0:T(8,128)(2,1)S(1)}, bf16[512,128]{1,0:T(8,128)(2,1)S(1)}, u32[]{:S(2)}, u32[]{:S(2)}) collective-permute-start(bf16[512,128]{1,0:T(8,128)(2,1)S(1)} %get-tuple-element.35), channel_id=1, source_target_pairs={{0,384},{64,448},{128,256},{192,320},{256,128},{320,192},{384,0},{... | collective-permute-start | bytes 393224 | tf_op jit(solution)/shard_map/ppermute | solution.py:409
